TPU v7x, 256 devices: a whole 4x4x8 slice. The times are simulated.
256 devices in a mesh: dp: 16 (over x, y_hi, core), vocab: 8 (over z), tensor: 2 (over y_lo).
Axes of the slice: x: 4, y: 4 (y_hi: 2, y_lo: 2; y = y_hi * 2 + y_lo), z: 8, core: 2. Of those that a mesh axis runs over, the one named last changes fastest.
Arguments:
- residual: bfloat16 [1408, 4096], P('dp', 'tensor'), may hold values from -400 to 400
- norm_gain: float32 [4096], P('tensor'), may hold values from 0.1 to 1.9
- gain_dir: float32 [4096], P('tensor'), may hold values from -6 to 6
- head_weight: bfloat16 [4096, 81920], P('tensor', ('dp', 'vocab')), may hold values from -0.8 to 0.8
- head_dir: bfloat16 [4096, 81920], P('tensor', ('dp', 'vocab')), may hold values from -0.25 to 0.25
- sampled: int32 [1408], replicated, may hold values from 0 to 81919
Outputs:
- fisher_head: float32 [4096, 81920], P('tensor', ('dp', 'vocab'))
- fisher_gain: float32 [4096], P('tensor')
All inputs are finite; a program needn't handle non-finite values.
Results may differ from a plain program's by a relative error of at most 0.012.
The roundings to bfloat16 on the way count: a program that leaves them out, or rounds other values in their place, can miss the bound.
Values may be sent and summed in bfloat16 or wider, within the bound.
No kernel may reach another device: no remote copies, remote signals or barrier semaphores. Data moves between devices by JAX's collectives and lax.ppermute only.
A program may use at most 128 MiB of HBM per device.

v0:
```python
import jax
import jax.numpy as jnp
from jax import lax
from jax.sharding import PartitionSpec as P

EPSILON = 1e-06


def local(residual, norm_gain, gain_dir, head_weight, head_dir, sampled):
    full_width = residual.shape[1] * lax.axis_size("tensor")
    entries = residual.astype(jnp.float32)
    squares = lax.psum(jnp.sum(entries * entries, axis=1), "tensor")
    normed = (entries * lax.rsqrt(squares / full_width + EPSILON)[:, None]).astype(jnp.bfloat16)
    gathered = lax.all_gather(normed, "dp", axis=0, tiled=True)
    spread = gathered.astype(jnp.float32)
    hidden = (spread * norm_gain).astype(jnp.bfloat16)
    tangent = (spread * gain_dir).astype(jnp.bfloat16)
    logits = jnp.dot(hidden, head_weight, preferred_element_type=jnp.float32)
    tangent_logits = jnp.dot(hidden, head_dir, preferred_element_type=jnp.float32) + jnp.dot(
        tangent, head_weight, preferred_element_type=jnp.float32
    )
    logits, tangent_logits = (
        lax.psum_scatter(logits, "tensor", scatter_dimension=0, tiled=True),
        lax.psum_scatter(tangent_logits, "tensor", scatter_dimension=0, tiled=True),
    )
    share_rows = logits.shape[0]
    picked_ids = lax.dynamic_slice_in_dim(
        sampled, lax.axis_index("tensor") * share_rows, share_rows
    )
    vocab_dev = head_weight.shape[1]
    offset = (lax.axis_index("dp") * lax.axis_size("vocab") + lax.axis_index("vocab")) * vocab_dev
    is_picked = lax.broadcasted_iota(jnp.int32, logits.shape, 1) == (picked_ids - offset)[:, None]
    picked_part = jnp.sum(jnp.where(is_picked, tangent_logits, 0.0), axis=1)
    row_top = lax.pmax(jnp.max(logits, axis=1), ("dp", "vocab"))
    scaled_exp = jnp.exp(logits - row_top[:, None])
    row_total, weighted, picked = lax.psum(
        (jnp.sum(scaled_exp, axis=1), jnp.sum(scaled_exp * tangent_logits, axis=1), picked_part),
        ("dp", "vocab"),
    )
    row_probs = scaled_exp / row_total[:, None]
    row_score = picked - weighted / row_total
    cotangent = (row_score[:, None] * (is_picked.astype(jnp.float32) - row_probs)).astype(
        jnp.bfloat16
    )
    full_cot = lax.all_gather(cotangent, "tensor", axis=0, tiled=True)
    product = lax.dot_general(
        gathered, full_cot, (((0,), (0,)), ((), ())), preferred_element_type=jnp.float32
    )
    fisher_head = norm_gain[:, None] * product
    fisher_gain = lax.psum(
        jnp.sum(head_weight.astype(jnp.float32) * product, axis=1), ("dp", "vocab")
    )
    return (fisher_head, fisher_gain)


def solution(mesh):
    in_specs = (
        P("dp", "tensor"),
        P("tensor"),
        P("tensor"),
        P("tensor", ("dp", "vocab")),
        P("tensor", ("dp", "vocab")),
        P(),
    )
    out_specs = (P("tensor", ("dp", "vocab")), P("tensor"))
    return jax.shard_map(local, mesh=mesh, in_specs=in_specs, out_specs=out_specs, check_vma=False)
```

profile of v0, /device:TPU:1, one launch (start us, length us, event | category | flops | bytes accessed | tf_op | source)
XLA Modules:
  0.0 1499.3 jit_solution(15969742382134527424)
XLA Ops:
  7.2 1.3 fusion.13
  8.5 4.4 psum.35
  13.0 1.9 fusion.14
  14.9 0.0 reduce-scatter.5.cloned.1.call-start
  14.9 71.9 %all-gather.3.cloned.1.call-done = bf16[1408,2048]{1,0:T(8,128)(2,1)} async-done(((bf16[88,2048]{1,0:T(8,128)(2,1)}), bf16[1408,2048]{1,0:T(8,128)(2,1)}) %all-gather.3.cloned.1.call-update) | async-done | bytes 5767184 | tf_op jit(solution)/shard_map/all_gather | solution.py:14
  86.8 9.9 fusion.5
  96.8 0.0 reduce-scatter.3.cloned.1.call-start
  96.8 0.6 copy-done.2
  97.4 7.4 fusion.2
  104.9 10.1 fusion.9
  115.0 0.0 all-gather.5.cloned.1.call-start
  115.0 0.6 copy-done.1
  115.7 0.1 dynamic-slice_subtract_fusion
  115.7 33.0 %reduce-scatter.5.cloned.1.call-done = f32[704,640]{1,0:T(8,128)} async-done(((f32[1408,640]{1,0:T(8,128)}), f32[704,640]{1,0:T(8,128)}) %reduce-scatter.5.cloned.1.call-update) | async-done | bytes 1802256 | tf_op jit(solution)/shard_map/reduce_scatter | solution.py:23
  148.8 1.7 reduce_max.9
  150.4 313.8 %pmax.7 = f32[704]{0:T(1024)S(1)} all-reduce(f32[704]{0:T(1024)S(1)} %reduce_max.9), channel_id=1, replica_groups=mesh['dp'=16,'vocab'=8,'tensor'=2] {'dp','vocab'}, use_global_device_ids=true, to_apply=%region_7.8 | all-reduce | flops 704 | bytes 5632 | tf_op jit(solution)/shard_map/pmax | solution.py:34
  464.2 2.9 multiply_reduce_fusion.1
  467.2 644.7 %all-reduce = (f32[704]{0:T(1024)S(1)}, f32[704]{0:T(1024)S(1)}, f32[704]{0:T(1024)S(1)}) all-reduce(f32[704]{0:T(1024)S(1)} %get-tuple-element.5, f32[704]{0:T(1024)S(1)} %get-tuple-element.6, f32[704]{0:T(1024)S(1)} %get-tuple-element.4), channel_id=1, replica_groups=mesh['dp'=16,'vocab'=8,'tensor'=2] {'dp','vocab'}, use_global_device_ids=true, to_apply=%region_11.12 | all-reduce | flops 2112 | bytes 16896 | tf_op jit(solution)/shard_map/psum | solution.py:36
  1111.9 2.7 multiply_convert_fusion
  1114.7 4.4 copy.8
  1119.1 39.5 %all-gather.5.cloned.1.call-done = bf16[1408,640]{1,0:T(8,128)(2,1)} async-done(((bf16[704,640]{1,0:T(8,128)(2,1)}), bf16[1408,640]{1,0:T(8,128)(2,1)}) %all-gather.5.cloned.1.call-update) | async-done | bytes 1802256 | tf_op jit(solution)/shard_map/all_gather | solution.py:45
  1158.5 10.9 multiply_reduce_fusion
  1169.4 5.9 copy.9
  1175.3 317.5 %psum.39 = f32[2048]{0:T(1024)} all-reduce(f32[2048]{0:T(1024)S(1)} %get-tuple-element.10), channel_id=1, replica_groups=mesh['dp'=16,'vocab'=8,'tensor'=2] {'dp','vocab'}, use_global_device_ids=true, to_apply=%region_13.14 | all-reduce | flops 2048 | bytes 16384 | tf_op jit(solution)/shard_map/psum | solution.py:50
  (14 shorter events, 0.2 us)
Async XLA Ops:
  7.2 97.7 %copy-start = (bf16[2048,640]{1,0:T(8,128)(2,1)S(1)}, bf16[2048,640]{1,0:T(8,128)(2,1)}, u32[]{:S(2)}) copy-start(bf16[2048,640]{1,0:T(8,128)(2,1)} %param.10) | copy-start | bytes 7864324
  7.2 79.6 %all-gather.3.cloned.1.call-start = ((), (), s32[]{:S(2)}) async-start(), calls=%async_computation.2 | async-start | bytes 6127616 | tf_op jit(solution)/shard_map/all_gather | solution.py:14
  14.9 133.9 %reduce-scatter.5.cloned.1.call-start = ((), (), s32[]{:S(2)}) async-start(), calls=%async_computation.4 | async-start | bytes 5406720 | tf_op jit(solution)/shard_map/reduce_scatter | solution.py:23
  96.7 0.7 copy-start.2
  96.8 8.1 copy-start.3
  96.8 367.5 %reduce-scatter.3.cloned.1.call-start = ((), (), s32[]{:S(2)}) async-start(), calls=%async_computation.3 | async-start | bytes 5406720 | tf_op jit(solution)/shard_map/reduce_scatter | solution.py:24
  115.0 0.7 copy-start.1
  115.0 1043.5 %all-gather.5.cloned.1.call-start = ((), (), s32[]{:S(2)}) async-start(), calls=%async_computation.5 | async-start | bytes 2703360 | tf_op jit(solution)/shard_map/all_gather | solution.py:45
Sparse Core Ops, SparseCore 0:
  15.0 71.7 all-gather.2
  96.9 51.8 reduce-scatter.4
  151.4 54.9 reduce-scatter.2
  1114.8 43.6 all-gather.4
where the time goes:
time: 1520 us; the launch traced here: 1500 us
  blocking collectives  1280 us (84%)
  waiting for transfers between devices  144 us (9%)
  matrix products  38.3 us (3%)
    psum x1, blocking collectives, local(): lax.psum((jnp.sum(scaled_exp, axis=1), jnp.sum(scaled_exp * tangent_logit...  645 us
    psum x1, blocking collectives, local(): lax.psum(jnp.sum(head_weight.astype(jnp.float32) * product, axis=1), ('dp...  317 us
    pmax x1, blocking collectives, local(): row_top = lax.pmax(jnp.max(logits, axis=1), ('dp', 'vocab'))  314 us
    all_gather x1, waiting for transfers between devices, local(): gathered = lax.all_gather(normed, 'dp', axis=0, tiled=True)  71.9 us
    all_gather x1, waiting for transfers between devices, local(): full_cot = lax.all_gather(cotangent, 'tensor', axis=0, tiled=True)  39.5 us
    reduce_scatter x1, waiting for transfers between devices, local(): lax.psum_scatter(logits, 'tensor', scatter_dimension=0, tiled=True)  33 us
  transfers between devices with their start and end apart: 4, of which 3 were waited for; matrix products, arithmetic and copies ran while one was open for 2% of the time, Pallas kernels for 0%

commit v1 on v0

--- a/solution.py
+++ b/solution.py
@@ -4,6 +4,30 @@
 from jax.sharding import PartitionSpec as P
 
 EPSILON = 1e-06
+
+
+def everyone(x, axis):
+    count = lax.axis_size(axis)
+    copies = jnp.broadcast_to(x[None], (count,) + x.shape)
+    return lax.all_to_all(copies, axis, 0, 0, tiled=True)
+
+
+def small_sum(x, axes):
+    for axis in axes:
+        x = jnp.sum(everyone(x, axis), axis=0)
+    return x
+
+
+def merge_stats(stats, axes):
+    for axis in axes:
+        parts = everyone(stats, axis)
+        top = jnp.max(parts[:, 0], axis=0)
+        factor = jnp.exp(parts[:, 0] - top[None])
+        total = jnp.sum(factor * parts[:, 1], axis=0)
+        weighted = jnp.sum(factor * parts[:, 2], axis=0)
+        picked = jnp.sum(parts[:, 3], axis=0)
+        stats = jnp.stack([top, total, weighted, picked])
+    return stats
 
 
 def local(residual, norm_gain, gain_dir, head_weight, head_dir, sampled):
@@ -31,13 +55,13 @@
     offset = (lax.axis_index("dp") * lax.axis_size("vocab") + lax.axis_index("vocab")) * vocab_dev
     is_picked = lax.broadcasted_iota(jnp.int32, logits.shape, 1) == (picked_ids - offset)[:, None]
     picked_part = jnp.sum(jnp.where(is_picked, tangent_logits, 0.0), axis=1)
-    row_top = lax.pmax(jnp.max(logits, axis=1), ("dp", "vocab"))
-    scaled_exp = jnp.exp(logits - row_top[:, None])
-    row_total, weighted, picked = lax.psum(
-        (jnp.sum(scaled_exp, axis=1), jnp.sum(scaled_exp * tangent_logits, axis=1), picked_part),
-        ("dp", "vocab"),
+    own_top = jnp.max(logits, axis=1)
+    scaled_exp = jnp.exp(logits - own_top[:, None])
+    own = jnp.stack(
+        [own_top, jnp.sum(scaled_exp, axis=1), jnp.sum(scaled_exp * tangent_logits, axis=1), picked_part]
     )
-    row_probs = scaled_exp / row_total[:, None]
+    row_top, row_total, weighted, picked = merge_stats(own, ("dp", "vocab"))
+    row_probs = scaled_exp * (jnp.exp(own_top - row_top) / row_total)[:, None]
     row_score = picked - weighted / row_total
     cotangent = (row_score[:, None] * (is_picked.astype(jnp.float32) - row_probs)).astype(
         jnp.bfloat16
@@ -47,7 +71,7 @@
         gathered, full_cot, (((0,), (0,)), ((), ())), preferred_element_type=jnp.float32
     )
     fisher_head = norm_gain[:, None] * product
-    fisher_gain = lax.psum(
+    fisher_gain = small_sum(
         jnp.sum(head_weight.astype(jnp.float32) * product, axis=1), ("dp", "vocab")
     )
     return (fisher_head, fisher_gain)

time: 1520 us -> 317 us (0.21); the launches traced: 1500 us -> 316 us
  blocking collectives: 1280 us -> 48.2 us
  waiting for transfers between devices: 144 us -> 186 us
    psum x2 -> x0, blocking collectives: 962 us -> none  [the longest x1 645 us: local(): lax.psum((jnp.sum(scaled_exp, axis=1), jnp.sum(scaled_exp * tangent_logit...]
    pmax x1 -> x0, blocking collectives: 314 us -> none  [local(): row_top = lax.pmax(jnp.max(logits, axis=1), ('dp', 'vocab'))]
    reduce_scatter x1, waiting for transfers between devices: 0.02 us -> 55.5 us  [local(): lax.psum_scatter(tangent_logits, 'tensor', scatter_dimension=0, tiled=True)]
    all_to_all x0 -> x3, blocking collectives: none -> 43.7 us  [everyone(): return lax.all_to_all(copies, axis, 0, 0, tiled=True)]
    all_gather x1, waiting for transfers between devices: 39.5 us -> 24.1 us  [local(): full_cot = lax.all_gather(cotangent, 'tensor', axis=0, tiled=True)]
  transfers between devices with their start and end apart: 4 -> 5, of which waited for: 3 -> 5; matrix products, arithmetic and copies ran while one was open for 2% -> 9% of each run, Pallas kernels for 0% -> 0%
where the time goes in v1:
time: 317 us; the launch traced here: 316 us
  waiting for transfers between devices  186 us (59%)
  blocking collectives  48.2 us (15%)
  matrix products  38.3 us (12%)
  between operations  14 us (4%)
  local copies, waits for them, and re-layouts  12.3 us (4%)
  other arithmetic  10.6 us (3%)
  starting transfers between devices  6.89 us (2%)
    all_gather x1, waiting for transfers between devices, local(): gathered = lax.all_gather(normed, 'dp', axis=0, tiled=True)  71.9 us
    reduce_scatter x1, waiting for transfers between devices, local(): lax.psum_scatter(tangent_logits, 'tensor', scatter_dimension=0, tiled=True)  55.5 us
    all_to_all x3, blocking collectives, everyone(): return lax.all_to_all(copies, axis, 0, 0, tiled=True)  43.7 us
    reduce_scatter x1, waiting for transfers between devices, local(): lax.psum_scatter(logits, 'tensor', scatter_dimension=0, tiled=True)  33 us
    all_gather x1, waiting for transfers between devices, local(): full_cot = lax.all_gather(cotangent, 'tensor', axis=0, tiled=True)  24.1 us
    unnamed x12, local copies, waits for them, and re-layouts  11.5 us
    dot_general x1, matrix products, local(): lax.dot_general(gathered, full_cot, (((0,), (0,)), ((), ())), preferred_e...  10.9 us
    dot_general x1, matrix products, local(): jnp.dot(hidden, head_dir, preferred_element_type=jnp.float32)  10.1 us
  transfers between devices with their start and end apart: 5, of which 5 were waited for; matrix products, arithmetic and copies ran while one was open for 9% of the time, Pallas kernels for 0%

profile of v1, /device:TPU:1, one launch (start us, length us, event | category | flops | bytes accessed | tf_op | source)
XLA Modules:
  0.0 316.2 jit_solution(15844853968231745018)
XLA Ops:
  7.2 1.3 fusion.13
  8.5 4.4 %psum.7 = f32[88]{0:T(128)S(1)} all-reduce(f32[88]{0:T(128)S(1)} %fusion.13), channel_id=1, replica_groups=mesh['dp'=16,'vocab'=8,'tensor'=2] {'tensor'}, use_global_device_ids=true, to_apply=%region_1.0 | all-reduce | flops 88 | bytes 704 | tf_op jit(solution)/shard_map/psum | solution.py:36
  13.0 1.9 fusion.14
  14.9 71.9 %all-gather.3.cloned.1.call-done = bf16[1408,2048]{1,0:T(8,128)(2,1)} async-done(((bf16[88,2048]{1,0:T(8,128)(2,1)}), bf16[1408,2048]{1,0:T(8,128)(2,1)}) %all-gather.3.cloned.1.call-update) | async-done | bytes 5767184 | tf_op jit(solution)/shard_map/all_gather | solution.py:38
  86.8 9.9 %fusion.7 = f32[1408,640]{1,0:T(8,128)} fusion(bf16[2048,640]{1,0:T(8,128)(2,1)} %param.9, bf16[1408,2048]{1,0:T(8,128)(2,1)} %all-gather.3.cloned.1.call-done, f32[2048]{0:T(1024)} %param.7), kind=kOutput, calls=%fused_computation.8 | convolution fusion | flops 3699638272 | bytes 12001280 | tf_op jit(solution)/shard_map/dot_general | solution.py:42
  97.4 7.4 %fusion.2 = f32[1408,640]{1,0:T(8,128)S(1)} fusion(bf16[2048,640]{1,0:T(8,128)(2,1)} %param.9, bf16[1408,2048]{1,0:T(8,128)(2,1)} %all-gather.3.cloned.1.call-done, f32[2048]{0:T(1024)S(1)} %copy-done.3), kind=kOutput, calls=%fused_computation.4 | convolution fusion | flops 3699638272 | bytes 12001280 | tf_op jit(solution)/shard_map/dot_general | solution.py:43
  104.9 10.1 %fusion.9 = f32[1408,640]{1,0:T(8,128)} fusion(f32[1408,640]{1,0:T(8,128)S(1)} %fusion.2, bf16[2048,640]{1,0:T(8,128)(2,1)S(1)} %copy-done, bf16[1408,2048]{1,0:T(8,128)(2,1)} %all-gather.3.cloned.1.call-done, f32[2048]{0:T(1024)S(1)} %copy-done.4), kind=kOutput, calls=%fused_computation.9 | convolution fusion | flops 3700539392 | bytes 15605760 | tf_op jit(solution)/shard_map/dot_general | solution.py:43
  115.0 0.6 copy-done.2
  115.7 33.0 %reduce-scatter.3.cloned.1.call-done = f32[704,640]{1,0:T(8,128)} async-done(((f32[1408,640]{1,0:T(8,128)}), f32[704,640]{1,0:T(8,128)}) %reduce-scatter.3.cloned.1.call-update) | async-done | bytes 1802256 | tf_op jit(solution)/shard_map/reduce_scatter | solution.py:47
  148.8 1.7 reduce_max.27
  150.4 55.5 %reduce-scatter.5.cloned.1.call-done = f32[704,640]{1,0:T(8,128)} async-done(((f32[1408,640]{1,0:T(8,128)}), f32[704,640]{1,0:T(8,128)}) %reduce-scatter.5.cloned.1.call-update) | async-done | bytes 1802256 | tf_op jit(solution)/shard_map/reduce_scatter | solution.py:48
  205.9 3.0 fusion.12
  209.1 15.2 %all_to_all.22 = f32[16,4,704]{2,1,0:T(4,128)S(1)} all-to-all(f32[16,4,704]{2,1,0:T(4,128)S(1)} %broadcast_in_dim.13), channel_id=1, replica_groups=mesh['dp'=16,'vocab'=8,'tensor'=2] {'dp'}, dimensions={0} | all-to-all | bytes 360448 | tf_op jit(solution)/shard_map/all_to_all | solution.py:12
  224.6 14.0 %all_to_all.23 = f32[8,4,704]{2,1,0:T(4,128)S(1)} all-to-all(f32[8,4,704]{2,1,0:T(4,128)S(1)} %broadcast_in_dim.14), channel_id=1, replica_groups=mesh['dp'=16,'vocab'=8,'tensor'=2] {'vocab'}, dimensions={0} | all-to-all | bytes 180224 | tf_op jit(solution)/shard_map/all_to_all | solution.py:12
  238.7 1.6 multiply_convert_fusion
  240.3 4.4 %copy.22 = bf16[2048,640]{0,1:T(8,128)(2,1)} copy(bf16[2048,640]{1,0:T(8,128)(2,1)} %param.9) | data formatting | bytes 5242880 | tf_op args[3]
  244.7 24.1 %all-gather.5.cloned.1.call-done = bf16[1408,640]{1,0:T(8,128)(2,1)} async-done(((bf16[704,640]{1,0:T(8,128)(2,1)}), bf16[1408,640]{1,0:T(8,128)(2,1)}) %all-gather.5.cloned.1.call-update) | async-done | bytes 1802256 | tf_op jit(solution)/shard_map/all_gather | solution.py:69
  268.8 10.9 %multiply_reduce_fusion = (f32[2048]{0:T(1024)S(1)}, f32[2048,640]{0,1:T(8,128)}) fusion(bf16[2048,640]{0,1:T(8,128)(2,1)} %copy.22, f32[2048]{0:T(1024)S(1)} %copy-done.4, bf16[1408,2048]{1,0:T(8,128)(2,1)} %all-gather.3.cloned.1.call-done, bf16[1408,640]{1,0:T(8,128)(2,1)} %all-gather.5.cloned.1.call-done), kind=kOutput, calls=%fused_computation.6 | convolution fusion | flops 3696228352 | bytes 15450112 | tf_op jit(solution)/shard_map/dot_general | solution.py:70
  279.7 14.6 %all_to_all.24 = f32[16,1,2048]{2,1,0:T(1,128)S(1)} all-to-all(f32[16,1,2048]{2,1,0:T(1,128)S(1)} %broadcast_in_dim.15), channel_id=1, replica_groups=mesh['dp'=16,'vocab'=8,'tensor'=2] {'dp'}, dimensions={0} | all-to-all | bytes 262144 | tf_op jit(solution)/shard_map/all_to_all | solution.py:12
  294.4 0.7 broadcast_in_dim.16
  295.0 6.7 %all-to-all-start.3 = ((f32[8,1,2048]{2,1,0:T(1,128)}), f32[8,1,2048]{2,1,0:T(1,128)S(1)}, u32[]{:S(2)}, u32[]{:S(2)}) async-start(f32[8,1,2048]{2,1,0:T(1,128)} %broadcast_in_dim.16), calls=%async_computation.5 | async-start | bytes 131072 | tf_op jit(solution)/shard_map/all_to_all | solution.py:12
  301.8 5.9 %copy.25 = f32[2048,640]{1,0:T(8,128)} copy(f32[2048,640]{0,1:T(8,128)} %get-tuple-element.20) | data formatting | bytes 10485760
  307.6 1.4 all-to-all-done.3
  309.0 0.7 reduce_sum.129
  (38 shorter events, 1.6 us)
Async XLA Ops:
  7.2 97.7 %copy-start = (bf16[2048,640]{1,0:T(8,128)(2,1)S(1)}, bf16[2048,640]{1,0:T(8,128)(2,1)}, u32[]{:S(2)}) copy-start(bf16[2048,640]{1,0:T(8,128)(2,1)} %param.10) | copy-start | bytes 7864324
  7.2 79.6 %all-gather.3.cloned.1.call-start = ((), (), s32[]{:S(2)}) async-start(), calls=%async_computation.6 | async-start | bytes 6127616 | tf_op jit(solution)/shard_map/all_gather | solution.py:38
  14.9 133.9 %reduce-scatter.3.cloned.1.call-start = ((), (), s32[]{:S(2)}) async-start(), calls=%async_computation.7 | async-start | bytes 5406720 | tf_op jit(solution)/shard_map/reduce_scatter | solution.py:47
  96.7 0.7 copy-start.3
  96.8 8.1 %copy-start.4 = (f32[2048]{0:T(1024)S(1)}, f32[2048]{0:T(1024)}, u32[]{:S(2)}) copy-start(f32[2048]{0:T(1024)} %param.7) | copy-start | bytes 24580
  96.8 109.1 %reduce-scatter.5.cloned.1.call-start = ((), (), s32[]{:S(2)}) async-start(), calls=%async_computation.8 | async-start | bytes 5406720 | tf_op jit(solution)/shard_map/reduce_scatter | solution.py:48
  115.0 0.7 copy-start.2
  115.0 153.8 %all-gather.5.cloned.1.call-start = ((), (), s32[]{:S(2)}) async-start(), calls=%async_computation.9 | async-start | bytes 2703360 | tf_op jit(solution)/shard_map/all_gather | solution.py:69
  205.9 32.8 %copy-start.1 = (f32[704,640]{1,0:T(8,128)S(1)}, f32[704,640]{1,0:T(8,128)}, u32[]{:S(2)}) copy-start(f32[704,640]{1,0:T(8,128)} %reduce-scatter.3.cloned.1.call-done) | copy-start | bytes 5406724
  295.0 14.0 %all-to-all-start.3 = ((f32[8,1,2048]{2,1,0:T(1,128)}), f32[8,1,2048]{2,1,0:T(1,128)S(1)}, u32[]{:S(2)}, u32[]{:S(2)}) async-start(f32[8,1,2048]{2,1,0:T(1,128)} %broadcast_in_dim.16), calls=%async_computation.5 | async-start | bytes 131072 | tf_op jit(solution)/shard_map/all_to_all | solution.py:12
Sparse Core Ops, SparseCore 0:
  15.0 71.7 all-gather.2
  96.9 51.8 reduce-scatter.2
  151.4 54.4 reduce-scatter.4
  240.4 28.3 all-gather.4

commit v2 on v0

v2 whole, which is shorter than its diff:
```python
import functools

import jax
import jax.numpy as jnp
from jax import lax
from jax.experimental import pallas as pl
from jax.experimental.pallas import tpu as pltpu
from jax.sharding import Mesh, PartitionSpec as P

EPSILON = 1e-06
F32 = jnp.float32
BF16 = jnp.bfloat16
I16 = jnp.int16
LANES = 128
TOP_CODE = 32000.0
MIB = 1024 * 1024
CHUNKS = (
    ((0, 0, 0), (0, 0, 1)),
    ((3, 0, 0), (3, 0, 1), (1, 0, 0), (1, 0, 1)),
    ((0, 1, 0), (0, 1, 1), (2, 0, 0), (2, 0, 1)),
    ((3, 1, 0), (3, 1, 1), (1, 1, 0), (1, 1, 1)),
    ((2, 1, 0), (2, 1, 1)),
)
BLOCKS = tuple(block for chunk in CHUNKS for block in chunk)


def whole(shape):
    return pl.BlockSpec(shape, lambda *_: (0,) * len(shape))


def front_kernel(*refs, pieces, steps, rows):
    x_refs = refs[:pieces]
    gain_ref, dir_ref, weight_ref, slope_ref, log_ref, code_ref, tan_ref, rows_ref = refs[pieces:]
    x = jnp.concatenate([r[...].astype(F32) for r in x_refs], axis=0)
    rows_ref[...] = x.astype(BF16)
    hidden = (x * gain_ref[...]).astype(BF16)
    tangent = (x * dir_ref[...]).astype(BF16)
    weight = weight_ref[...]
    log = jnp.dot(hidden, weight, preferred_element_type=F32)
    tan = jnp.dot(hidden, slope_ref[...], preferred_element_type=F32) + jnp.dot(
        tangent, weight, preferred_element_type=F32
    )
    step = pl.program_id(0)

    @pl.when(step == 0)
    def _():
        log_ref[...] = log
        tan_ref[...] = tan

    @pl.when(step > 0)
    def _():
        log_ref[...] += log
        tan_ref[...] += tan

    @pl.when(step == steps - 1)
    def _():
        value = log_ref[...]
        most = jnp.max(jnp.abs(value), axis=0, keepdims=True)
        scale = jnp.ceil(jnp.log2(jnp.maximum(most, 1e-30)) * 256.0)
        coded = jnp.round(value * (TOP_CODE * jnp.exp2(scale * (-1.0 / 256.0))))
        code_ref[:rows, :] = coded.astype(jnp.int32).astype(I16)
        code_ref[rows:, :] = jnp.broadcast_to(scale, (16, scale.shape[1])).astype(jnp.int32).astype(I16)


def front(pieces, gain, slope_gain, weight, slope, steps=2):
    rows = sum(p.shape[0] for p in pieces)
    width, cols = weight.shape
    part = width // steps
    return pl.pallas_call(
        functools.partial(front_kernel, pieces=len(pieces), steps=steps, rows=rows),
        grid=(steps,),
        in_specs=[pl.BlockSpec((p.shape[0], part), lambda k: (0, k)) for p in pieces]
        + [pl.BlockSpec((1, part), lambda k: (0, k))] * 2
        + [pl.BlockSpec((part, cols), lambda k: (k, 0))] * 2,
        out_specs=[
            whole((rows, cols)),
            whole((rows + 16, cols)),
            whole((rows, cols)),
            pl.BlockSpec((rows, part), lambda k: (0, k)),
        ],
        out_shape=[
            jax.ShapeDtypeStruct((rows, cols), F32),
            jax.ShapeDtypeStruct((rows + 16, cols), I16),
            jax.ShapeDtypeStruct((rows, cols), F32),
            jax.ShapeDtypeStruct((rows, width), BF16),
        ],
        compiler_params=pltpu.CompilerParams(vmem_limit_bytes=40 * MIB),
        cost_estimate=pl.CostEstimate(
            flops=6 * rows * width * cols,
            bytes_accessed=4 * width * cols + 4 * rows * width + 10 * rows * cols,
            transcendentals=0,
        ),
        name="front",
    )(*pieces, gain, slope_gain, weight, slope)


def column(rows_of_lanes, size):
    filled = jnp.concatenate(
        [rows_of_lanes, jnp.zeros((8 - rows_of_lanes.shape[0], LANES), F32)], axis=0
    )
    return filled.T[:size]


def expo_kernel(place_ref, log_ref, code_ref, tan_ref, ids_ref, e_ref, stats_ref, *, first, size, count):
    rows = size * count
    cols = log_ref.shape[1]
    scale = code_ref[rows:, :].astype(jnp.int32).astype(F32)[0:1]
    back = jnp.exp2(scale * (1.0 / 256.0)) * (1.0 / TOP_CODE)
    logits = log_ref[...] + code_ref[:rows, :].astype(jnp.int32).astype(F32) * back
    tan = tan_ref[...]
    top = jnp.max(logits, axis=1, keepdims=True)
    e = jnp.exp(logits - top)
    e_ref[...] = e
    total = jnp.sum(e, axis=1, keepdims=True)
    weighted = jnp.sum(e * tan, axis=1, keepdims=True)
    ids = jnp.concatenate(
        [column(ids_ref[pl.ds(place_ref[first + j], 1), :], size) for j in range(count)], axis=0
    )[:, 0:1]
    hit = lax.broadcasted_iota(jnp.int32, (rows, cols), 1).astype(F32) == ids
    picked = jnp.sum(jnp.where(hit, tan, 0.0), axis=1, keepdims=True)
    lane = lax.broadcasted_iota(jnp.int32, (rows, LANES), 1)
    stats = jnp.where(lane == 0, top, jnp.where(lane == 1, total, jnp.where(lane == 2, weighted, picked)))
    for j in range(count):
        block = jnp.concatenate(
            [stats[j * size : (j + 1) * size], jnp.zeros((LANES - size, LANES), F32)], axis=0
        ).T
        for i in range(4):
            stats_ref[i, j : j + 1, :] = block[i : i + 1, :]


def expo(place, log, code, tan, ids, first, size):
    rows, cols = log.shape
    count = rows // size
    return pl.pallas_call(
        functools.partial(expo_kernel, first=first, size=size, count=count),
        in_specs=[pl.BlockSpec(memory_space=pltpu.SMEM)] + [pl.BlockSpec(memory_space=pltpu.VMEM)] * 4,
        out_specs=[pl.BlockSpec(memory_space=pltpu.VMEM)] * 2,
        out_shape=[
            jax.ShapeDtypeStruct((rows, cols), F32),
            jax.ShapeDtypeStruct((4, count, LANES), F32),
        ],
        compiler_params=pltpu.CompilerParams(vmem_limit_bytes=40 * MIB),
        cost_estimate=pl.CostEstimate(
            flops=12 * rows * cols, bytes_accessed=14 * rows * cols, transcendentals=rows * cols
        ),
        name="expo",
    )(place, log, code, tan, ids)


def merge(parts):
    count = parts.shape[0]
    top = parts[0, 0]
    for s in range(1, count):
        top = jnp.maximum(top, parts[s, 0])
    total = jnp.zeros_like(top)
    weighted = jnp.zeros_like(top)
    picked = jnp.zeros_like(top)
    for s in range(count):
        factor = jnp.exp(parts[s, 0] - top)
        total += factor * parts[s, 1]
        weighted += factor * parts[s, 2]
        picked += parts[s, 3]
    return top, total, weighted, picked


def first_merge_kernel(place_ref, parts_ref, out_ref):
    merged = merge(parts_ref)
    for i in range(4):
        for b in range(len(BLOCKS)):
            out_ref[i, pl.ds(place_ref[b], 1), :] = merged[i][b : b + 1]


def last_merge_kernel(parts_ref, out_ref, *, repeats):
    top, total, weighted, picked = merge(parts_ref)
    total = total * (1.0 / repeats)
    score = picked - weighted / total
    out_ref[0] = top
    out_ref[1] = score
    out_ref[2] = score / total
    out_ref[3] = total


def small_kernel(kernel, name, shape, *args):
    specs = [
        pl.BlockSpec(memory_space=pltpu.SMEM if a.dtype == jnp.int32 else pltpu.VMEM) for a in args
    ]
    return pl.pallas_call(
        kernel,
        in_specs=specs,
        out_specs=pl.BlockSpec(memory_space=pltpu.VMEM),
        out_shape=jax.ShapeDtypeStruct(shape, F32),
        compiler_params=pltpu.CompilerParams(vmem_limit_bytes=16 * MIB),
        name=name,
    )(*args)


def product_kernel(*refs, chunks, size, pairs):
    place_ref, ids_ref, merged_ref = refs[:3]
    e_refs = refs[3 : 3 + chunks]
    stats_refs = refs[3 + chunks : 3 + 2 * chunks]
    x_refs = refs[3 + 2 * chunks : 3 + 3 * chunks]
    weight_ref, gain_ref, out_ref, part_ref, cot_ref = refs[3 + 3 * chunks :]

    @pl.when(pl.program_id(0) == 0)
    def _():
        base = 0
        for chunk in range(chunks):
            count = e_refs[chunk].shape[0] // size
            for j in range(0, count, 2):
                both = []
                for i in (j, j + 1):
                    spot = place_ref[base + i]
                    score = merged_ref[1, pl.ds(spot, 1), :]
                    own = stats_refs[chunk][0, i : i + 1, :]
                    coef = jnp.exp(own - merged_ref[0, pl.ds(spot, 1), :]) * merged_ref[2, pl.ds(spot, 1), :]
                    cols = column(
                        jnp.concatenate([coef, score, ids_ref[pl.ds(spot, 1), :]], axis=0), size
                    )
                    e = e_refs[chunk][i * size : (i + 1) * size, :]
                    hit = lax.broadcasted_iota(jnp.int32, e.shape, 1).astype(F32) == cols[:, 2:3]
                    both.append(jnp.where(hit, cols[:, 1:2], 0.0) - cols[:, 0:1] * e)
                start = (base + j) * size
                cot_ref[start : start + 2 * size, :] = jnp.concatenate(both, axis=0).astype(BF16)
            base += count

    x = jnp.concatenate([r[...] for r in x_refs], axis=0)
    product = lax.dot_general(x, cot_ref[...], (((0,), (0,)), ((), ())), preferred_element_type=F32)
    out_ref[...] = gain_ref[...] * product
    part = jnp.sum(weight_ref[...].astype(F32) * product, axis=1, keepdims=True)
    part_ref[...] = jnp.broadcast_to(part, (part.shape[0], LANES)).T[:8]


def finish(place, ids, merged, e, stats, x, weight, gain, size, block=512):
    width, cols = weight.shape
    rows = sum(a.shape[0] for a in x)
    chunks = len(x)
    return pl.pallas_call(
        functools.partial(product_kernel, chunks=chunks, size=size, pairs=rows // (2 * size)),
        grid=(width // block,),
        in_specs=[pl.BlockSpec(memory_space=pltpu.SMEM), whole(ids.shape), whole(merged.shape)]
        + [whole(a.shape) for a in e]
        + [whole(a.shape) for a in stats]
        + [pl.BlockSpec((a.shape[0], block), lambda i: (0, i)) for a in x]
        + [pl.BlockSpec((block, cols), lambda i: (i, 0)), pl.BlockSpec((block, 1), lambda i: (i, 0))],
        out_specs=[
            pl.BlockSpec((block, cols), lambda i: (i, 0)),
            pl.BlockSpec((8, block), lambda i: (0, i)),
        ],
        out_shape=[
            jax.ShapeDtypeStruct((width, cols), F32),
            jax.ShapeDtypeStruct((8, width), F32),
        ],
        scratch_shapes=[pltpu.VMEM((rows, cols), BF16)],
        compiler_params=pltpu.CompilerParams(vmem_limit_bytes=48 * MIB),
        cost_estimate=pl.CostEstimate(
            flops=2 * rows * width * cols,
            bytes_accessed=4 * rows * cols + 2 * rows * width + 6 * width * cols,
            transcendentals=0,
        ),
        name="product",
    )(place, ids, merged, *e, *stats, *x, weight, gain)


def everyone(x, axes):
    count = 1
    for axis in axes:
        count *= lax.axis_size(axis)
    copies = jnp.broadcast_to(x[None], (count,) + x.shape)
    return lax.all_to_all(copies, axes, 0, 0, tiled=True)


def shift(x, axes, by):
    count = 1
    for axis in axes:
        count *= lax.axis_size(axis)
    return lax.ppermute(x, axes, [(i, (i + by) % count) for i in range(count)])


def swap(x, axis):
    return lax.ppermute(x, (axis,), [(0, 1), (1, 0)])


def local(residual, norm_gain, gain_dir, head_weight, head_dir, sampled):
    size, width = residual.shape
    vocab_dev = head_weight.shape[1]
    x_at, y_at, c_at, z_at = (lax.axis_index(a) for a in ("x", "yh", "c", "z"))
    around = lax.axis_size("x")
    place = jnp.stack(
        [(((x_at + o) % around) * 2 + (y_at ^ h)) * 2 + (c_at ^ g) for o, h, g in BLOCKS]
    ).astype(jnp.int32)
    offset = (((x_at * 2 + y_at) * 2 + c_at) * lax.axis_size("z") + z_at) * vocab_dev
    ids = jnp.pad(
        (sampled - offset).astype(F32).reshape(len(BLOCKS), size), ((0, 0), (0, LANES - size))
    )
    gain_row, dir_row, gain_col = norm_gain[None], gain_dir[None], norm_gain[:, None]

    entries = residual.astype(F32)
    squares = lax.psum(jnp.sum(entries * entries, axis=1), "t")
    normed = (entries * lax.rsqrt(squares / (2 * width) + EPSILON)[:, None]).astype(BF16)

    half = (size // 2 + 8) // 16 * 16
    ring = ("yh", "t")
    up = shift(shift(normed[:half], ring, 1), ring, 1)
    down = shift(shift(normed[half:], ring, -1), ring, -1)
    across = jnp.concatenate([up, down], axis=0)
    got = {}
    for h, block in ((0, normed), (1, across)):
        before, after = shift(block, ("x",), 1), shift(block, ("x",), -1)
        far = [shift(before[:half], ("x",), 1), shift(after[half:], ("x",), -1)]
        for o, pieces in ((0, [block]), (3, [before]), (1, [after]), (2, far)):
            got[o, h, 0] = pieces
            got[o, h, 1] = [swap(p, "c") for p in pieces]

    logs, tans, xs, es, stats = [], [], [], [], []
    first = 0
    for chunk in CHUNKS:
        pieces = [p for b in chunk for p in got[b]]
        log, code, tan, rows = front(pieces, gain_row, dir_row, head_weight, head_dir)
        e, stat = expo(place, log, swap(code, "t"), tan, ids, first, size)
        xs.append(rows)
        es.append(e)
        stats.append(stat)
        first += len(chunk)
    own = jnp.concatenate(stats, axis=1)
    shape = own.shape
    near = small_kernel(first_merge_kernel, "first_merge", shape, place, everyone(own, ("z",)))
    merged = small_kernel(
        functools.partial(last_merge_kernel, repeats=2.0),
        "last_merge",
        shape,
        everyone(near, ("x", "yh", "c", "t")),
    )
    fisher_head, part = finish(place, ids, merged, es, stats, xs, head_weight, gain_col, size)
    part = jnp.sum(everyone(part[0], ("x", "yh", "c")), axis=0)
    fisher_gain = jnp.sum(everyone(part, ("z",)), axis=0)
    return (fisher_head, fisher_gain)


def solution(mesh):
    fine = Mesh(mesh.devices.reshape(4, 2, 2, 8, 2), ("x", "yh", "c", "z", "t"))
    dp, vocab = ("x", "yh", "c"), ("x", "yh", "c", "z")
    in_specs = (P(dp, "t"), P("t"), P("t"), P("t", vocab), P("t", vocab), P())
    out_specs = (P("t", vocab), P("t"))
    return jax.shard_map(local, mesh=fine, in_specs=in_specs, out_specs=out_specs, check_vma=False)
```

time: 1520 us -> 201 us (0.13); the launches traced: 1500 us -> 200 us
  blocking collectives: 1280 us -> 41.9 us
  waiting for transfers between devices: 144 us -> 45.6 us
  Pallas kernels: 0 us -> 40.4 us
  starting transfers between devices: 0.16 us -> 40.2 us
  matrix products: 38.3 us -> 0 us
  local copies, waits for them, and re-layouts: 11.5 us -> 27.6 us
    psum x3 -> x1, blocking collectives: 967 us -> 4.44 us  [local(): squares = lax.psum(jnp.sum(entries * entries, axis=1), 't')]
    pmax x1 -> x0, blocking collectives: 314 us -> none  [local(): row_top = lax.pmax(jnp.max(logits, axis=1), ('dp', 'vocab'))]
    all_gather x2 -> x0, waiting for transfers between devices: 111 us -> none  [the longest x1 71.9 us: local(): gathered = lax.all_gather(normed, 'dp', axis=0, tiled=True)]
    pallas_call x0 -> x13, Pallas kernels: none -> 40.4 us  [the longest x5 21.7 us: front(): pl.pallas_call(functools.partial(front_kernel, pieces=len(pieces), steps=...]
    dot_general x4 -> x0, matrix products: 38.3 us -> none  [the longest x1 10.9 us: local(): lax.dot_general(gathered, full_cot, (((0,), (0,)), ((), ())), preferred_e...]
    all_to_all x0 -> x3, blocking collectives: none -> 37.5 us  [everyone(): return lax.all_to_all(copies, axes, 0, 0, tiled=True)]
    reduce_scatter x2 -> x0, waiting for transfers between devices: 33 us -> none  [the longest x1 33 us: local(): lax.psum_scatter(logits, 'tensor', scatter_dimension=0, tiled=True)]
    ppermute x0 -> x27, starting transfers between devices: none -> 32.3 us  [the longest x12 17.4 us: shift(): return lax.ppermute(x, axes, [(i, (i + by) % count) for i in range(count)])]
  transfers between devices with their start and end apart: 4 -> 28, of which waited for: 3 -> 5; matrix products, arithmetic and copies ran while one was open for 2% -> 1% of each run, Pallas kernels for 0% -> 14%
where the time goes in v2:
time: 201 us; the launch traced here: 200 us
  waiting for transfers between devices  45.6 us (23%)
  blocking collectives  41.9 us (21%)
  Pallas kernels  40.4 us (20%)
  starting transfers between devices  40.2 us (20%)
  local copies, waits for them, and re-layouts  27.6 us (14%)
  other arithmetic  3.17 us (2%)
    all_to_all x3, blocking collectives, everyone(): return lax.all_to_all(copies, axes, 0, 0, tiled=True)  37.5 us
    unnamed x83, local copies, waits for them, and re-layouts  24.6 us
    pallas_call x5, Pallas kernels, front(): pl.pallas_call(functools.partial(front_kernel, pieces=len(pieces), steps=...  21.7 us
    ppermute x12, starting transfers between devices, shift(): return lax.ppermute(x, axes, [(i, (i + by) % count) for i in range(count)])  17.4 us
    all_to_all x1, waiting for transfers between devices, everyone(): return lax.all_to_all(copies, axes, 0, 0, tiled=True)  16 us
    ppermute x15, waiting for transfers between devices, swap(): return lax.ppermute(x, (axis,), [(0, 1), (1, 0)])  15.5 us
    ppermute x15, starting transfers between devices, swap(): return lax.ppermute(x, (axis,), [(0, 1), (1, 0)])  15 us
    ppermute x12, waiting for transfers between devices, shift(): return lax.ppermute(x, axes, [(i, (i + by) % count) for i in range(count)])  14.1 us
  transfers between devices with their start and end apart: 28, of which 5 were waited for; matrix products, arithmetic and copies ran while one was open for 1% of the time, Pallas kernels for 14%

profile of v2, /device:TPU:1, one launch (start us, length us, event | category | flops | bytes accessed | tf_op | source)
XLA Modules:
  0.0 199.9 jit_solution(5179154457904150638)
XLA Ops:
  2.0 4.4 %psum.7 = f32[88]{0:T(128)S(1)} all-reduce(f32[88]{0:T(128)S(1)} %fusion), channel_id=1, replica_groups=mesh['x'=4,'yh'=2,'c'=2,'z'=8,'t'=2] {'t'}, use_global_device_ids=true, to_apply=%region_1.2 | all-reduce | flops 88 | bytes 704 | tf_op jit(solution)/shard_map/psum | solution.py:298
  9.1 2.5 %collective-permute-start.4 = (bf16[88,2048]{1,0:T(8,128)(2,1)S(1)}, bf16[88,2048]{1,0:T(8,128)(2,1)S(1)}, u32[]{:S(2)}, u32[]{:S(2)}) collective-permute-start(bf16[88,2048]{1,0:T(8,128)(2,1)S(1)} %fusion.1.refs_0_), channel_id=1, source_target_pairs={{0,192},{64,0},{128,64},{192,128},{1,193},{65,1},{129,65},{193,129... | collective-permute-start | bytes 1081352 | tf_op jit(solution)/shard_map/ppermute | solution.py:276
  11.6 2.0 %collective-permute-done.7 = bf16[48,2048]{1,0:T(8,128)(2,1)S(1)} collective-permute-done((bf16[48,2048]{1,0:T(8,128)(2,1)S(1)}, bf16[48,2048]{1,0:T(8,128)(2,1)S(1)}, u32[]{:S(2)}, u32[]{:S(2)}) %collective-permute-start.7) | collective-permute-done | bytes 196640 | tf_op jit(solution)/shard_map/ppermute | solution.py:276
  13.7 2.7 %collective-permute-start.9 = (bf16[40,2048]{1,0:T(8,128)(2,1)S(1)}, bf16[40,2048]{1,0:T(8,128)(2,1)S(1)}, u32[]{:S(2)}, u32[]{:S(2)}) collective-permute-start(bf16[40,2048]{1,0:T(8,128)(2,1)S(1)} %slice.32), channel_id=1, source_target_pairs={{0,33},{1,0},{32,1},{33,32},{2,35},{3,2},{34,3},{35,34},{4,37},{5,... | collective-permute-start | bytes 491528 | tf_op jit(solution)/shard_map/ppermute | solution.py:276
  16.4 2.3 %collective-permute-done.9 = bf16[40,2048]{1,0:T(8,128)(2,1)S(1)} collective-permute-done((bf16[40,2048]{1,0:T(8,128)(2,1)S(1)}, bf16[40,2048]{1,0:T(8,128)(2,1)S(1)}, u32[]{:S(2)}, u32[]{:S(2)}) %collective-permute-start.9) | collective-permute-done | bytes 163872 | tf_op jit(solution)/shard_map/ppermute | solution.py:276
  18.7 3.4 %collective-permute-start.10 = (bf16[40,2048]{1,0:T(8,128)(2,1)S(1)}, bf16[40,2048]{1,0:T(8,128)(2,1)S(1)}, u32[]{:S(2)}, u32[]{:S(2)}) collective-permute-start(bf16[40,2048]{1,0:T(8,128)(2,1)S(1)} %collective-permute-done.9), channel_id=1, source_target_pairs={{0,33},{1,0},{32,1},{33,32},{2,35},{3,2},{34,3},{35,34},{4,37},{5,... | collective-permute-start | bytes 491528 | tf_op jit(solution)/shard_map/ppermute | solution.py:276
  22.1 2.6 %collective-permute-start.13 = (bf16[40,2048]{1,0:T(8,128)(2,1)S(1)}, bf16[40,2048]{1,0:T(8,128)(2,1)S(1)}, u32[]{:S(2)}, u32[]{:S(2)}) collective-permute-start(bf16[40,2048]{1,0:T(8,128)(2,1)S(1)} %slice.34), channel_id=1, source_target_pairs={{0,192},{64,0},{128,64},{192,128},{1,193},{65,1},{129,65},{193,129... | collective-permute-start | bytes 491528 | tf_op jit(solution)/shard_map/ppermute | solution.py:276
  24.6 5.6 %collective-permute-start.5 = (bf16[88,2048]{1,0:T(8,128)(2,1)S(1)}, bf16[88,2048]{1,0:T(8,128)(2,1)S(1)}, u32[]{:S(2)}, u32[]{:S(2)}) collective-permute-start(bf16[88,2048]{1,0:T(8,128)(2,1)S(1)} %collective-permute-done.4.refs_2_), channel_id=1, source_target_pairs={{0,16},{16,0},{1,17},{17,1},{2,18},{18,2},{3,19},{19,3},{4,20},{20... | collective-permute-start | bytes 1081352 | tf_op jit(solution)/shard_map/ppermute | solution.py:280
  33.7 9.8 %collective-permute-done.12.refs_2_ = bf16[48,2048]{1,0:T(8,128)(2,1)S(1)} collective-permute-done((bf16[48,2048]{1,0:T(8,128)(2,1)S(1)}, bf16[48,2048]{1,0:T(8,128)(2,1)S(1)}, u32[]{:S(2)}, u32[]{:S(2)}) %collective-permute-start.12) | collective-permute-done | bytes 196640 | tf_op jit(solution)/shard_map/ppermute | solution.py:276
  43.5 3.4 %collective-permute-start.11 = (bf16[88,2048]{1,0:T(8,128)(2,1)S(1)}, bf16[88,2048]{1,0:T(8,128)(2,1)S(1)}, u32[]{:S(2)}, u32[]{:S(2)}) collective-permute-start(bf16[88,2048]{1,0:T(8,128)(2,1)S(1)} %constant_dynamic-update-slice_fusion.refs_0_), channel_id=1, source_target_pairs={{0,16},{16,0},{1,17},{17,1},{2,18},{18,2},{3,19},{19,3},{4,20},{20... | collective-permute-start | bytes 1081352 | tf_op jit(solution)/shard_map/ppermute | solution.py:280
  49.7 5.1 %front.6 = (f32[352,640]{1,0:T(8,128)S(1)}, s16[368,640]{1,0:T(8,128)(2,1)}, f32[352,640]{1,0:T(8,128)S(1)}, bf16[352,2048]{1,0:T(8,128)(2,1)S(1)}) custom-call(bf16[88,2048]{1,0:T(8,128)(2,1)S(1)} %collective-permute-done.2.refs_0_, bf16[88,2048]{1,0:T(8,128)(2,1)S(1)} %collective-permute-done.3.refs_1_, ...), custom_call_target="tpu_custom_call" | custom-call | flops 2768240640 | bytes 10379264 | tf_op jit(solution)/shard_map/front/pallas_call | solution.py:69
  58.7 5.1 %front.7 = (f32[352,640]{1,0:T(8,128)S(1)}, s16[368,640]{1,0:T(8,128)(2,1)}, f32[352,640]{1,0:T(8,128)S(1)}, bf16[352,2048]{1,0:T(8,128)(2,1)S(1)}) custom-call(bf16[88,2048]{1,0:T(8,128)(2,1)S(1)} %constant_dynamic-update-slice_fusion.refs_0_, bf16[88,2048]{1,0:T(8,128)(2,1)S(1)} %collective-permute-done.11.refs_1_, ...), custom_call_target="tpu_custom_call" | custom-call | flops 2768240640 | bytes 10379264 | tf_op jit(solution)/shard_map/front/pallas_call | solution.py:69
  69.9 5.1 %front.8 = (f32[352,640]{1,0:T(8,128)S(1)}, s16[368,640]{1,0:T(8,128)(2,1)}, f32[352,640]{1,0:T(8,128)S(1)}, bf16[352,2048]{1,0:T(8,128)(2,1)S(1)}) custom-call(bf16[88,2048]{1,0:T(8,128)(2,1)S(1)} %collective-permute-done.17.refs_0_, bf16[88,2048]{1,0:T(8,128)(2,1)S(1)} %collective-permute-done.18.refs_1_, ...), custom_call_target="tpu_custom_call" | custom-call | flops 2768240640 | bytes 10379264 | tf_op jit(solution)/shard_map/front/pallas_call | solution.py:69
  76.0 3.1 %front.5 = (f32[176,640]{1,0:T(8,128)S(1)}, s16[192,640]{1,0:T(8,128)(2,1)}, f32[176,640]{1,0:T(8,128)S(1)}, bf16[176,2048]{1,0:T(8,128)(2,1)S(1)}) custom-call(bf16[88,2048]{1,0:T(8,128)(2,1)S(1)} %fusion.1.refs_0_, bf16[88,2048]{1,0:T(8,128)(2,1)S(1)} %collective-permute-done.refs_1_, f32[1,2048]{1,0:T(1,128)S(1)} %bitcast.23, f32[1,2048]{1,0:T(1,128)S(1)} %bitcast.29, ...), custom_call_target="tpu_custom_call" | custom-call | flops 1384120320 | bytes 7811072 | tf_op jit(solution)/shard_map/front/pallas_call | solution.py:69
  83.0 3.1 %front.9 = (f32[176,640]{1,0:T(8,128)S(1)}, s16[192,640]{1,0:T(8,128)(2,1)}, f32[176,640]{1,0:T(8,128)S(1)}, bf16[176,2048]{1,0:T(8,128)(2,1)S(1)}) custom-call(bf16[48,2048]{1,0:T(8,128)(2,1)S(1)} %collective-permute-done.22.refs_0_, bf16[40,2048]{1,0:T(8,128)(2,1)S(1)} %collective-permute-done.23.refs_1_, ...), custom_call_target="tpu_custom_call" | custom-call | flops 1384120320 | bytes 7811072 | tf_op jit(solution)/shard_map/front/pallas_call | solution.py:69
  88.8 15.4 %collective-permute-done.1.code_ref = s16[192,640]{1,0:T(8,128)(2,1)} collective-permute-done((s16[192,640]{1,0:T(8,128)(2,1)}, s16[192,640]{1,0:T(8,128)(2,1)}, u32[]{:S(2)}, u32[]{:S(2)}) %collective-permute-start.1) | collective-permute-done | bytes 245792 | tf_op jit(solution)/shard_map/ppermute | solution.py:280
  109.7 1.8 expo.6
  115.9 1.9 expo.8
  118.9 16.7 %all_to_all.22.parts_ref = f32[8,4,16,128]{3,2,1,0:T(8,128)S(1)} all-to-all(f32[8,4,16,128]{3,2,1,0:T(8,128)S(1)} %broadcast_in_dim.16), channel_id=1, replica_groups=mesh['x'=4,'yh'=2,'c'=2,'z'=8,'t'=2] {'z'}, dimensions={0} | all-to-all | bytes 524288 | tf_op jit(solution)/shard_map/all_to_all | solution.py:269
  137.4 7.9 %all-to-all-start.1 = ((f32[32,4,16,128]{3,2,1,0:T(8,128)}), f32[32,4,16,128]{3,2,1,0:T(8,128)S(1)}, u32[]{:S(2)}, u32[]{:S(2)}) async-start(f32[32,4,16,128]{3,2,1,0:T(8,128)} %broadcast_in_dim.17), calls=%async_computation.1 | async-start | bytes 2097152 | tf_op jit(solution)/shard_map/all_to_all | solution.py:269
  146.6 16.0 %all-to-all-done.1.parts_ref = f32[32,4,16,128]{3,2,1,0:T(8,128)S(1)} async-done(((f32[32,4,16,128]{3,2,1,0:T(8,128)}), f32[32,4,16,128]{3,2,1,0:T(8,128)S(1)}, u32[]{:S(2)}, u32[]{:S(2)}) %all-to-all-start.1) | async-done | bytes 1048608 | tf_op jit(solution)/shard_map/all_to_all | solution.py:269
  168.2 10.1 %product.1 = (f32[2048,640]{1,0:T(8,128)}, f32[8,2048]{1,0:T(8,128)S(1)}) custom-call(s32[16]{0:T(128)S(1)} %stack.67.place_ref.refs_0_, f32[16,128]{1,0:T(8,128)S(1)} %pad.4.ids_ref.refs_1_, f32[4,16,128]{2,1,0:T(8,128)S(1)} %last_merge.1.refs_2_, f32[176,640]{1,0:T(8,128)S(1)} %copy-done.34, f32[352,640]{1,0:T(8,128)S(1)} %copy-done.24, ...), custom_call_target="tpu_custom_call" | custom-call | flops 3690987520 | bytes 17235968 | tf_op jit(solution)/shard_map/product/pallas_call | solution.py:237
  178.3 11.2 %all_to_all.23 = f32[16,1,2048]{2,1,0:T(1,128)S(1)} all-to-all(f32[16,1,2048]{2,1,0:T(1,128)S(1)} %broadcast_in_dim.38), channel_id=1, replica_groups=mesh['x'=4,'yh'=2,'c'=2,'z'=8,'t'=2] {'x','yh','c'}, dimensions={0} | all-to-all | bytes 262144 | tf_op jit(solution)/shard_map/all_to_all | solution.py:269
  189.7 9.5 %all_to_all.24 = f32[8,1,2048]{2,1,0:T(1,128)S(1)} all-to-all(f32[8,1,2048]{2,1,0:T(1,128)S(1)} %broadcast_in_dim.39), channel_id=1, replica_groups=mesh['x'=4,'yh'=2,'c'=2,'z'=8,'t'=2] {'z'}, dimensions={0} | all-to-all | bytes 131072 | tf_op jit(solution)/shard_map/all_to_all | solution.py:269
  (155 shorter events, 47.9 us)
Async XLA Ops:
  9.1 12.9 %collective-permute-start.4 = (bf16[88,2048]{1,0:T(8,128)(2,1)S(1)}, bf16[88,2048]{1,0:T(8,128)(2,1)S(1)}, u32[]{:S(2)}, u32[]{:S(2)}) collective-permute-start(bf16[88,2048]{1,0:T(8,128)(2,1)S(1)} %fusion.1.refs_0_), channel_id=1, source_target_pairs={{0,192},{64,0},{128,64},{192,128},{1,193},{65,1},{129,65},{193,129... | collective-permute-start | bytes 1081352 | tf_op jit(solution)/shard_map/ppermute | solution.py:276
  11.6 18.7 %collective-permute-start.2 = (bf16[88,2048]{1,0:T(8,128)(2,1)S(1)}, bf16[88,2048]{1,0:T(8,128)(2,1)S(1)}, u32[]{:S(2)}, u32[]{:S(2)}) collective-permute-start(bf16[88,2048]{1,0:T(8,128)(2,1)S(1)} %fusion.1.refs_0_), channel_id=1, source_target_pairs={{0,64},{64,128},{128,192},{192,0},{1,65},{65,129},{129,193},{193,1... | collective-permute-start | bytes 1081352 | tf_op jit(solution)/shard_map/ppermute | solution.py:276
  13.6 16.8 %collective-permute-start.8 = (bf16[48,2048]{1,0:T(8,128)(2,1)S(1)}, bf16[48,2048]{1,0:T(8,128)(2,1)S(1)}, u32[]{:S(2)}, u32[]{:S(2)}) collective-permute-start(bf16[48,2048]{1,0:T(8,128)(2,1)S(1)} %collective-permute-done.7), channel_id=1, source_target_pairs={{0,1},{1,32},{32,33},{33,0},{2,3},{3,34},{34,35},{35,2},{4,5},{5,3... | collective-permute-start | bytes 589832 | tf_op jit(solution)/shard_map/ppermute | solution.py:276
  18.7 11.8 %collective-permute-start.10 = (bf16[40,2048]{1,0:T(8,128)(2,1)S(1)}, bf16[40,2048]{1,0:T(8,128)(2,1)S(1)}, u32[]{:S(2)}, u32[]{:S(2)}) collective-permute-start(bf16[40,2048]{1,0:T(8,128)(2,1)S(1)} %collective-permute-done.9), channel_id=1, source_target_pairs={{0,33},{1,0},{32,1},{33,32},{2,35},{3,2},{34,3},{35,34},{4,37},{5,... | collective-permute-start | bytes 491528 | tf_op jit(solution)/shard_map/ppermute | solution.py:276
  22.1 10.1 %collective-permute-start.13 = (bf16[40,2048]{1,0:T(8,128)(2,1)S(1)}, bf16[40,2048]{1,0:T(8,128)(2,1)S(1)}, u32[]{:S(2)}, u32[]{:S(2)}) collective-permute-start(bf16[40,2048]{1,0:T(8,128)(2,1)S(1)} %slice.34), channel_id=1, source_target_pairs={{0,192},{64,0},{128,64},{192,128},{1,193},{65,1},{129,65},{193,129... | collective-permute-start | bytes 491528 | tf_op jit(solution)/shard_map/ppermute | solution.py:276
  24.6 22.2 %collective-permute-start.5 = (bf16[88,2048]{1,0:T(8,128)(2,1)S(1)}, bf16[88,2048]{1,0:T(8,128)(2,1)S(1)}, u32[]{:S(2)}, u32[]{:S(2)}) collective-permute-start(bf16[88,2048]{1,0:T(8,128)(2,1)S(1)} %collective-permute-done.4.refs_2_), channel_id=1, source_target_pairs={{0,16},{16,0},{1,17},{17,1},{2,18},{18,2},{3,19},{19,3},{4,20},{20... | collective-permute-start | bytes 1081352 | tf_op jit(solution)/shard_map/ppermute | solution.py:280
  30.3 16.6 %collective-permute-start.3 = (bf16[88,2048]{1,0:T(8,128)(2,1)S(1)}, bf16[88,2048]{1,0:T(8,128)(2,1)S(1)}, u32[]{:S(2)}, u32[]{:S(2)}) collective-permute-start(bf16[88,2048]{1,0:T(8,128)(2,1)S(1)} %collective-permute-done.2.refs_0_), channel_id=1, source_target_pairs={{0,16},{16,0},{1,17},{17,1},{2,18},{18,2},{3,19},{19,3},{4,20},{20... | collective-permute-start | bytes 1081352 | tf_op jit(solution)/shard_map/ppermute | solution.py:280
  30.5 16.9 %collective-permute-start.19 = (bf16[88,2048]{1,0:T(8,128)(2,1)S(1)}, bf16[88,2048]{1,0:T(8,128)(2,1)S(1)}, u32[]{:S(2)}, u32[]{:S(2)}) collective-permute-start(bf16[88,2048]{1,0:T(8,128)(2,1)S(1)} %constant_dynamic-update-slice_fusion.refs_0_), channel_id=1, source_target_pairs={{0,192},{64,0},{128,64},{192,128},{1,193},{65,1},{129,65},{193,129... | collective-permute-start | bytes 1081352 | tf_op jit(solution)/shard_map/ppermute | solution.py:276
  30.5 16.9 %collective-permute-start.17 = (bf16[88,2048]{1,0:T(8,128)(2,1)S(1)}, bf16[88,2048]{1,0:T(8,128)(2,1)S(1)}, u32[]{:S(2)}, u32[]{:S(2)}) collective-permute-start(bf16[88,2048]{1,0:T(8,128)(2,1)S(1)} %constant_dynamic-update-slice_fusion.refs_0_), channel_id=1, source_target_pairs={{0,64},{64,128},{128,192},{192,0},{1,65},{65,129},{129,193},{193,1... | collective-permute-start | bytes 1081352 | tf_op jit(solution)/shard_map/ppermute | solution.py:276
  32.2 11.3 %collective-permute-start.12 = (bf16[48,2048]{1,0:T(8,128)(2,1)S(1)}, bf16[48,2048]{1,0:T(8,128)(2,1)S(1)}, u32[]{:S(2)}, u32[]{:S(2)}) collective-permute-start(bf16[48,2048]{1,0:T(8,128)(2,1)S(1)} %slice.33), channel_id=1, source_target_pairs={{0,64},{64,128},{128,192},{192,0},{1,65},{65,129},{129,193},{193,1... | collective-permute-start | bytes 589832 | tf_op jit(solution)/shard_map/ppermute | solution.py:276
  43.5 13.8 %collective-permute-start.11 = (bf16[88,2048]{1,0:T(8,128)(2,1)S(1)}, bf16[88,2048]{1,0:T(8,128)(2,1)S(1)}, u32[]{:S(2)}, u32[]{:S(2)}) collective-permute-start(bf16[88,2048]{1,0:T(8,128)(2,1)S(1)} %constant_dynamic-update-slice_fusion.refs_0_), channel_id=1, source_target_pairs={{0,16},{16,0},{1,17},{17,1},{2,18},{18,2},{3,19},{19,3},{4,20},{20... | collective-permute-start | bytes 1081352 | tf_op jit(solution)/shard_map/ppermute | solution.py:280
  46.9 10.0 %collective-permute-start.15 = (bf16[40,2048]{1,0:T(8,128)(2,1)S(1)}, bf16[40,2048]{1,0:T(8,128)(2,1)S(1)}, u32[]{:S(2)}, u32[]{:S(2)}) collective-permute-start(bf16[40,2048]{1,0:T(8,128)(2,1)S(1)} %collective-permute-done.13.refs_3_), channel_id=1, source_target_pairs={{0,16},{16,0},{1,17},{17,1},{2,18},{18,2},{3,19},{19,3},{4,20},{20... | collective-permute-start | bytes 491528 | tf_op jit(solution)/shard_map/ppermute | solution.py:280
  46.9 11.2 %collective-permute-start.14 = (bf16[48,2048]{1,0:T(8,128)(2,1)S(1)}, bf16[48,2048]{1,0:T(8,128)(2,1)S(1)}, u32[]{:S(2)}, u32[]{:S(2)}) collective-permute-start(bf16[48,2048]{1,0:T(8,128)(2,1)S(1)} %collective-permute-done.12.refs_2_), channel_id=1, source_target_pairs={{0,16},{16,0},{1,17},{17,1},{2,18},{18,2},{3,19},{19,3},{4,20},{20... | collective-permute-start | bytes 589832 | tf_op jit(solution)/shard_map/ppermute | solution.py:280
  47.4 21.0 %collective-permute-start.20 = (bf16[88,2048]{1,0:T(8,128)(2,1)S(1)}, bf16[88,2048]{1,0:T(8,128)(2,1)S(1)}, u32[]{:S(2)}, u32[]{:S(2)}) collective-permute-start(bf16[88,2048]{1,0:T(8,128)(2,1)S(1)} %collective-permute-done.19.refs_2_), channel_id=1, source_target_pairs={{0,16},{16,0},{1,17},{17,1},{2,18},{18,2},{3,19},{19,3},{4,20},{20... | collective-permute-start | bytes 1081352 | tf_op jit(solution)/shard_map/ppermute | solution.py:280
  47.5 22.3 %collective-permute-start.18 = (bf16[88,2048]{1,0:T(8,128)(2,1)S(1)}, bf16[88,2048]{1,0:T(8,128)(2,1)S(1)}, u32[]{:S(2)}, u32[]{:S(2)}) collective-permute-start(bf16[88,2048]{1,0:T(8,128)(2,1)S(1)} %collective-permute-done.17.refs_0_), channel_id=1, source_target_pairs={{0,16},{16,0},{1,17},{17,1},{2,18},{18,2},{3,19},{19,3},{4,20},{20... | collective-permute-start | bytes 1081352 | tf_op jit(solution)/shard_map/ppermute | solution.py:280
  56.9 19.1 %collective-permute-start = (bf16[88,2048]{1,0:T(8,128)(2,1)S(1)}, bf16[88,2048]{1,0:T(8,128)(2,1)S(1)}, u32[]{:S(2)}, u32[]{:S(2)}) collective-permute-start(bf16[88,2048]{1,0:T(8,128)(2,1)S(1)} %fusion.1.refs_0_), channel_id=1, source_target_pairs={{0,16},{16,0},{1,17},{17,1},{2,18},{18,2},{3,19},{19,3},{4,20},{20... | collective-permute-start | bytes 1081352 | tf_op jit(solution)/shard_map/ppermute | solution.py:280
  66.9 41.6 %collective-permute-start.6 = (s16[368,640]{1,0:T(8,128)(2,1)}, s16[368,640]{1,0:T(8,128)(2,1)}, u32[]{:S(2)}, u32[]{:S(2)}) collective-permute-start(s16[368,640]{1,0:T(8,128)(2,1)} %get-tuple-element.39), channel_id=1, source_target_pairs={{0,1},{1,0},{2,3},{3,2},{4,5},{5,4},{6,7},{7,6},{8,9},{9,8},{10,11... | collective-permute-start | bytes 1413128 | tf_op jit(solution)/shard_map/ppermute | solution.py:280
  66.9 44.6 %collective-permute-start.16 = (s16[368,640]{1,0:T(8,128)(2,1)}, s16[368,640]{1,0:T(8,128)(2,1)}, u32[]{:S(2)}, u32[]{:S(2)}) collective-permute-start(s16[368,640]{1,0:T(8,128)(2,1)} %get-tuple-element.43), channel_id=1, source_target_pairs={{0,1},{1,0},{2,3},{3,2},{4,5},{5,4},{6,7},{7,6},{8,9},{9,8},{10,11... | collective-permute-start | bytes 1413128 | tf_op jit(solution)/shard_map/ppermute | solution.py:280
  68.4 13.2 %collective-permute-start.25 = (bf16[40,2048]{1,0:T(8,128)(2,1)S(1)}, bf16[40,2048]{1,0:T(8,128)(2,1)S(1)}, u32[]{:S(2)}, u32[]{:S(2)}) collective-permute-start(bf16[40,2048]{1,0:T(8,128)(2,1)S(1)} %collective-permute-done.23.refs_1_), channel_id=1, source_target_pairs={{0,16},{16,0},{1,17},{17,1},{2,18},{18,2},{3,19},{19,3},{4,20},{20... | collective-permute-start | bytes 491528 | tf_op jit(solution)/shard_map/ppermute | solution.py:280
  69.8 13.2 %collective-permute-start.24 = (bf16[48,2048]{1,0:T(8,128)(2,1)S(1)}, bf16[48,2048]{1,0:T(8,128)(2,1)S(1)}, u32[]{:S(2)}, u32[]{:S(2)}) collective-permute-start(bf16[48,2048]{1,0:T(8,128)(2,1)S(1)} %collective-permute-done.22.refs_0_), channel_id=1, source_target_pairs={{0,16},{16,0},{1,17},{17,1},{2,18},{18,2},{3,19},{19,3},{4,20},{20... | collective-permute-start | bytes 589832 | tf_op jit(solution)/shard_map/ppermute | solution.py:280
  76.0 39.9 %collective-permute-start.21 = (s16[368,640]{1,0:T(8,128)(2,1)}, s16[368,640]{1,0:T(8,128)(2,1)}, u32[]{:S(2)}, u32[]{:S(2)}) collective-permute-start(s16[368,640]{1,0:T(8,128)(2,1)} %get-tuple-element.47), channel_id=1, source_target_pairs={{0,1},{1,0},{2,3},{3,2},{4,5},{5,4},{6,7},{7,6},{8,9},{9,8},{10,11... | collective-permute-start | bytes 1413128 | tf_op jit(solution)/shard_map/ppermute | solution.py:280
  81.6 22.6 %collective-permute-start.1 = (s16[192,640]{1,0:T(8,128)(2,1)}, s16[192,640]{1,0:T(8,128)(2,1)}, u32[]{:S(2)}, u32[]{:S(2)}) collective-permute-start(s16[192,640]{1,0:T(8,128)(2,1)} %get-tuple-element.35), channel_id=1, source_target_pairs={{0,1},{1,0},{2,3},{3,2},{4,5},{5,4},{6,7},{7,6},{8,9},{9,8},{10,11... | collective-permute-start | bytes 737288 | tf_op jit(solution)/shard_map/ppermute | solution.py:280
  88.5 26.2 %collective-permute-start.26 = (s16[192,640]{1,0:T(8,128)(2,1)}, s16[192,640]{1,0:T(8,128)(2,1)S(1)}, u32[]{:S(2)}, u32[]{:S(2)}) collective-permute-start(s16[192,640]{1,0:T(8,128)(2,1)} %get-tuple-element.51), channel_id=1, source_target_pairs={{0,1},{1,0},{2,3},{3,2},{4,5},{5,4},{6,7},{7,6},{8,9},{9,8},{10,11... | collective-permute-start | bytes 737288 | tf_op jit(solution)/shard_map/ppermute | solution.py:280
  137.4 25.3 %all-to-all-start.1 = ((f32[32,4,16,128]{3,2,1,0:T(8,128)}), f32[32,4,16,128]{3,2,1,0:T(8,128)S(1)}, u32[]{:S(2)}, u32[]{:S(2)}) async-start(f32[32,4,16,128]{3,2,1,0:T(8,128)} %broadcast_in_dim.17), calls=%async_computation.1 | async-start | bytes 2097152 | tf_op jit(solution)/shard_map/all_to_all | solution.py:269
  (45 other events, 344.4 us)

commit v3 on v2

v3 whole, which is shorter than its diff:
```python
import functools
import math

import jax
import jax.numpy as jnp
from jax import lax
from jax.experimental import pallas as pl
from jax.experimental.pallas import tpu as pltpu
from jax.sharding import Mesh, PartitionSpec as P

EPSILON = 1e-06
F32 = jnp.float32
BF16 = jnp.bfloat16
I16 = jnp.int16
LANES = 128
TOP_CODE = 32000.0
MIB = 1024 * 1024
CHUNKS = (
    ((0, 0, 0), (0, 0, 1)),
    ((1, 0, 0), (1, 0, 1), (2, 0, 0), (2, 0, 1)),
    ((0, 1, 0), (0, 1, 1), (3, 0, 0), (3, 0, 1)),
    ((1, 1, 0), (1, 1, 1), (2, 1, 0), (2, 1, 1)),
    ((3, 1, 0), (3, 1, 1)),
)
BLOCKS = tuple(block for chunk in CHUNKS for block in chunk)
FIRST = tuple(sum(len(chunk) for chunk in CHUNKS[:k]) for k in range(len(CHUNKS)))
VMEM_BYTES = 16 * MIB
ON_CHIP = pl.BlockSpec(memory_space=pltpu.VMEM)
SCALARS = pl.BlockSpec(memory_space=pltpu.SMEM)


def whole(shape):
    return pl.BlockSpec(shape, lambda *_: (0,) * len(shape))


def column(rows_of_lanes, size):
    filled = jnp.concatenate(
        [rows_of_lanes, jnp.zeros((8 - rows_of_lanes.shape[0], LANES), F32)], axis=0
    )
    return filled.T[:size]


def load_kernel(*refs, count):
    copies = [
        pltpu.make_async_copy(refs[i], refs[count + i], refs[2 * count].at[i]) for i in range(count)
    ]
    for copy in copies:
        copy.start()
    for copy in copies:
        copy.wait()


def load(*arrays):
    count = len(arrays)
    return pl.pallas_call(
        functools.partial(load_kernel, count=count),
        in_specs=[pl.BlockSpec(memory_space=pl.ANY)] * count,
        out_specs=[ON_CHIP] * count,
        out_shape=[pltpu.VMEM(a.shape, a.dtype) for a in arrays],
        scratch_shapes=[pltpu.SemaphoreType.DMA((count,))],
        compiler_params=pltpu.CompilerParams(vmem_limit_bytes=VMEM_BYTES),
        name="load",
    )(*arrays)


def front_kernel(*refs, pieces, rows):
    x_refs = refs[:pieces]
    gain_ref, dir_ref, weight_ref, slope_ref, log_ref, code_ref, tan_ref, rows_ref = refs[pieces:]
    x = jnp.concatenate([r[...].astype(F32) for r in x_refs], axis=0)
    rows_ref[...] = x.astype(BF16)
    hidden = (x * gain_ref[...]).astype(BF16)
    tangent = (x * dir_ref[...]).astype(BF16)
    weight = weight_ref[...]
    log = jnp.dot(hidden, weight, preferred_element_type=F32)
    log_ref[...] = log
    tan_ref[...] = jnp.dot(hidden, slope_ref[...], preferred_element_type=F32) + jnp.dot(
        tangent, weight, preferred_element_type=F32
    )
    most = jnp.max(jnp.abs(log), axis=0, keepdims=True)
    scale = jnp.ceil(jnp.log2(jnp.maximum(most, 1e-30)) * 256.0)
    coded = jnp.round(log * (TOP_CODE * jnp.exp2(scale * (-1.0 / 256.0))))
    code_ref[:rows, :] = coded.astype(jnp.int32).astype(I16)
    code_ref[rows:, :] = jnp.broadcast_to(scale, (16, scale.shape[1])).astype(jnp.int32).astype(I16)


def front(pieces, gain, slope_gain, weight, slope):
    rows = sum(p.shape[0] for p in pieces)
    width, cols = weight.shape
    return pl.pallas_call(
        functools.partial(front_kernel, pieces=len(pieces), rows=rows),
        in_specs=[ON_CHIP] * (len(pieces) + 4),
        out_specs=[ON_CHIP] * 4,
        out_shape=[
            pltpu.VMEM((rows, cols), F32),
            pltpu.VMEM((rows + 16, cols), I16),
            pltpu.VMEM((rows, cols), F32),
            pltpu.VMEM((rows, width), BF16),
        ],
        compiler_params=pltpu.CompilerParams(vmem_limit_bytes=VMEM_BYTES),
        cost_estimate=pl.CostEstimate(
            flops=6 * rows * width * cols, bytes_accessed=4 * rows * width, transcendentals=0
        ),
        name="front",
    )(*pieces, gain, slope_gain, weight, slope)


def expo_kernel(place_ref, log_ref, code_ref, tan_ref, ids_ref, e_ref, stats_ref, dense_ref, *, first, size, count):
    rows = size * count
    cols = log_ref.shape[1]
    scale = code_ref[rows:, :].astype(jnp.int32).astype(F32)[0:1]
    back = jnp.exp2(scale * (1.0 / 256.0)) * (1.0 / TOP_CODE)
    logits = log_ref[...] + code_ref[:rows, :].astype(jnp.int32).astype(F32) * back
    tan = tan_ref[...]
    top = jnp.max(logits, axis=1, keepdims=True)
    e = jnp.exp(logits - top)
    e_ref[...] = e
    total = jnp.sum(e, axis=1, keepdims=True)
    weighted = jnp.sum(e * tan, axis=1, keepdims=True)
    ids = jnp.concatenate(
        [column(ids_ref[pl.ds(place_ref[first + j], 1), :], size) for j in range(count)], axis=0
    )[:, 0:1]
    hit = lax.broadcasted_iota(jnp.int32, (rows, cols), 1).astype(F32) == ids
    picked = jnp.sum(jnp.where(hit, tan, 0.0), axis=1, keepdims=True)
    lane = lax.broadcasted_iota(jnp.int32, (rows, LANES), 1)
    stats = jnp.where(lane == 0, top, jnp.where(lane == 1, total, jnp.where(lane == 2, weighted, picked)))
    spare = jnp.zeros((-rows % LANES, LANES), F32)
    dense_ref[...] = jnp.concatenate([stats, spare], axis=0).T[:4, :rows]
    for j in range(count):
        block = jnp.concatenate(
            [stats[j * size : (j + 1) * size], jnp.zeros((LANES - size, LANES), F32)], axis=0
        ).T
        for i in range(4):
            stats_ref[i, j : j + 1, :] = block[i : i + 1, :]


def expo(place, log, code, tan, ids, first, size):
    rows, cols = log.shape
    count = rows // size
    return pl.pallas_call(
        functools.partial(expo_kernel, first=first, size=size, count=count),
        in_specs=[SCALARS] + [ON_CHIP] * 4,
        out_specs=[ON_CHIP] * 3,
        out_shape=[
            pltpu.VMEM(shape, F32) for shape in ((rows, cols), (4, count, LANES), (4, rows))
        ],
        compiler_params=pltpu.CompilerParams(vmem_limit_bytes=VMEM_BYTES),
        cost_estimate=pl.CostEstimate(
            flops=12 * rows * cols, bytes_accessed=2 * rows * cols, transcendentals=rows * cols
        ),
        name="expo",
    )(place, log, code, tan, ids)


def merge(parts):
    count = parts.shape[0]
    top = parts[0, 0:1]
    for s in range(1, count):
        top = jnp.maximum(top, parts[s, 0:1])
    total = jnp.zeros_like(top)
    weighted = jnp.zeros_like(top)
    picked = jnp.zeros_like(top)
    for s in range(count):
        factor = jnp.exp(parts[s, 0:1] - top)
        total += factor * parts[s, 1:2]
        weighted += factor * parts[s, 2:3]
        picked += parts[s, 3:4]
    return top, total, weighted, picked


def copies_kernel(*refs):
    joined = jnp.concatenate([r[...] for r in refs[:-1]], axis=1)
    for copy in range(refs[-1].shape[0]):
        refs[-1][copy] = joined


def first_merge_kernel(place_ref, parts_ref, out_ref, moved_ref, *, size):
    merged = jnp.concatenate(merge(parts_ref), axis=0)
    for b in range(len(BLOCKS)):
        moved_ref[place_ref[b], :, :size] = merged[:, b * size : (b + 1) * size]
    out_ref[...] = jnp.concatenate([moved_ref[b, :, :size] for b in range(len(BLOCKS))], axis=1)


def pair_merge_kernel(one_ref, other_ref, out_ref):
    merged = jnp.concatenate(merge(jnp.stack([one_ref[...], other_ref[...]])), axis=0)
    for copy in range(out_ref.shape[0]):
        out_ref[copy] = merged


def last_merge_kernel(parts_ref, out_ref, *, size, repeats):
    top, total, weighted, picked = merge(parts_ref)
    total = total * (1.0 / repeats)
    score = picked - weighted / total
    merged = jnp.concatenate([top, score, score / total, total], axis=0)
    for b in range(len(BLOCKS)):
        out_ref[b, :, :size] = merged[:, b * size : (b + 1) * size]


def small_kernel(kernel, name, shape, scratch, *args):
    return pl.pallas_call(
        kernel,
        in_specs=[SCALARS if a.dtype == jnp.int32 else ON_CHIP for a in args],
        out_specs=ON_CHIP,
        out_shape=pltpu.VMEM(shape, F32),
        scratch_shapes=[pltpu.VMEM(a, F32) for a in scratch],
        compiler_params=pltpu.CompilerParams(vmem_limit_bytes=VMEM_BYTES),
        name=name,
    )(*args)


def product_kernel(*refs, chunks, size, pairs):
    place_ref, ids_ref, merged_ref = refs[:3]
    e_refs = refs[3 : 3 + chunks]
    stats_refs = refs[3 + chunks : 3 + 2 * chunks]
    x_refs = refs[3 + 2 * chunks : 3 + 3 * chunks]
    weight_ref, gain_ref, out_ref, part_ref, cot_ref = refs[3 + 3 * chunks :]

    @pl.when(pl.program_id(0) == 0)
    def _():
        base = 0
        for chunk in range(chunks):
            count = e_refs[chunk].shape[0] // size
            for j in range(0, count, 2):
                both = []
                for i in (j, j + 1):
                    spot = place_ref[base + i]
                    found = merged_ref[spot]
                    score = found[1:2]
                    own = stats_refs[chunk][0, i : i + 1, :]
                    coef = jnp.exp(own - found[0:1]) * found[2:3]
                    cols = column(
                        jnp.concatenate([coef, score, ids_ref[pl.ds(spot, 1), :]], axis=0), size
                    )
                    e = e_refs[chunk][i * size : (i + 1) * size, :]
                    hit = lax.broadcasted_iota(jnp.int32, e.shape, 1).astype(F32) == cols[:, 2:3]
                    both.append(jnp.where(hit, cols[:, 1:2], 0.0) - cols[:, 0:1] * e)
                start = (base + j) * size
                cot_ref[start : start + 2 * size, :] = jnp.concatenate(both, axis=0).astype(BF16)
            base += count

    block = out_ref.shape[0]
    here = pl.ds(pl.multiple_of(pl.program_id(0) * block, block), block)
    x = jnp.concatenate([r[:, here] for r in x_refs], axis=0)
    product = lax.dot_general(x, cot_ref[...], (((0,), (0,)), ((), ())), preferred_element_type=F32)
    gain = jnp.broadcast_to(gain_ref[...], (8, gain_ref.shape[1])).T[:, 0:1]
    out_ref[...] = gain * product
    part = jnp.sum(weight_ref[here, :].astype(F32) * product, axis=1, keepdims=True)
    part_ref[...] = jnp.broadcast_to(part, (part.shape[0], LANES)).T[:1]


def finish(place, ids, merged, e, stats, x, weight, gain, size, block=512):
    width, cols = weight.shape
    rows = sum(a.shape[0] for a in x)
    chunks = len(x)
    return pl.pallas_call(
        functools.partial(product_kernel, chunks=chunks, size=size, pairs=rows // (2 * size)),
        grid=(width // block,),
        in_specs=[SCALARS]
        + [ON_CHIP] * (2 + 2 * chunks)
        + [ON_CHIP] * (chunks + 1)
        + [pl.BlockSpec((1, block), lambda i: (0, i))],
        out_specs=[
            pl.BlockSpec((block, cols), lambda i: (i, 0)),
            pl.BlockSpec((1, block), lambda i: (0, i)),
        ],
        out_shape=[
            jax.ShapeDtypeStruct((width, cols), F32),
            jax.ShapeDtypeStruct((1, width), F32),
        ],
        scratch_shapes=[pltpu.VMEM((rows, cols), BF16)],
        compiler_params=pltpu.CompilerParams(vmem_limit_bytes=VMEM_BYTES),
        cost_estimate=pl.CostEstimate(
            flops=2 * rows * width * cols,
            bytes_accessed=4 * width * cols,
            transcendentals=0,
        ),
        name="product",
    )(place, ids, merged, *e, *stats, *x, weight, gain)


def members(axes):
    return math.prod(lax.axis_size(axis) for axis in axes)


def everyone(x, axes):
    copies = jnp.broadcast_to(x[None], (members(axes),) + x.shape)
    return lax.all_to_all(copies, axes, 0, 0, tiled=True)


def along_x(x, by):
    count = lax.axis_size("x")
    pairs = [
        (2 * i + core, 2 * ((i + (by, -by)[core]) % count) + core) for i in range(count) for core in (0, 1)
    ]
    return lax.ppermute(x, ("x", "c"), pairs)


def along_y(x):
    def at(y, core):
        return (y // 2 * 2 + core) * 2 + y % 2

    count = lax.axis_size("yh") * lax.axis_size("t")
    pairs = [
        (at(y, core), at((y + (1, -1)[core]) % count, core)) for y in range(count) for core in (0, 1)
    ]
    return lax.ppermute(x, ("yh", "c", "t"), pairs)


def swap(x, axis):
    return lax.ppermute(x, (axis,), [(0, 1), (1, 0)])


def together(*values):
    return lax.optimization_barrier(values)


def local(residual, norm_gain, gain_dir, head_weight, head_dir, sampled):
    size, width = residual.shape
    vocab_dev = head_weight.shape[1]
    x_at, y_at, c_at, z_at = (lax.axis_index(a) for a in ("x", "yh", "c", "z"))
    around = lax.axis_size("x")
    place = []
    for way, h, g in BLOCKS:
        back = 1 - 2 * (c_at ^ g)
        x_of = x_at + (0, -back, back, 2)[way]
        place.append((((x_of + around) % around) * 2 + (y_at ^ h)) * 2 + (c_at ^ g))
    place = jnp.stack(place).astype(jnp.int32)
    offset = (((x_at * 2 + y_at) * 2 + c_at) * lax.axis_size("z") + z_at) * vocab_dev
    ids = jnp.pad(
        (sampled - offset).astype(F32).reshape(len(BLOCKS), size), ((0, 0), (0, LANES - size))
    )
    gain_row, dir_row = norm_gain[None], gain_dir[None]

    place, ids, residual, gain_row, dir_row = together(place, ids, residual, gain_row, dir_row)
    entries = residual.astype(F32)
    squares = lax.psum(jnp.sum(entries * entries, axis=1), "t")
    normed = (entries * lax.rsqrt(squares / (2 * width) + EPSILON)[:, None]).astype(BF16)

    weight, slope = load(head_weight, head_dir)

    def chunk_front(*pieces):
        return front(pieces, gain_row, dir_row, weight, slope)

    def chunk_expo(k, made, code):
        return expo(place, made[0], code, made[2], ids, FIRST[k], size)

    across = along_y(normed)
    one, two = along_x(normed, 1), along_x(normed, -1)
    own2 = swap(normed, "c")
    across, one, two, own2, weight, slope = together(across, one, two, own2, weight, slope)

    across = along_y(across)
    far = along_x(one, 1)
    one2, two2 = swap(one, "c"), swap(two, "c")
    made0 = chunk_front(normed, own2)
    code0 = swap(made0[1], "t")
    across, far, one, two, one2, two2, made0 = together(across, far, one, two, one2, two2, made0)

    y_one, y_two = along_x(across, 1), along_x(across, -1)
    across2, far2 = swap(across, "c"), swap(far, "c")
    made1 = chunk_front(one, one2, two, two2)
    code1 = swap(made1[1], "t")
    y_one, y_two, across, across2, far, far2, made1, code0 = together(
        y_one, y_two, across, across2, far, far2, made1, code0
    )

    y_far = along_x(y_one, 1)
    y_one2, y_two2 = swap(y_one, "c"), swap(y_two, "c")
    expo0 = chunk_expo(0, made0, code0)
    made2 = chunk_front(across, across2, far, far2)
    code2 = swap(made2[1], "t")
    y_far, y_one, y_two, y_one2, y_two2, made2, expo0, code1 = together(
        y_far, y_one, y_two, y_one2, y_two2, made2, expo0, code1
    )

    y_far2 = swap(y_far, "c")
    made3 = chunk_front(y_one, y_one2, y_two, y_two2)
    code3 = swap(made3[1], "t")
    y_far, y_far2, made3 = together(y_far, y_far2, made3)

    made4 = chunk_front(y_far, y_far2)
    code4 = swap(made4[1], "t")
    expo1 = chunk_expo(1, made1, code1)
    made4, expo1, code2 = together(made4, expo1, code2)

    expo2 = chunk_expo(2, made2, code2)
    expo2, code3 = together(expo2, code3)
    expo3 = chunk_expo(3, made3, code3)
    expo3, code4 = together(expo3, code4)
    expo4 = chunk_expo(4, made4, code4)
    xs = [m[3] for m in (made0, made1, made2, made3, made4)]
    es, stats, dense = zip(expo0, expo1, expo2, expo3, expo4)
    tokens = size * len(BLOCKS)
    own = small_kernel(copies_kernel, "copies", (lax.axis_size("z"), 4, tokens), [], *dense)
    rest = ("x", "yh", "t")
    spread = (len(BLOCKS), 4, LANES)
    along_z = small_kernel(
        functools.partial(first_merge_kernel, size=size),
        "first_merge",
        own.shape[1:],
        [spread],
        place,
        lax.all_to_all(own, "z", 0, 0, tiled=True),
    )
    on_chip = small_kernel(
        pair_merge_kernel, "pair_merge", (members(rest),) + own.shape[1:], [], along_z, swap(along_z, "c")
    )
    merged = small_kernel(
        functools.partial(last_merge_kernel, size=size, repeats=2.0),
        "last_merge",
        spread,
        [],
        lax.all_to_all(on_chip, rest, 0, 0, tiled=True),
    )
    fisher_head, part = finish(place, ids, merged, es, stats, xs, weight, gain_row, size)
    part = jnp.sum(everyone(part, ("x", "yh", "c")), axis=0)
    fisher_gain = jnp.sum(everyone(part, ("z",)), axis=(0, 1))
    return (fisher_head, fisher_gain)


def solution(mesh):
    fine = Mesh(mesh.devices.reshape(4, 2, 2, 8, 2), ("x", "yh", "c", "z", "t"))
    dp, vocab = ("x", "yh", "c"), ("x", "yh", "c", "z")
    in_specs = (P(dp, "t"), P("t"), P("t"), P("t", vocab), P("t", vocab), P())
    out_specs = (P("t", vocab), P("t"))
    return jax.shard_map(local, mesh=fine, in_specs=in_specs, out_specs=out_specs, check_vma=False)
```

time: 201 us -> 150 us (0.75)
  local copies, waits for them, and re-layouts: 27.6 us -> 3.77 us
  waiting for transfers between devices: 45.6 us -> 24.2 us
  blocking collectives: 41.9 us -> 55.5 us
  starting transfers between devices: 40.2 us -> 29.6 us
  Pallas kernels: 40.4 us -> 31.6 us
    all_to_all x0 -> x2, blocking collectives: none -> 28.8 us  [the longest x1 16.3 us: local(): lax.all_to_all(own, 'z', 0, 0, tiled=True)]
    unnamed x83 -> x8, local copies, waits for them, and re-layouts: 24.6 us -> 3.49 us
    all_to_all x1 -> x0, waiting for transfers between devices: 16 us -> none  [everyone(): return lax.all_to_all(copies, axes, 0, 0, tiled=True)]
    all_to_all x3 -> x2, blocking collectives: 37.5 us -> 22.2 us  [everyone(): return lax.all_to_all(copies, axes, 0, 0, tiled=True)]
    all_to_all x1 -> x0, starting transfers between devices: 7.9 us -> none  [everyone(): return lax.all_to_all(copies, axes, 0, 0, tiled=True)]
    ppermute x12 -> x8, waiting for transfers between devices: 14.1 us -> 7.66 us  [the longest x6 7.66 us: along_x(): return lax.ppermute(x, ('x', 'c'), pairs)]
    pallas_call x7 -> x10, Pallas kernels: 22.4 us -> 16.6 us  [the longest x5 15.2 us: front(): pl.pallas_call(functools.partial(front_kernel, pieces=len(pieces), rows=r...]
    ppermute x12 -> x8, starting transfers between devices: 17.4 us -> 14.1 us  [the longest x6 11.1 us: along_x(): return lax.ppermute(x, ('x', 'c'), pairs)]
  transfers between devices with their start and end apart: 28 -> 22, of which waited for: 5 -> 8; matrix products, arithmetic and copies ran while one was open for 1% -> 0% of each run, Pallas kernels for 14% -> 14%
where the time goes in v3:
time: 150 us; the launch traced here: 149 us
  blocking collectives  55.5 us (37%)
  Pallas kernels  31.6 us (21%)
  starting transfers between devices  29.6 us (20%)
  waiting for transfers between devices  24.2 us (16%)
  local copies, waits for them, and re-layouts  3.77 us (3%)
  other arithmetic  3.75 us (2%)
    all_to_all x2, blocking collectives, everyone(): return lax.all_to_all(copies, axes, 0, 0, tiled=True)  22.2 us
    ppermute x14, waiting for transfers between devices, swap(): return lax.ppermute(x, (axis,), [(0, 1), (1, 0)])  16.5 us
    all_to_all x1, blocking collectives, local(): lax.all_to_all(own, 'z', 0, 0, tiled=True)  16.3 us
    ppermute x14, starting transfers between devices, swap(): return lax.ppermute(x, (axis,), [(0, 1), (1, 0)])  15.5 us
    pallas_call x5, Pallas kernels, front(): pl.pallas_call(functools.partial(front_kernel, pieces=len(pieces), rows=r...  15.2 us
    all_to_all x1, blocking collectives, local(): lax.all_to_all(on_chip, rest, 0, 0, tiled=True)  12.5 us
    ppermute x6, starting transfers between devices, along_x(): return lax.ppermute(x, ('x', 'c'), pairs)  11.1 us
    pallas_call x1, Pallas kernels, finish(): pl.pallas_call(functools.partial(product_kernel, chunks=chunks, size=size...  9.18 us
  transfers between devices with their start and end apart: 22, of which 8 were waited for; matrix products, arithmetic and copies ran while one was open for 0% of the time, Pallas kernels for 14%

profile of v3, /device:TPU:1, one launch (start us, length us, event | category | flops | bytes accessed | tf_op | source)
XLA Modules:
  0.0 149.3 jit_solution(7246267989102853696)
XLA Ops:
  2.8 4.4 %psum.7 = f32[88]{0:T(128)S(1)} all-reduce(f32[88]{0:T(128)S(1)} %fusion), channel_id=1, replica_groups=mesh['x'=4,'yh'=2,'c'=2,'z'=8,'t'=2] {'t'}, use_global_device_ids=true, to_apply=%region_1.2 | all-reduce | flops 88 | bytes 704 | tf_op jit(solution)/shard_map/psum | solution.py:335
  8.4 3.8 %collective-permute-start.3 = (bf16[88,2048]{1,0:T(8,128)(2,1)S(1)}, bf16[88,2048]{1,0:T(8,128)(2,1)S(1)}, u32[]{:S(2)}, u32[]{:S(2)}) collective-permute-start(bf16[88,2048]{1,0:T(8,128)(2,1)S(1)} %fusion.1.refs_0_), channel_id=1, source_target_pairs={{0,16},{16,0},{1,17},{17,1},{2,18},{18,2},{3,19},{19,3},{4,20},{20... | collective-permute-start | bytes 1081352 | tf_op jit(solution)/shard_map/ppermute | solution.py:309
  12.2 2.7 %collective-permute-start.1 = (bf16[88,2048]{1,0:T(8,128)(2,1)S(1)}, bf16[88,2048]{1,0:T(8,128)(2,1)S(1)}, u32[]{:S(2)}, u32[]{:S(2)}) collective-permute-start(bf16[88,2048]{1,0:T(8,128)(2,1)S(1)} %fusion.1.refs_0_), channel_id=1, source_target_pairs={{0,64},{16,208},{64,128},{80,16},{128,192},{144,80},{192,0},{208,1... | collective-permute-start | bytes 1081352 | tf_op jit(solution)/shard_map/ppermute | solution.py:294
  19.8 2.5 %collective-permute-done.2.refs_2_ = bf16[88,2048]{1,0:T(8,128)(2,1)S(1)} collective-permute-done((bf16[88,2048]{1,0:T(8,128)(2,1)S(1)}, bf16[88,2048]{1,0:T(8,128)(2,1)S(1)}, u32[]{:S(2)}, u32[]{:S(2)}) %collective-permute-start.2) | collective-permute-done | bytes 360480 | tf_op jit(solution)/shard_map/ppermute | solution.py:294
  22.3 2.0 %collective-permute-start.4 = (bf16[88,2048]{1,0:T(8,128)(2,1)S(1)}, bf16[88,2048]{1,0:T(8,128)(2,1)S(1)}, u32[]{:S(2)}, u32[]{:S(2)}) collective-permute-start(bf16[88,2048]{1,0:T(8,128)(2,1)S(1)} %collective-permute-done), channel_id=1, source_target_pairs={{0,1},{16,49},{1,32},{17,16},{32,33},{48,17},{33,0},{49,48},{2,3},... | collective-permute-start | bytes 1081352 | tf_op jit(solution)/shard_map/ppermute | solution.py:305
  24.7 3.1 %collective-permute-start.5 = (bf16[88,2048]{1,0:T(8,128)(2,1)S(1)}, bf16[88,2048]{1,0:T(8,128)(2,1)S(1)}, u32[]{:S(2)}, u32[]{:S(2)}) collective-permute-start(bf16[88,2048]{1,0:T(8,128)(2,1)S(1)} %collective-permute-done.1.refs_0_), channel_id=1, source_target_pairs={{0,64},{16,208},{64,128},{80,16},{128,192},{144,80},{192,0},{208,1... | collective-permute-start | bytes 1081352 | tf_op jit(solution)/shard_map/ppermute | solution.py:294
  27.8 2.0 %front.5 = (f32[176,640]{1,0:T(8,128)S(1)}, s16[192,640]{1,0:T(8,128)(2,1)S(1)}, f32[176,640]{1,0:T(8,128)S(1)}, bf16[176,2048]{1,0:T(8,128)(2,1)S(1)}) custom-call(bf16[88,2048]{1,0:T(8,128)(2,1)S(1)} %fusion.1.refs_0_, bf16[88,2048]{1,0:T(8,128)(2,1)S(1)} %collective-permute-done.3.refs_1_, f32[1,2048]{1,0:T(1,128)S(1)} %bitcast.24, ...), custom_call_target="tpu_custom_call" | custom-call | flops 1384120320 | bytes 1441792 | tf_op jit(solution)/shard_map/front/pallas_call | solution.py:89
  30.2 2.0 %collective-permute-done.5.refs_2_ = bf16[88,2048]{1,0:T(8,128)(2,1)S(1)} collective-permute-done((bf16[88,2048]{1,0:T(8,128)(2,1)S(1)}, bf16[88,2048]{1,0:T(8,128)(2,1)S(1)}, u32[]{:S(2)}, u32[]{:S(2)}) %collective-permute-start.5) | collective-permute-done | bytes 360480 | tf_op jit(solution)/shard_map/ppermute | solution.py:294
  33.5 2.7 %collective-permute-start.8 = (bf16[88,2048]{1,0:T(8,128)(2,1)S(1)}, bf16[88,2048]{1,0:T(8,128)(2,1)S(1)}, u32[]{:S(2)}, u32[]{:S(2)}) collective-permute-start(bf16[88,2048]{1,0:T(8,128)(2,1)S(1)} %collective-permute-done.4.refs_0_), channel_id=1, source_target_pairs={{0,64},{16,208},{64,128},{80,16},{128,192},{144,80},{192,0},{208,1... | collective-permute-start | bytes 1081352 | tf_op jit(solution)/shard_map/ppermute | solution.py:294
  36.2 3.7 %front.6 = (f32[352,640]{1,0:T(8,128)S(1)}, s16[368,640]{1,0:T(8,128)(2,1)S(1)}, f32[352,640]{1,0:T(8,128)S(1)}, bf16[352,2048]{1,0:T(8,128)(2,1)S(1)}) custom-call(bf16[88,2048]{1,0:T(8,128)(2,1)S(1)} %collective-permute-done.1.refs_0_, bf16[88,2048]{1,0:T(8,128)(2,1)S(1)} %collective-permute-done.6.refs_1_, ...), custom_call_target="tpu_custom_call" | custom-call | flops 2768240640 | bytes 2883584 | tf_op jit(solution)/shard_map/front/pallas_call | solution.py:89
  42.0 2.3 %collective-permute-done.8.refs_0_ = bf16[88,2048]{1,0:T(8,128)(2,1)S(1)} collective-permute-done((bf16[88,2048]{1,0:T(8,128)(2,1)S(1)}, bf16[88,2048]{1,0:T(8,128)(2,1)S(1)}, u32[]{:S(2)}, u32[]{:S(2)}) %collective-permute-start.8) | collective-permute-done | bytes 360480 | tf_op jit(solution)/shard_map/ppermute | solution.py:294
  45.6 2.7 %collective-permute-start.13 = (bf16[88,2048]{1,0:T(8,128)(2,1)S(1)}, bf16[88,2048]{1,0:T(8,128)(2,1)S(1)}, u32[]{:S(2)}, u32[]{:S(2)}) collective-permute-start(bf16[88,2048]{1,0:T(8,128)(2,1)S(1)} %collective-permute-done.8.refs_0_), channel_id=1, source_target_pairs={{0,64},{16,208},{64,128},{80,16},{128,192},{144,80},{192,0},{208,1... | collective-permute-start | bytes 1081352 | tf_op jit(solution)/shard_map/ppermute | solution.py:294
  49.3 3.7 %front.7 = (f32[352,640]{1,0:T(8,128)S(1)}, s16[368,640]{1,0:T(8,128)(2,1)S(1)}, f32[352,640]{1,0:T(8,128)S(1)}, bf16[352,2048]{1,0:T(8,128)(2,1)S(1)}) custom-call(bf16[88,2048]{1,0:T(8,128)(2,1)S(1)} %collective-permute-done.4.refs_0_, bf16[88,2048]{1,0:T(8,128)(2,1)S(1)} %collective-permute-done.10.refs_1_, ...), custom_call_target="tpu_custom_call" | custom-call | flops 2768240640 | bytes 2883584 | tf_op jit(solution)/shard_map/front/pallas_call | solution.py:89
  55.8 3.7 %front.8 = (f32[352,640]{1,0:T(8,128)S(1)}, s16[368,640]{1,0:T(8,128)(2,1)S(1)}, f32[352,640]{1,0:T(8,128)S(1)}, bf16[352,2048]{1,0:T(8,128)(2,1)S(1)}) custom-call(bf16[88,2048]{1,0:T(8,128)(2,1)S(1)} %collective-permute-done.8.refs_0_, bf16[88,2048]{1,0:T(8,128)(2,1)S(1)} %collective-permute-done.14.refs_1_, ...), custom_call_target="tpu_custom_call" | custom-call | flops 2768240640 | bytes 2883584 | tf_op jit(solution)/shard_map/front/pallas_call | solution.py:89
  60.0 2.0 %front.9 = (f32[176,640]{1,0:T(8,128)S(1)}, s16[192,640]{1,0:T(8,128)(2,1)S(1)}, f32[176,640]{1,0:T(8,128)S(1)}, bf16[176,2048]{1,0:T(8,128)(2,1)S(1)}) custom-call(bf16[88,2048]{1,0:T(8,128)(2,1)S(1)} %collective-permute-done.13.refs_0_, bf16[88,2048]{1,0:T(8,128)(2,1)S(1)} %collective-permute-done.17.refs_1_, f32[1,2048]{1,0:T(1,128)S(1)} %bitcast.28, ...), custom_call_target="tpu_custom_call" | custom-call | flops 1384120320 | bytes 1441792 | tf_op jit(solution)/shard_map/front/pallas_call | solution.py:89
  64.4 2.7 %collective-permute-done.18.code_ref = s16[368,640]{1,0:T(8,128)(2,1)S(1)} collective-permute-done((s16[368,640]{1,0:T(8,128)(2,1)S(1)}, s16[368,640]{1,0:T(8,128)(2,1)S(1)}, u32[]{:S(2)}, u32[]{:S(2)}) %collective-permute-start.18) | collective-permute-done | bytes 471072 | tf_op jit(solution)/shard_map/ppermute | solution.py:309
  68.3 8.9 %collective-permute-done.19.code_ref = s16[368,640]{1,0:T(8,128)(2,1)S(1)} collective-permute-done((s16[368,640]{1,0:T(8,128)(2,1)S(1)}, s16[368,640]{1,0:T(8,128)(2,1)S(1)}, u32[]{:S(2)}, u32[]{:S(2)}) %collective-permute-start.19) | collective-permute-done | bytes 471072 | tf_op jit(solution)/shard_map/ppermute | solution.py:309
  78.4 4.0 %collective-permute-done.20.code_ref = s16[192,640]{1,0:T(8,128)(2,1)S(1)} collective-permute-done((s16[192,640]{1,0:T(8,128)(2,1)S(1)}, s16[192,640]{1,0:T(8,128)(2,1)S(1)}, u32[]{:S(2)}, u32[]{:S(2)}) %collective-permute-start.20) | collective-permute-done | bytes 245792 | tf_op jit(solution)/shard_map/ppermute | solution.py:309
  83.6 16.3 %all_to_all.20.parts_ref = f32[8,4,1408]{2,1,0:T(4,128)S(1)} all-to-all(f32[8,4,1408]{2,1,0:T(4,128)S(1)} %copies.1), channel_id=1, replica_groups=mesh['x'=4,'yh'=2,'c'=2,'z'=8,'t'=2] {'z'}, dimensions={0} | all-to-all | bytes 360448 | tf_op jit(solution)/shard_map/all_to_all | solution.py:402
  100.7 2.8 %collective-permute-start.21 = (f32[4,1408]{1,0:T(4,128)S(1)}, f32[4,1408]{1,0:T(4,128)S(1)}, u32[]{:S(2)}, u32[]{:S(2)}) collective-permute-start(f32[4,1408]{1,0:T(4,128)S(1)} %first_merge.1.one_ref), channel_id=1, source_target_pairs={{0,16},{16,0},{1,17},{17,1},{2,18},{18,2},{3,19},{19,3},{4,20},{20... | collective-permute-start | bytes 67592 | tf_op jit(solution)/shard_map/ppermute | solution.py:309
  104.4 12.5 %all_to_all.21.parts_ref = f32[16,4,1408]{2,1,0:T(4,128)S(1)} all-to-all(f32[16,4,1408]{2,1,0:T(4,128)S(1)} %pair_merge.1), channel_id=1, replica_groups=mesh['x'=4,'yh'=2,'c'=2,'z'=8,'t'=2] {'x','yh','t'}, dimensions={0} | all-to-all | bytes 720896 | tf_op jit(solution)/shard_map/all_to_all | solution.py:412
  117.1 9.2 %product.1 = (f32[2048,640]{1,0:T(8,128)}, f32[1,2048]{1,0:T(1,128)S(1)}) custom-call(s32[16]{0:T(128)S(1)} %stack.67.place_ref.refs_0_, f32[16,128]{1,0:T(8,128)S(1)} %pad.4.ids_ref.refs_1_, f32[16,4,128]{2,1,0:T(4,128)S(1)} %last_merge.1.refs_2_, f32[176,640]{1,0:T(8,128)S(1)} %get-tuple-element.187.refs_3_, f32[352,640]{1,0:T(8,128)S(1)} %get-tuple-element.188.refs_4_, ...), custom_call_target="tpu_custom_call" | custom-call | flops 3690987520 | bytes 5242880 | tf_op jit(solution)/shard_map/product/pallas_call | solution.py:254
  126.3 12.7 %all_to_all.22 = f32[16,1,2048]{2,1,0:T(1,128)S(1)} all-to-all(f32[16,1,2048]{2,1,0:T(1,128)S(1)} %broadcast_in_dim.24), channel_id=1, replica_groups=mesh['x'=4,'yh'=2,'c'=2,'z'=8,'t'=2] {'x','yh','c'}, dimensions={0} | all-to-all | bytes 262144 | tf_op jit(solution)/shard_map/all_to_all | solution.py:286
  139.1 9.5 %all_to_all.23 = f32[8,1,2048]{2,1,0:T(1,128)S(1)} all-to-all(f32[8,1,2048]{2,1,0:T(1,128)S(1)} %broadcast_in_dim.25), channel_id=1, replica_groups=mesh['x'=4,'yh'=2,'c'=2,'z'=8,'t'=2] {'z'}, dimensions={0} | all-to-all | bytes 131072 | tf_op jit(solution)/shard_map/all_to_all | solution.py:286
  (60 shorter events, 26.5 us)
Async XLA Ops:
  7.3 20.6 %copy-start.2 = (f32[2048]{0:T(1024)S(1)}, f32[2048]{0:T(1024)}, u32[]{:S(2)}) copy-start(f32[2048]{0:T(1024)} %param.8) | copy-start | bytes 24580
  7.3 20.6 %copy-start.3 = (f32[2048]{0:T(1024)S(1)}, f32[2048]{0:T(1024)}, u32[]{:S(2)}) copy-start(f32[2048]{0:T(1024)} %param.7) | copy-start | bytes 24580
  8.4 11.4 %collective-permute-start.3 = (bf16[88,2048]{1,0:T(8,128)(2,1)S(1)}, bf16[88,2048]{1,0:T(8,128)(2,1)S(1)}, u32[]{:S(2)}, u32[]{:S(2)}) collective-permute-start(bf16[88,2048]{1,0:T(8,128)(2,1)S(1)} %fusion.1.refs_0_), channel_id=1, source_target_pairs={{0,16},{16,0},{1,17},{17,1},{2,18},{18,2},{3,19},{19,3},{4,20},{20... | collective-permute-start | bytes 1081352 | tf_op jit(solution)/shard_map/ppermute | solution.py:309
  12.2 10.0 %collective-permute-start.2 = (bf16[88,2048]{1,0:T(8,128)(2,1)S(1)}, bf16[88,2048]{1,0:T(8,128)(2,1)S(1)}, u32[]{:S(2)}, u32[]{:S(2)}) collective-permute-start(bf16[88,2048]{1,0:T(8,128)(2,1)S(1)} %fusion.1.refs_0_), channel_id=1, source_target_pairs={{0,192},{16,80},{64,0},{80,144},{128,64},{144,208},{192,128},{208,... | collective-permute-start | bytes 1081352 | tf_op jit(solution)/shard_map/ppermute | solution.py:294
  12.2 10.0 %collective-permute-start.1 = (bf16[88,2048]{1,0:T(8,128)(2,1)S(1)}, bf16[88,2048]{1,0:T(8,128)(2,1)S(1)}, u32[]{:S(2)}, u32[]{:S(2)}) collective-permute-start(bf16[88,2048]{1,0:T(8,128)(2,1)S(1)} %fusion.1.refs_0_), channel_id=1, source_target_pairs={{0,64},{16,208},{64,128},{80,16},{128,192},{144,80},{192,0},{208,1... | collective-permute-start | bytes 1081352 | tf_op jit(solution)/shard_map/ppermute | solution.py:294
  14.9 7.3 %collective-permute-start = (bf16[88,2048]{1,0:T(8,128)(2,1)S(1)}, bf16[88,2048]{1,0:T(8,128)(2,1)S(1)}, u32[]{:S(2)}, u32[]{:S(2)}) collective-permute-start(bf16[88,2048]{1,0:T(8,128)(2,1)S(1)} %fusion.1.refs_0_), channel_id=1, source_target_pairs={{0,1},{16,49},{1,32},{17,16},{32,33},{48,17},{33,0},{49,48},{2,3},... | collective-permute-start | bytes 1081352 | tf_op jit(solution)/shard_map/ppermute | solution.py:305
  22.3 8.0 %collective-permute-start.4 = (bf16[88,2048]{1,0:T(8,128)(2,1)S(1)}, bf16[88,2048]{1,0:T(8,128)(2,1)S(1)}, u32[]{:S(2)}, u32[]{:S(2)}) collective-permute-start(bf16[88,2048]{1,0:T(8,128)(2,1)S(1)} %collective-permute-done), channel_id=1, source_target_pairs={{0,1},{16,49},{1,32},{17,16},{32,33},{48,17},{33,0},{49,48},{2,3},... | collective-permute-start | bytes 1081352 | tf_op jit(solution)/shard_map/ppermute | solution.py:305
  24.2 6.0 %collective-permute-start.7 = (bf16[88,2048]{1,0:T(8,128)(2,1)S(1)}, bf16[88,2048]{1,0:T(8,128)(2,1)S(1)}, u32[]{:S(2)}, u32[]{:S(2)}) collective-permute-start(bf16[88,2048]{1,0:T(8,128)(2,1)S(1)} %collective-permute-done.2.refs_2_), channel_id=1, source_target_pairs={{0,16},{16,0},{1,17},{17,1},{2,18},{18,2},{3,19},{19,3},{4,20},{20... | collective-permute-start | bytes 1081352 | tf_op jit(solution)/shard_map/ppermute | solution.py:309
  24.3 5.9 %collective-permute-start.6 = (bf16[88,2048]{1,0:T(8,128)(2,1)S(1)}, bf16[88,2048]{1,0:T(8,128)(2,1)S(1)}, u32[]{:S(2)}, u32[]{:S(2)}) collective-permute-start(bf16[88,2048]{1,0:T(8,128)(2,1)S(1)} %collective-permute-done.1.refs_0_), channel_id=1, source_target_pairs={{0,16},{16,0},{1,17},{17,1},{2,18},{18,2},{3,19},{19,3},{4,20},{20... | collective-permute-start | bytes 1081352 | tf_op jit(solution)/shard_map/ppermute | solution.py:309
  24.7 7.4 %collective-permute-start.5 = (bf16[88,2048]{1,0:T(8,128)(2,1)S(1)}, bf16[88,2048]{1,0:T(8,128)(2,1)S(1)}, u32[]{:S(2)}, u32[]{:S(2)}) collective-permute-start(bf16[88,2048]{1,0:T(8,128)(2,1)S(1)} %collective-permute-done.1.refs_0_), channel_id=1, source_target_pairs={{0,64},{16,208},{64,128},{80,16},{128,192},{144,80},{192,0},{208,1... | collective-permute-start | bytes 1081352 | tf_op jit(solution)/shard_map/ppermute | solution.py:294
  29.8 10.1 %collective-permute-start.12 = (s16[192,640]{1,0:T(8,128)(2,1)S(1)}, s16[192,640]{1,0:T(8,128)(2,1)S(1)}, u32[]{:S(2)}, u32[]{:S(2)}) collective-permute-start(s16[192,640]{1,0:T(8,128)(2,1)S(1)} %get-tuple-element.117), channel_id=1, source_target_pairs={{0,1},{1,0},{2,3},{3,2},{4,5},{5,4},{6,7},{7,6},{8,9},{9,8},{10,11... | collective-permute-start | bytes 737288 | tf_op jit(solution)/shard_map/ppermute | solution.py:309
  32.2 8.9 %collective-permute-start.10 = (bf16[88,2048]{1,0:T(8,128)(2,1)S(1)}, bf16[88,2048]{1,0:T(8,128)(2,1)S(1)}, u32[]{:S(2)}, u32[]{:S(2)}) collective-permute-start(bf16[88,2048]{1,0:T(8,128)(2,1)S(1)} %collective-permute-done.4.refs_0_), channel_id=1, source_target_pairs={{0,16},{16,0},{1,17},{17,1},{2,18},{18,2},{3,19},{19,3},{4,20},{20... | collective-permute-start | bytes 1081352 | tf_op jit(solution)/shard_map/ppermute | solution.py:309
  33.5 8.5 %collective-permute-start.9 = (bf16[88,2048]{1,0:T(8,128)(2,1)S(1)}, bf16[88,2048]{1,0:T(8,128)(2,1)S(1)}, u32[]{:S(2)}, u32[]{:S(2)}) collective-permute-start(bf16[88,2048]{1,0:T(8,128)(2,1)S(1)} %collective-permute-done.4.refs_0_), channel_id=1, source_target_pairs={{0,192},{16,80},{64,0},{80,144},{128,64},{144,208},{192,128},{208,... | collective-permute-start | bytes 1081352 | tf_op jit(solution)/shard_map/ppermute | solution.py:294
  33.5 10.8 %collective-permute-start.8 = (bf16[88,2048]{1,0:T(8,128)(2,1)S(1)}, bf16[88,2048]{1,0:T(8,128)(2,1)S(1)}, u32[]{:S(2)}, u32[]{:S(2)}) collective-permute-start(bf16[88,2048]{1,0:T(8,128)(2,1)S(1)} %collective-permute-done.4.refs_0_), channel_id=1, source_target_pairs={{0,64},{16,208},{64,128},{80,16},{128,192},{144,80},{192,0},{208,1... | collective-permute-start | bytes 1081352 | tf_op jit(solution)/shard_map/ppermute | solution.py:294
  36.2 4.9 %collective-permute-start.11 = (bf16[88,2048]{1,0:T(8,128)(2,1)S(1)}, bf16[88,2048]{1,0:T(8,128)(2,1)S(1)}, u32[]{:S(2)}, u32[]{:S(2)}) collective-permute-start(bf16[88,2048]{1,0:T(8,128)(2,1)S(1)} %collective-permute-done.5.refs_2_), channel_id=1, source_target_pairs={{0,16},{16,0},{1,17},{17,1},{2,18},{18,2},{3,19},{19,3},{4,20},{20... | collective-permute-start | bytes 1081352 | tf_op jit(solution)/shard_map/ppermute | solution.py:309
  39.9 13.1 %collective-permute-start.16 = (s16[368,640]{1,0:T(8,128)(2,1)S(1)}, s16[368,640]{1,0:T(8,128)(2,1)S(1)}, u32[]{:S(2)}, u32[]{:S(2)}) collective-permute-start(s16[368,640]{1,0:T(8,128)(2,1)S(1)} %get-tuple-element.127), channel_id=1, source_target_pairs={{0,1},{1,0},{2,3},{3,2},{4,5},{5,4},{6,7},{7,6},{8,9},{9,8},{10,11... | collective-permute-start | bytes 1413128 | tf_op jit(solution)/shard_map/ppermute | solution.py:309
  44.3 8.7 %collective-permute-start.15 = (bf16[88,2048]{1,0:T(8,128)(2,1)S(1)}, bf16[88,2048]{1,0:T(8,128)(2,1)S(1)}, u32[]{:S(2)}, u32[]{:S(2)}) collective-permute-start(bf16[88,2048]{1,0:T(8,128)(2,1)S(1)} %collective-permute-done.9.refs_2_), channel_id=1, source_target_pairs={{0,16},{16,0},{1,17},{17,1},{2,18},{18,2},{3,19},{19,3},{4,20},{20... | collective-permute-start | bytes 1081352 | tf_op jit(solution)/shard_map/ppermute | solution.py:309
  45.5 7.5 %collective-permute-start.14 = (bf16[88,2048]{1,0:T(8,128)(2,1)S(1)}, bf16[88,2048]{1,0:T(8,128)(2,1)S(1)}, u32[]{:S(2)}, u32[]{:S(2)}) collective-permute-start(bf16[88,2048]{1,0:T(8,128)(2,1)S(1)} %collective-permute-done.8.refs_0_), channel_id=1, source_target_pairs={{0,16},{16,0},{1,17},{17,1},{2,18},{18,2},{3,19},{19,3},{4,20},{20... | collective-permute-start | bytes 1081352 | tf_op jit(solution)/shard_map/ppermute | solution.py:309
  45.6 7.5 %collective-permute-start.13 = (bf16[88,2048]{1,0:T(8,128)(2,1)S(1)}, bf16[88,2048]{1,0:T(8,128)(2,1)S(1)}, u32[]{:S(2)}, u32[]{:S(2)}) collective-permute-start(bf16[88,2048]{1,0:T(8,128)(2,1)S(1)} %collective-permute-done.8.refs_0_), channel_id=1, source_target_pairs={{0,64},{16,208},{64,128},{80,16},{128,192},{144,80},{192,0},{208,1... | collective-permute-start | bytes 1081352 | tf_op jit(solution)/shard_map/ppermute | solution.py:294
  53.1 6.9 %collective-permute-start.17 = (bf16[88,2048]{1,0:T(8,128)(2,1)S(1)}, bf16[88,2048]{1,0:T(8,128)(2,1)S(1)}, u32[]{:S(2)}, u32[]{:S(2)}) collective-permute-start(bf16[88,2048]{1,0:T(8,128)(2,1)S(1)} %collective-permute-done.13.refs_0_), channel_id=1, source_target_pairs={{0,16},{16,0},{1,17},{17,1},{2,18},{18,2},{3,19},{19,3},{4,20},{20... | collective-permute-start | bytes 1081352 | tf_op jit(solution)/shard_map/ppermute | solution.py:309
  54.7 12.4 %collective-permute-start.18 = (s16[368,640]{1,0:T(8,128)(2,1)S(1)}, s16[368,640]{1,0:T(8,128)(2,1)S(1)}, u32[]{:S(2)}, u32[]{:S(2)}) collective-permute-start(s16[368,640]{1,0:T(8,128)(2,1)S(1)} %get-tuple-element.137), channel_id=1, source_target_pairs={{0,1},{1,0},{2,3},{3,2},{4,5},{5,4},{6,7},{7,6},{8,9},{9,8},{10,11... | collective-permute-start | bytes 1413128 | tf_op jit(solution)/shard_map/ppermute | solution.py:309
  59.5 17.7 %collective-permute-start.19 = (s16[368,640]{1,0:T(8,128)(2,1)S(1)}, s16[368,640]{1,0:T(8,128)(2,1)S(1)}, u32[]{:S(2)}, u32[]{:S(2)}) collective-permute-start(s16[368,640]{1,0:T(8,128)(2,1)S(1)} %get-tuple-element.153), channel_id=1, source_target_pairs={{0,1},{1,0},{2,3},{3,2},{4,5},{5,4},{6,7},{7,6},{8,9},{9,8},{10,11... | collective-permute-start | bytes 1413128 | tf_op jit(solution)/shard_map/ppermute | solution.py:309
  62.0 20.5 %collective-permute-start.20 = (s16[192,640]{1,0:T(8,128)(2,1)S(1)}, s16[192,640]{1,0:T(8,128)(2,1)S(1)}, u32[]{:S(2)}, u32[]{:S(2)}) collective-permute-start(s16[192,640]{1,0:T(8,128)(2,1)S(1)} %get-tuple-element.159), channel_id=1, source_target_pairs={{0,1},{1,0},{2,3},{3,2},{4,5},{5,4},{6,7},{7,6},{8,9},{9,8},{10,11... | collective-permute-start | bytes 737288 | tf_op jit(solution)/shard_map/ppermute | solution.py:309
  100.7 3.6 %collective-permute-start.21 = (f32[4,1408]{1,0:T(4,128)S(1)}, f32[4,1408]{1,0:T(4,128)S(1)}, u32[]{:S(2)}, u32[]{:S(2)}) collective-permute-start(f32[4,1408]{1,0:T(4,128)S(1)} %first_merge.1.one_ref), channel_id=1, source_target_pairs={{0,16},{16,0},{1,17},{17,1},{2,18},{18,2},{3,19},{19,3},{4,20},{20... | collective-permute-start | bytes 67592 | tf_op jit(solution)/shard_map/ppermute | solution.py:309
  (2 other events, 3.5 us)

commit v4 on v3

--- a/solution.py
+++ b/solution.py
@@ -16,11 +16,10 @@
 TOP_CODE = 32000.0
 MIB = 1024 * 1024
 CHUNKS = (
-    ((0, 0, 0), (0, 0, 1)),
-    ((1, 0, 0), (1, 0, 1), (2, 0, 0), (2, 0, 1)),
-    ((0, 1, 0), (0, 1, 1), (3, 0, 0), (3, 0, 1)),
-    ((1, 1, 0), (1, 1, 1), (2, 1, 0), (2, 1, 1)),
-    ((3, 1, 0), (3, 1, 1)),
+    ((0, 0, 0), (0, 0, 1), (1, 0, 0), (2, 0, 0)),
+    ((1, 0, 1), (2, 0, 1), (0, 1, 0), (3, 0, 0)),
+    ((0, 1, 1), (3, 0, 1), (1, 1, 0), (2, 1, 0)),
+    ((1, 1, 1), (2, 1, 1), (3, 1, 0), (3, 1, 1)),
 )
 BLOCKS = tuple(block for chunk in CHUNKS for block in chunk)
 FIRST = tuple(sum(len(chunk) for chunk in CHUNKS[:k]) for k in range(len(CHUNKS)))
@@ -351,44 +350,34 @@
     across = along_y(across)
     far = along_x(one, 1)
     one2, two2 = swap(one, "c"), swap(two, "c")
-    made0 = chunk_front(normed, own2)
+    made0 = chunk_front(normed, own2, one, two)
     code0 = swap(made0[1], "t")
-    across, far, one, two, one2, two2, made0 = together(across, far, one, two, one2, two2, made0)
+    across, far, one2, two2, made0 = together(across, far, one2, two2, made0)
 
     y_one, y_two = along_x(across, 1), along_x(across, -1)
     across2, far2 = swap(across, "c"), swap(far, "c")
-    made1 = chunk_front(one, one2, two, two2)
+    made1 = chunk_front(one2, two2, across, far)
     code1 = swap(made1[1], "t")
-    y_one, y_two, across, across2, far, far2, made1, code0 = together(
-        y_one, y_two, across, across2, far, far2, made1, code0
-    )
+    y_one, y_two, across2, far2, made1, code0 = together(y_one, y_two, across2, far2, made1, code0)
 
     y_far = along_x(y_one, 1)
     y_one2, y_two2 = swap(y_one, "c"), swap(y_two, "c")
     expo0 = chunk_expo(0, made0, code0)
-    made2 = chunk_front(across, across2, far, far2)
+    made2 = chunk_front(across2, far2, y_one, y_two)
     code2 = swap(made2[1], "t")
-    y_far, y_one, y_two, y_one2, y_two2, made2, expo0, code1 = together(
-        y_far, y_one, y_two, y_one2, y_two2, made2, expo0, code1
-    )
+    y_far, y_one2, y_two2, made2, expo0, code1 = together(y_far, y_one2, y_two2, made2, expo0, code1)
 
     y_far2 = swap(y_far, "c")
-    made3 = chunk_front(y_one, y_one2, y_two, y_two2)
+    expo1 = chunk_expo(1, made1, code1)
+    y_far2, expo1 = together(y_far2, expo1)
+    made3 = chunk_front(y_one2, y_two2, y_far, y_far2)
     code3 = swap(made3[1], "t")
-    y_far, y_far2, made3 = together(y_far, y_far2, made3)
-
-    made4 = chunk_front(y_far, y_far2)
-    code4 = swap(made4[1], "t")
-    expo1 = chunk_expo(1, made1, code1)
-    made4, expo1, code2 = together(made4, expo1, code2)
-
+    made3, code2 = together(made3, code2)
     expo2 = chunk_expo(2, made2, code2)
     expo2, code3 = together(expo2, code3)
     expo3 = chunk_expo(3, made3, code3)
-    expo3, code4 = together(expo3, code4)
-    expo4 = chunk_expo(4, made4, code4)
-    xs = [m[3] for m in (made0, made1, made2, made3, made4)]
-    es, stats, dense = zip(expo0, expo1, expo2, expo3, expo4)
+    xs = [m[3] for m in (made0, made1, made2, made3)]
+    es, stats, dense = zip(expo0, expo1, expo2, expo3)
     tokens = size * len(BLOCKS)
     own = small_kernel(copies_kernel, "copies", (lax.axis_size("z"), 4, tokens), [], *dense)
     rest = ("x", "yh", "t")

time: 150 us -> 147 us (0.980)
    ppermute x6, waiting for transfers between devices: 7.66 us -> 2.61 us  [along_x(): return lax.ppermute(x, ('x', 'c'), pairs)]
    ppermute x14 -> x13, waiting for transfers between devices: 16.5 us -> 20.5 us  [swap(): return lax.ppermute(x, (axis,), [(0, 1), (1, 0)])]
    ppermute x6, starting transfers between devices: 11.1 us -> 8.82 us  [along_x(): return lax.ppermute(x, ('x', 'c'), pairs)]
    pallas_call x5 -> x4, Pallas kernels: 5.81 us -> 4.91 us  [expo(): pl.pallas_call(functools.partial(expo_kernel, first=first, size=size, cou...]
    pallas_call x5 -> x4, Pallas kernels: 15.2 us -> 14.7 us  [front(): pl.pallas_call(functools.partial(front_kernel, pieces=len(pieces), rows=r...]
    ppermute x14 -> x13, starting transfers between devices: 15.5 us -> 15.5 us  [swap(): return lax.ppermute(x, (axis,), [(0, 1), (1, 0)])]
  transfers between devices with their start and end apart: 22 -> 21, of which waited for: 8 -> 8; matrix products, arithmetic and copies ran while one was open for 0% -> 0% of each run, Pallas kernels for 14% -> 13%
where the time goes in v4:
time: 147 us
  blocking collectives  56.2 us (38%)
  Pallas kernels  30.2 us (21%)
  starting transfers between devices  28.4 us (19%)
  waiting for transfers between devices  23.7 us (16%)
  local copies, waits for them, and re-layouts  3.77 us (3%)
  other arithmetic  3.75 us (3%)
    all_to_all x2, blocking collectives, everyone(): return lax.all_to_all(copies, axes, 0, 0, tiled=True)  22.2 us
    ppermute x13, waiting for transfers between devices, swap(): return lax.ppermute(x, (axis,), [(0, 1), (1, 0)])  20.5 us
    all_to_all x1, blocking collectives, local(): lax.all_to_all(own, 'z', 0, 0, tiled=True)  16.3 us
    ppermute x13, starting transfers between devices, swap(): return lax.ppermute(x, (axis,), [(0, 1), (1, 0)])  15.5 us
    pallas_call x4, Pallas kernels, front(): pl.pallas_call(functools.partial(front_kernel, pieces=len(pieces), rows=r...  14.7 us
    all_to_all x1, blocking collectives, local(): lax.all_to_all(on_chip, rest, 0, 0, tiled=True)  13.3 us
    pallas_call x1, Pallas kernels, finish(): pl.pallas_call(functools.partial(product_kernel, chunks=chunks, size=size...  9.22 us
    ppermute x6, starting transfers between devices, along_x(): return lax.ppermute(x, ('x', 'c'), pairs)  8.82 us
  transfers between devices with their start and end apart: 21, of which 8 were waited for; matrix products, arithmetic and copies ran while one was open for 0% of the time, Pallas kernels for 13%

profile of v4, /device:TPU:1, one launch (start us, length us, event | category | flops | bytes accessed | tf_op | source)
XLA Modules:
  0.0 146.9 jit_solution(1001279460451311183)
XLA Ops:
  2.8 4.4 %psum.7 = f32[88]{0:T(128)S(1)} all-reduce(f32[88]{0:T(128)S(1)} %fusion), channel_id=1, replica_groups=mesh['x'=4,'yh'=2,'c'=2,'z'=8,'t'=2] {'t'}, use_global_device_ids=true, to_apply=%region_1.2 | all-reduce | flops 88 | bytes 704 | tf_op jit(solution)/shard_map/psum | solution.py:334
  8.4 3.8 %collective-permute-start.3 = (bf16[88,2048]{1,0:T(8,128)(2,1)S(1)}, bf16[88,2048]{1,0:T(8,128)(2,1)S(1)}, u32[]{:S(2)}, u32[]{:S(2)}) collective-permute-start(bf16[88,2048]{1,0:T(8,128)(2,1)S(1)} %fusion.1.refs_0_), channel_id=1, source_target_pairs={{0,16},{16,0},{1,17},{17,1},{2,18},{18,2},{3,19},{19,3},{4,20},{20... | collective-permute-start | bytes 1081352 | tf_op jit(solution)/shard_map/ppermute | solution.py:308
  12.2 2.7 %collective-permute-start.1 = (bf16[88,2048]{1,0:T(8,128)(2,1)S(1)}, bf16[88,2048]{1,0:T(8,128)(2,1)S(1)}, u32[]{:S(2)}, u32[]{:S(2)}) collective-permute-start(bf16[88,2048]{1,0:T(8,128)(2,1)S(1)} %fusion.1.refs_0_), channel_id=1, source_target_pairs={{0,64},{16,208},{64,128},{80,16},{128,192},{144,80},{192,0},{208,1... | collective-permute-start | bytes 1081352 | tf_op jit(solution)/shard_map/ppermute | solution.py:293
  15.9 1.7 %copy-done = bf16[2048,640]{1,0:T(8,128)(2,1)S(1)} copy-done((bf16[2048,640]{1,0:T(8,128)(2,1)S(1)}, bf16[2048,640]{1,0:T(8,128)(2,1)}, u32[]{:S(2)}) %copy-start) | copy-done | bytes 2621464
  17.7 1.7 %copy-done.1 = bf16[2048,640]{1,0:T(8,128)(2,1)S(1)} copy-done((bf16[2048,640]{1,0:T(8,128)(2,1)S(1)}, bf16[2048,640]{1,0:T(8,128)(2,1)}, u32[]{:S(2)}) %copy-start.1) | copy-done | bytes 2621464
  19.8 2.5 %collective-permute-done.2.refs_3_ = bf16[88,2048]{1,0:T(8,128)(2,1)S(1)} collective-permute-done((bf16[88,2048]{1,0:T(8,128)(2,1)S(1)}, bf16[88,2048]{1,0:T(8,128)(2,1)S(1)}, u32[]{:S(2)}, u32[]{:S(2)}) %collective-permute-start.2) | collective-permute-done | bytes 360480 | tf_op jit(solution)/shard_map/ppermute | solution.py:293
  22.3 2.0 %collective-permute-start.6 = (bf16[88,2048]{1,0:T(8,128)(2,1)S(1)}, bf16[88,2048]{1,0:T(8,128)(2,1)S(1)}, u32[]{:S(2)}, u32[]{:S(2)}) collective-permute-start(bf16[88,2048]{1,0:T(8,128)(2,1)S(1)} %collective-permute-done.1.refs_2_), channel_id=1, source_target_pairs={{0,16},{16,0},{1,17},{17,1},{2,18},{18,2},{3,19},{19,3},{4,20},{20... | collective-permute-start | bytes 1081352 | tf_op jit(solution)/shard_map/ppermute | solution.py:308
  25.0 3.0 %collective-permute-start.4 = (bf16[88,2048]{1,0:T(8,128)(2,1)S(1)}, bf16[88,2048]{1,0:T(8,128)(2,1)S(1)}, u32[]{:S(2)}, u32[]{:S(2)}) collective-permute-start(bf16[88,2048]{1,0:T(8,128)(2,1)S(1)} %collective-permute-done), channel_id=1, source_target_pairs={{0,1},{16,49},{1,32},{17,16},{32,33},{48,17},{33,0},{49,48},{2,3},... | collective-permute-start | bytes 1081352 | tf_op jit(solution)/shard_map/ppermute | solution.py:304
  28.0 3.7 %front.4 = (f32[352,640]{1,0:T(8,128)S(1)}, s16[368,640]{1,0:T(8,128)(2,1)S(1)}, f32[352,640]{1,0:T(8,128)S(1)}, bf16[352,2048]{1,0:T(8,128)(2,1)S(1)}) custom-call(bf16[88,2048]{1,0:T(8,128)(2,1)S(1)} %fusion.1.refs_0_, bf16[88,2048]{1,0:T(8,128)(2,1)S(1)} %collective-permute-done.3.refs_1_, bf16[88,2048]{1,0:T(8,128)(2,1)S(1)} %collective-permute-done.1.refs_2_, ...), custom_call_target="tpu_custom_call" | custom-call | flops 2768240640 | bytes 2883584 | tf_op jit(solution)/shard_map/front/pallas_call | solution.py:88
  33.2 2.8 %collective-permute-start.8 = (bf16[88,2048]{1,0:T(8,128)(2,1)S(1)}, bf16[88,2048]{1,0:T(8,128)(2,1)S(1)}, u32[]{:S(2)}, u32[]{:S(2)}) collective-permute-start(bf16[88,2048]{1,0:T(8,128)(2,1)S(1)} %collective-permute-done.4.refs_2_), channel_id=1, source_target_pairs={{0,64},{16,208},{64,128},{80,16},{128,192},{144,80},{192,0},{208,1... | collective-permute-start | bytes 1081352 | tf_op jit(solution)/shard_map/ppermute | solution.py:293
  36.4 3.6 %front.5 = (f32[352,640]{1,0:T(8,128)S(1)}, s16[368,640]{1,0:T(8,128)(2,1)S(1)}, f32[352,640]{1,0:T(8,128)S(1)}, bf16[352,2048]{1,0:T(8,128)(2,1)S(1)}) custom-call(bf16[88,2048]{1,0:T(8,128)(2,1)S(1)} %collective-permute-done.6.refs_0_, bf16[88,2048]{1,0:T(8,128)(2,1)S(1)} %collective-permute-done.7.refs_1_, ...), custom_call_target="tpu_custom_call" | custom-call | flops 2768240640 | bytes 2883584 | tf_op jit(solution)/shard_map/front/pallas_call | solution.py:88
  40.0 3.6 %collective-permute-done.12.code_ref = s16[368,640]{1,0:T(8,128)(2,1)S(1)} collective-permute-done((s16[368,640]{1,0:T(8,128)(2,1)S(1)}, s16[368,640]{1,0:T(8,128)(2,1)S(1)}, u32[]{:S(2)}, u32[]{:S(2)}) %collective-permute-start.12) | collective-permute-done | bytes 471072 | tf_op jit(solution)/shard_map/ppermute | solution.py:308
  45.5 2.6 %collective-permute-start.13 = (bf16[88,2048]{1,0:T(8,128)(2,1)S(1)}, bf16[88,2048]{1,0:T(8,128)(2,1)S(1)}, u32[]{:S(2)}, u32[]{:S(2)}) collective-permute-start(bf16[88,2048]{1,0:T(8,128)(2,1)S(1)} %collective-permute-done.8.refs_2_), channel_id=1, source_target_pairs={{0,64},{16,208},{64,128},{80,16},{128,192},{144,80},{192,0},{208,1... | collective-permute-start | bytes 1081352 | tf_op jit(solution)/shard_map/ppermute | solution.py:293
  49.3 3.7 %front.6 = (f32[352,640]{1,0:T(8,128)S(1)}, s16[368,640]{1,0:T(8,128)(2,1)S(1)}, f32[352,640]{1,0:T(8,128)S(1)}, bf16[352,2048]{1,0:T(8,128)(2,1)S(1)}) custom-call(bf16[88,2048]{1,0:T(8,128)(2,1)S(1)} %collective-permute-done.10.refs_0_, bf16[88,2048]{1,0:T(8,128)(2,1)S(1)} %collective-permute-done.11.refs_1_, ...), custom_call_target="tpu_custom_call" | custom-call | flops 2768240640 | bytes 2883584 | tf_op jit(solution)/shard_map/front/pallas_call | solution.py:88
  54.5 2.4 %collective-permute-start.17 = (bf16[88,2048]{1,0:T(8,128)(2,1)S(1)}, bf16[88,2048]{1,0:T(8,128)(2,1)S(1)}, u32[]{:S(2)}, u32[]{:S(2)}) collective-permute-start(bf16[88,2048]{1,0:T(8,128)(2,1)S(1)} %collective-permute-done.13.refs_2_), channel_id=1, source_target_pairs={{0,16},{16,0},{1,17},{17,1},{2,18},{18,2},{3,19},{19,3},{4,20},{20... | collective-permute-start | bytes 1081352 | tf_op jit(solution)/shard_map/ppermute | solution.py:308
  58.5 3.7 %front.7 = (f32[352,640]{1,0:T(8,128)S(1)}, s16[368,640]{1,0:T(8,128)(2,1)S(1)}, f32[352,640]{1,0:T(8,128)S(1)}, bf16[352,2048]{1,0:T(8,128)(2,1)S(1)}) custom-call(bf16[88,2048]{1,0:T(8,128)(2,1)S(1)} %collective-permute-done.14.refs_0_, bf16[88,2048]{1,0:T(8,128)(2,1)S(1)} %collective-permute-done.15.refs_1_, ...), custom_call_target="tpu_custom_call" | custom-call | flops 2768240640 | bytes 2883584 | tf_op jit(solution)/shard_map/front/pallas_call | solution.py:88
  63.4 5.6 %collective-permute-done.18.code_ref = s16[368,640]{1,0:T(8,128)(2,1)S(1)} collective-permute-done((s16[368,640]{1,0:T(8,128)(2,1)S(1)}, s16[368,640]{1,0:T(8,128)(2,1)S(1)}, u32[]{:S(2)}, u32[]{:S(2)}) %collective-permute-start.18) | collective-permute-done | bytes 471072 | tf_op jit(solution)/shard_map/ppermute | solution.py:308
  70.2 8.9 %collective-permute-done.19.code_ref = s16[368,640]{1,0:T(8,128)(2,1)S(1)} collective-permute-done((s16[368,640]{1,0:T(8,128)(2,1)S(1)}, s16[368,640]{1,0:T(8,128)(2,1)S(1)}, u32[]{:S(2)}, u32[]{:S(2)}) %collective-permute-start.19) | collective-permute-done | bytes 471072 | tf_op jit(solution)/shard_map/ppermute | solution.py:308
  80.4 16.3 %all_to_all.20.parts_ref = f32[8,4,1408]{2,1,0:T(4,128)S(1)} all-to-all(f32[8,4,1408]{2,1,0:T(4,128)S(1)} %copies.1), channel_id=1, replica_groups=mesh['x'=4,'yh'=2,'c'=2,'z'=8,'t'=2] {'z'}, dimensions={0} | all-to-all | bytes 360448 | tf_op jit(solution)/shard_map/all_to_all | solution.py:391
  97.4 2.8 %collective-permute-start.20 = (f32[4,1408]{1,0:T(4,128)S(1)}, f32[4,1408]{1,0:T(4,128)S(1)}, u32[]{:S(2)}, u32[]{:S(2)}) collective-permute-start(f32[4,1408]{1,0:T(4,128)S(1)} %first_merge.1.one_ref), channel_id=1, source_target_pairs={{0,16},{16,0},{1,17},{17,1},{2,18},{18,2},{3,19},{19,3},{4,20},{20... | collective-permute-start | bytes 67592 | tf_op jit(solution)/shard_map/ppermute | solution.py:308
  101.2 13.3 %all_to_all.21.parts_ref = f32[16,4,1408]{2,1,0:T(4,128)S(1)} all-to-all(f32[16,4,1408]{2,1,0:T(4,128)S(1)} %pair_merge.1), channel_id=1, replica_groups=mesh['x'=4,'yh'=2,'c'=2,'z'=8,'t'=2] {'x','yh','t'}, dimensions={0} | all-to-all | bytes 720896 | tf_op jit(solution)/shard_map/all_to_all | solution.py:401
  114.6 9.2 %product.1 = (f32[2048,640]{1,0:T(8,128)}, f32[1,2048]{1,0:T(1,128)S(1)}) custom-call(s32[16]{0:T(128)S(1)} %stack.67.place_ref.refs_0_, f32[16,128]{1,0:T(8,128)S(1)} %pad.4.ids_ref.refs_1_, f32[16,4,128]{2,1,0:T(4,128)S(1)} %last_merge.1.refs_2_, f32[352,640]{1,0:T(8,128)S(1)} %get-tuple-element.148.refs_3_, f32[352,640]{1,0:T(8,128)S(1)} %get-tuple-element.149.refs_4_, ...), custom_call_target="tpu_custom_call" | custom-call | flops 3690987520 | bytes 5242880 | tf_op jit(solution)/shard_map/product/pallas_call | solution.py:253
  123.9 12.7 %all_to_all.22 = f32[16,1,2048]{2,1,0:T(1,128)S(1)} all-to-all(f32[16,1,2048]{2,1,0:T(1,128)S(1)} %broadcast_in_dim.24), channel_id=1, replica_groups=mesh['x'=4,'yh'=2,'c'=2,'z'=8,'t'=2] {'x','yh','c'}, dimensions={0} | all-to-all | bytes 262144 | tf_op jit(solution)/shard_map/all_to_all | solution.py:285
  136.7 9.5 %all_to_all.23 = f32[8,1,2048]{2,1,0:T(1,128)S(1)} all-to-all(f32[8,1,2048]{2,1,0:T(1,128)S(1)} %broadcast_in_dim.25), channel_id=1, replica_groups=mesh['x'=4,'yh'=2,'c'=2,'z'=8,'t'=2] {'z'}, dimensions={0} | all-to-all | bytes 131072 | tf_op jit(solution)/shard_map/all_to_all | solution.py:285
  (56 shorter events, 19.7 us)
Async XLA Ops:
  7.3 20.7 %copy-start.2 = (f32[2048]{0:T(1024)S(1)}, f32[2048]{0:T(1024)}, u32[]{:S(2)}) copy-start(f32[2048]{0:T(1024)} %param.8) | copy-start | bytes 24580
  7.3 20.7 %copy-start.3 = (f32[2048]{0:T(1024)S(1)}, f32[2048]{0:T(1024)}, u32[]{:S(2)}) copy-start(f32[2048]{0:T(1024)} %param.7) | copy-start | bytes 24580
  8.4 11.4 %collective-permute-start.3 = (bf16[88,2048]{1,0:T(8,128)(2,1)S(1)}, bf16[88,2048]{1,0:T(8,128)(2,1)S(1)}, u32[]{:S(2)}, u32[]{:S(2)}) collective-permute-start(bf16[88,2048]{1,0:T(8,128)(2,1)S(1)} %fusion.1.refs_0_), channel_id=1, source_target_pairs={{0,16},{16,0},{1,17},{17,1},{2,18},{18,2},{3,19},{19,3},{4,20},{20... | collective-permute-start | bytes 1081352 | tf_op jit(solution)/shard_map/ppermute | solution.py:308
  12.2 10.0 %collective-permute-start.2 = (bf16[88,2048]{1,0:T(8,128)(2,1)S(1)}, bf16[88,2048]{1,0:T(8,128)(2,1)S(1)}, u32[]{:S(2)}, u32[]{:S(2)}) collective-permute-start(bf16[88,2048]{1,0:T(8,128)(2,1)S(1)} %fusion.1.refs_0_), channel_id=1, source_target_pairs={{0,192},{16,80},{64,0},{80,144},{128,64},{144,208},{192,128},{208,... | collective-permute-start | bytes 1081352 | tf_op jit(solution)/shard_map/ppermute | solution.py:293
  12.2 10.0 %collective-permute-start.1 = (bf16[88,2048]{1,0:T(8,128)(2,1)S(1)}, bf16[88,2048]{1,0:T(8,128)(2,1)S(1)}, u32[]{:S(2)}, u32[]{:S(2)}) collective-permute-start(bf16[88,2048]{1,0:T(8,128)(2,1)S(1)} %fusion.1.refs_0_), channel_id=1, source_target_pairs={{0,64},{16,208},{64,128},{80,16},{128,192},{144,80},{192,0},{208,1... | collective-permute-start | bytes 1081352 | tf_op jit(solution)/shard_map/ppermute | solution.py:293
  14.9 7.3 %collective-permute-start = (bf16[88,2048]{1,0:T(8,128)(2,1)S(1)}, bf16[88,2048]{1,0:T(8,128)(2,1)S(1)}, u32[]{:S(2)}, u32[]{:S(2)}) collective-permute-start(bf16[88,2048]{1,0:T(8,128)(2,1)S(1)} %fusion.1.refs_0_), channel_id=1, source_target_pairs={{0,1},{16,49},{1,32},{17,16},{32,33},{48,17},{33,0},{49,48},{2,3},... | collective-permute-start | bytes 1081352 | tf_op jit(solution)/shard_map/ppermute | solution.py:304
  15.9 1.7 %copy-start = (bf16[2048,640]{1,0:T(8,128)(2,1)S(1)}, bf16[2048,640]{1,0:T(8,128)(2,1)}, u32[]{:S(2)}) copy-start(bf16[2048,640]{1,0:T(8,128)(2,1)} %refs_0_.1) | copy-start | bytes 7864324
  22.3 10.1 %collective-permute-start.6 = (bf16[88,2048]{1,0:T(8,128)(2,1)S(1)}, bf16[88,2048]{1,0:T(8,128)(2,1)S(1)}, u32[]{:S(2)}, u32[]{:S(2)}) collective-permute-start(bf16[88,2048]{1,0:T(8,128)(2,1)S(1)} %collective-permute-done.1.refs_2_), channel_id=1, source_target_pairs={{0,16},{16,0},{1,17},{17,1},{2,18},{18,2},{3,19},{19,3},{4,20},{20... | collective-permute-start | bytes 1081352 | tf_op jit(solution)/shard_map/ppermute | solution.py:308
  24.3 8.1 %collective-permute-start.5 = (bf16[88,2048]{1,0:T(8,128)(2,1)S(1)}, bf16[88,2048]{1,0:T(8,128)(2,1)S(1)}, u32[]{:S(2)}, u32[]{:S(2)}) collective-permute-start(bf16[88,2048]{1,0:T(8,128)(2,1)S(1)} %collective-permute-done.1.refs_2_), channel_id=1, source_target_pairs={{0,64},{16,208},{64,128},{80,16},{128,192},{144,80},{192,0},{208,1... | collective-permute-start | bytes 1081352 | tf_op jit(solution)/shard_map/ppermute | solution.py:293
  25.0 7.4 %collective-permute-start.4 = (bf16[88,2048]{1,0:T(8,128)(2,1)S(1)}, bf16[88,2048]{1,0:T(8,128)(2,1)S(1)}, u32[]{:S(2)}, u32[]{:S(2)}) collective-permute-start(bf16[88,2048]{1,0:T(8,128)(2,1)S(1)} %collective-permute-done), channel_id=1, source_target_pairs={{0,1},{16,49},{1,32},{17,16},{32,33},{48,17},{33,0},{49,48},{2,3},... | collective-permute-start | bytes 1081352 | tf_op jit(solution)/shard_map/ppermute | solution.py:304
  28.0 4.4 %collective-permute-start.7 = (bf16[88,2048]{1,0:T(8,128)(2,1)S(1)}, bf16[88,2048]{1,0:T(8,128)(2,1)S(1)}, u32[]{:S(2)}, u32[]{:S(2)}) collective-permute-start(bf16[88,2048]{1,0:T(8,128)(2,1)S(1)} %collective-permute-done.2.refs_3_), channel_id=1, source_target_pairs={{0,16},{16,0},{1,17},{17,1},{2,18},{18,2},{3,19},{19,3},{4,20},{20... | collective-permute-start | bytes 1081352 | tf_op jit(solution)/shard_map/ppermute | solution.py:308
  31.7 11.9 %collective-permute-start.12 = (s16[368,640]{1,0:T(8,128)(2,1)S(1)}, s16[368,640]{1,0:T(8,128)(2,1)S(1)}, u32[]{:S(2)}, u32[]{:S(2)}) collective-permute-start(s16[368,640]{1,0:T(8,128)(2,1)S(1)} %get-tuple-element.96), channel_id=1, source_target_pairs={{0,1},{1,0},{2,3},{3,2},{4,5},{5,4},{6,7},{7,6},{8,9},{9,8},{10,11... | collective-permute-start | bytes 1413128 | tf_op jit(solution)/shard_map/ppermute | solution.py:308
  32.4 11.6 %collective-permute-start.10 = (bf16[88,2048]{1,0:T(8,128)(2,1)S(1)}, bf16[88,2048]{1,0:T(8,128)(2,1)S(1)}, u32[]{:S(2)}, u32[]{:S(2)}) collective-permute-start(bf16[88,2048]{1,0:T(8,128)(2,1)S(1)} %collective-permute-done.4.refs_2_), channel_id=1, source_target_pairs={{0,16},{16,0},{1,17},{17,1},{2,18},{18,2},{3,19},{19,3},{4,20},{20... | collective-permute-start | bytes 1081352 | tf_op jit(solution)/shard_map/ppermute | solution.py:308
  33.1 10.8 %collective-permute-start.9 = (bf16[88,2048]{1,0:T(8,128)(2,1)S(1)}, bf16[88,2048]{1,0:T(8,128)(2,1)S(1)}, u32[]{:S(2)}, u32[]{:S(2)}) collective-permute-start(bf16[88,2048]{1,0:T(8,128)(2,1)S(1)} %collective-permute-done.4.refs_2_), channel_id=1, source_target_pairs={{0,192},{16,80},{64,0},{80,144},{128,64},{144,208},{192,128},{208,... | collective-permute-start | bytes 1081352 | tf_op jit(solution)/shard_map/ppermute | solution.py:293
  33.2 10.9 %collective-permute-start.8 = (bf16[88,2048]{1,0:T(8,128)(2,1)S(1)}, bf16[88,2048]{1,0:T(8,128)(2,1)S(1)}, u32[]{:S(2)}, u32[]{:S(2)}) collective-permute-start(bf16[88,2048]{1,0:T(8,128)(2,1)S(1)} %collective-permute-done.4.refs_2_), channel_id=1, source_target_pairs={{0,64},{16,208},{64,128},{80,16},{128,192},{144,80},{192,0},{208,1... | collective-permute-start | bytes 1081352 | tf_op jit(solution)/shard_map/ppermute | solution.py:293
  36.0 7.9 %collective-permute-start.11 = (bf16[88,2048]{1,0:T(8,128)(2,1)S(1)}, bf16[88,2048]{1,0:T(8,128)(2,1)S(1)}, u32[]{:S(2)}, u32[]{:S(2)}) collective-permute-start(bf16[88,2048]{1,0:T(8,128)(2,1)S(1)} %collective-permute-done.5.refs_3_), channel_id=1, source_target_pairs={{0,16},{16,0},{1,17},{17,1},{2,18},{18,2},{3,19},{19,3},{4,20},{20... | collective-permute-start | bytes 1081352 | tf_op jit(solution)/shard_map/ppermute | solution.py:308
  43.6 10.9 %collective-permute-start.16 = (s16[368,640]{1,0:T(8,128)(2,1)S(1)}, s16[368,640]{1,0:T(8,128)(2,1)S(1)}, u32[]{:S(2)}, u32[]{:S(2)}) collective-permute-start(s16[368,640]{1,0:T(8,128)(2,1)S(1)} %get-tuple-element.104), channel_id=1, source_target_pairs={{0,1},{1,0},{2,3},{3,2},{4,5},{5,4},{6,7},{7,6},{8,9},{9,8},{10,11... | collective-permute-start | bytes 1413128 | tf_op jit(solution)/shard_map/ppermute | solution.py:308
  44.1 10.4 %collective-permute-start.15 = (bf16[88,2048]{1,0:T(8,128)(2,1)S(1)}, bf16[88,2048]{1,0:T(8,128)(2,1)S(1)}, u32[]{:S(2)}, u32[]{:S(2)}) collective-permute-start(bf16[88,2048]{1,0:T(8,128)(2,1)S(1)} %collective-permute-done.9.refs_3_), channel_id=1, source_target_pairs={{0,16},{16,0},{1,17},{17,1},{2,18},{18,2},{3,19},{19,3},{4,20},{20... | collective-permute-start | bytes 1081352 | tf_op jit(solution)/shard_map/ppermute | solution.py:308
  45.4 9.2 %collective-permute-start.14 = (bf16[88,2048]{1,0:T(8,128)(2,1)S(1)}, bf16[88,2048]{1,0:T(8,128)(2,1)S(1)}, u32[]{:S(2)}, u32[]{:S(2)}) collective-permute-start(bf16[88,2048]{1,0:T(8,128)(2,1)S(1)} %collective-permute-done.8.refs_2_), channel_id=1, source_target_pairs={{0,16},{16,0},{1,17},{17,1},{2,18},{18,2},{3,19},{19,3},{4,20},{20... | collective-permute-start | bytes 1081352 | tf_op jit(solution)/shard_map/ppermute | solution.py:308
  45.5 9.1 %collective-permute-start.13 = (bf16[88,2048]{1,0:T(8,128)(2,1)S(1)}, bf16[88,2048]{1,0:T(8,128)(2,1)S(1)}, u32[]{:S(2)}, u32[]{:S(2)}) collective-permute-start(bf16[88,2048]{1,0:T(8,128)(2,1)S(1)} %collective-permute-done.8.refs_2_), channel_id=1, source_target_pairs={{0,64},{16,208},{64,128},{80,16},{128,192},{144,80},{192,0},{208,1... | collective-permute-start | bytes 1081352 | tf_op jit(solution)/shard_map/ppermute | solution.py:293
  54.5 3.9 %collective-permute-start.17 = (bf16[88,2048]{1,0:T(8,128)(2,1)S(1)}, bf16[88,2048]{1,0:T(8,128)(2,1)S(1)}, u32[]{:S(2)}, u32[]{:S(2)}) collective-permute-start(bf16[88,2048]{1,0:T(8,128)(2,1)S(1)} %collective-permute-done.13.refs_2_), channel_id=1, source_target_pairs={{0,16},{16,0},{1,17},{17,1},{2,18},{18,2},{3,19},{19,3},{4,20},{20... | collective-permute-start | bytes 1081352 | tf_op jit(solution)/shard_map/ppermute | solution.py:308
  56.9 12.1 %collective-permute-start.18 = (s16[368,640]{1,0:T(8,128)(2,1)S(1)}, s16[368,640]{1,0:T(8,128)(2,1)S(1)}, u32[]{:S(2)}, u32[]{:S(2)}) collective-permute-start(s16[368,640]{1,0:T(8,128)(2,1)S(1)} %get-tuple-element.112), channel_id=1, source_target_pairs={{0,1},{1,0},{2,3},{3,2},{4,5},{5,4},{6,7},{7,6},{8,9},{9,8},{10,11... | collective-permute-start | bytes 1413128 | tf_op jit(solution)/shard_map/ppermute | solution.py:308
  62.2 16.9 %collective-permute-start.19 = (s16[368,640]{1,0:T(8,128)(2,1)S(1)}, s16[368,640]{1,0:T(8,128)(2,1)S(1)}, u32[]{:S(2)}, u32[]{:S(2)}) collective-permute-start(s16[368,640]{1,0:T(8,128)(2,1)S(1)} %get-tuple-element.135), channel_id=1, source_target_pairs={{0,1},{1,0},{2,3},{3,2},{4,5},{5,4},{6,7},{7,6},{8,9},{9,8},{10,11... | collective-permute-start | bytes 1413128 | tf_op jit(solution)/shard_map/ppermute | solution.py:308
  97.4 3.7 %collective-permute-start.20 = (f32[4,1408]{1,0:T(4,128)S(1)}, f32[4,1408]{1,0:T(4,128)S(1)}, u32[]{:S(2)}, u32[]{:S(2)}) collective-permute-start(f32[4,1408]{1,0:T(4,128)S(1)} %first_merge.1.one_ref), channel_id=1, source_target_pairs={{0,16},{16,0},{1,17},{17,1},{2,18},{18,2},{3,19},{19,3},{4,20},{20... | collective-permute-start | bytes 67592 | tf_op jit(solution)/shard_map/ppermute | solution.py:308
  (1 other events, 1.7 us)

commit v5 on v4

--- a/solution.py
+++ b/solution.py
@@ -16,7 +16,8 @@
 TOP_CODE = 32000.0
 MIB = 1024 * 1024
 CHUNKS = (
-    ((0, 0, 0), (0, 0, 1), (1, 0, 0), (2, 0, 0)),
+    ((0, 0, 0), (0, 0, 1)),
+    ((1, 0, 0), (2, 0, 0)),
     ((1, 0, 1), (2, 0, 1), (0, 1, 0), (3, 0, 0)),
     ((0, 1, 1), (3, 0, 1), (1, 1, 0), (2, 1, 0)),
     ((1, 1, 1), (2, 1, 1), (3, 1, 0), (3, 1, 1)),
@@ -344,40 +345,44 @@
 
     across = along_y(normed)
     one, two = along_x(normed, 1), along_x(normed, -1)
-    own2 = swap(normed, "c")
-    across, one, two, own2, weight, slope = together(across, one, two, own2, weight, slope)
+    made0 = chunk_front(normed, swap(normed, "c"))
+    code0 = swap(made0[1], "t")
+    across, one, two, made0 = together(across, one, two, made0)
 
     across = along_y(across)
     far = along_x(one, 1)
     one2, two2 = swap(one, "c"), swap(two, "c")
-    made0 = chunk_front(normed, own2, one, two)
-    code0 = swap(made0[1], "t")
-    across, far, one2, two2, made0 = together(across, far, one2, two2, made0)
+    made1 = chunk_front(one, two)
+    code1 = swap(made1[1], "t")
+    across, far, one2, two2, made1, code0 = together(across, far, one2, two2, made1, code0)
 
     y_one, y_two = along_x(across, 1), along_x(across, -1)
     across2, far2 = swap(across, "c"), swap(far, "c")
-    made1 = chunk_front(one2, two2, across, far)
-    code1 = swap(made1[1], "t")
-    y_one, y_two, across2, far2, made1, code0 = together(y_one, y_two, across2, far2, made1, code0)
+    expo0 = chunk_expo(0, made0, code0)
+    made2 = chunk_front(one2, two2, across, far)
+    code2 = swap(made2[1], "t")
+    y_one, y_two, across2, far2, made2, expo0, code1 = together(
+        y_one, y_two, across2, far2, made2, expo0, code1
+    )
 
     y_far = along_x(y_one, 1)
     y_one2, y_two2 = swap(y_one, "c"), swap(y_two, "c")
-    expo0 = chunk_expo(0, made0, code0)
-    made2 = chunk_front(across2, far2, y_one, y_two)
-    code2 = swap(made2[1], "t")
-    y_far, y_one2, y_two2, made2, expo0, code1 = together(y_far, y_one2, y_two2, made2, expo0, code1)
+    expo1 = chunk_expo(1, made1, code1)
+    made3 = chunk_front(across2, far2, y_one, y_two)
+    code3 = swap(made3[1], "t")
+    y_far, y_one2, y_two2, made3, expo1, code2 = together(y_far, y_one2, y_two2, made3, expo1, code2)
 
     y_far2 = swap(y_far, "c")
-    expo1 = chunk_expo(1, made1, code1)
-    y_far2, expo1 = together(y_far2, expo1)
-    made3 = chunk_front(y_one2, y_two2, y_far, y_far2)
-    code3 = swap(made3[1], "t")
-    made3, code2 = together(made3, code2)
     expo2 = chunk_expo(2, made2, code2)
-    expo2, code3 = together(expo2, code3)
+    y_far2, expo2 = together(y_far2, expo2)
+    made4 = chunk_front(y_one2, y_two2, y_far, y_far2)
+    code4 = swap(made4[1], "t")
+    made4, code3 = together(made4, code3)
     expo3 = chunk_expo(3, made3, code3)
-    xs = [m[3] for m in (made0, made1, made2, made3)]
-    es, stats, dense = zip(expo0, expo1, expo2, expo3)
+    expo3, code4 = together(expo3, code4)
+    expo4 = chunk_expo(4, made4, code4)
+    xs = [m[3] for m in (made0, made1, made2, made3, made4)]
+    es, stats, dense = zip(expo0, expo1, expo2, expo3, expo4)
     tokens = size * len(BLOCKS)
     own = small_kernel(copies_kernel, "copies", (lax.axis_size("z"), 4, tokens), [], *dense)
     rest = ("x", "yh", "t")

time: 147 us -> 149 us (1.014)
    ppermute x6, starting transfers between devices: 8.82 us -> 11.1 us  [along_x(): return lax.ppermute(x, ('x', 'c'), pairs)]
    pallas_call x4 -> x5, Pallas kernels: 4.91 us -> 5.8 us  [expo(): pl.pallas_call(functools.partial(expo_kernel, first=first, size=size, cou...]
    ppermute x13 -> x14, waiting for transfers between devices: 20.5 us -> 19.7 us  [swap(): return lax.ppermute(x, (axis,), [(0, 1), (1, 0)])]
    pallas_call x4 -> x5, Pallas kernels: 14.7 us -> 15.2 us  [front(): pl.pallas_call(functools.partial(front_kernel, pieces=len(pieces), rows=r...]
    ppermute x13 -> x14, starting transfers between devices: 15.5 us -> 15.6 us  [swap(): return lax.ppermute(x, (axis,), [(0, 1), (1, 0)])]
  transfers between devices with their start and end apart: 21 -> 22, of which waited for: 8 -> 8; matrix products, arithmetic and copies ran while one was open for 0% -> 0% of each run, Pallas kernels for 13% -> 13%
where the time goes in v5:
time: 149 us
  blocking collectives  56.6 us (38%)
  Pallas kernels  31.6 us (21%)
  starting transfers between devices  29.7 us (20%)
  waiting for transfers between devices  22.6 us (15%)
  local copies, waits for them, and re-layouts  3.77 us (3%)
  other arithmetic  3.75 us (3%)
    all_to_all x2, blocking collectives, everyone(): return lax.all_to_all(copies, axes, 0, 0, tiled=True)  22.2 us
    ppermute x14, waiting for transfers between devices, swap(): return lax.ppermute(x, (axis,), [(0, 1), (1, 0)])  19.7 us
    all_to_all x1, blocking collectives, local(): lax.all_to_all(own, 'z', 0, 0, tiled=True)  16.2 us
    ppermute x14, starting transfers between devices, swap(): return lax.ppermute(x, (axis,), [(0, 1), (1, 0)])  15.6 us
    pallas_call x5, Pallas kernels, front(): pl.pallas_call(functools.partial(front_kernel, pieces=len(pieces), rows=r...  15.2 us
    all_to_all x1, blocking collectives, local(): lax.all_to_all(on_chip, rest, 0, 0, tiled=True)  13.8 us
    ppermute x6, starting transfers between devices, along_x(): return lax.ppermute(x, ('x', 'c'), pairs)  11.1 us
    pallas_call x1, Pallas kernels, finish(): pl.pallas_call(functools.partial(product_kernel, chunks=chunks, size=size...  9.27 us
  transfers between devices with their start and end apart: 22, of which 8 were waited for; matrix products, arithmetic and copies ran while one was open for 0% of the time, Pallas kernels for 13%

profile of v5, /device:TPU:1, one launch (start us, length us, event | category | flops | bytes accessed | tf_op | source)
XLA Modules:
  0.0 149.0 jit_solution(16075355734884094366)
XLA Ops:
  2.8 4.4 %psum.7 = f32[88]{0:T(128)S(1)} all-reduce(f32[88]{0:T(128)S(1)} %fusion), channel_id=1, replica_groups=mesh['x'=4,'yh'=2,'c'=2,'z'=8,'t'=2] {'t'}, use_global_device_ids=true, to_apply=%region_1.2 | all-reduce | flops 88 | bytes 704 | tf_op jit(solution)/shard_map/psum | solution.py:335
  8.4 3.8 %collective-permute-start.3 = (bf16[88,2048]{1,0:T(8,128)(2,1)S(1)}, bf16[88,2048]{1,0:T(8,128)(2,1)S(1)}, u32[]{:S(2)}, u32[]{:S(2)}) collective-permute-start(bf16[88,2048]{1,0:T(8,128)(2,1)S(1)} %fusion.1.refs_0_), channel_id=1, source_target_pairs={{0,16},{16,0},{1,17},{17,1},{2,18},{18,2},{3,19},{19,3},{4,20},{20... | collective-permute-start | bytes 1081352 | tf_op jit(solution)/shard_map/ppermute | solution.py:309
  12.2 2.7 %collective-permute-start.1 = (bf16[88,2048]{1,0:T(8,128)(2,1)S(1)}, bf16[88,2048]{1,0:T(8,128)(2,1)S(1)}, u32[]{:S(2)}, u32[]{:S(2)}) collective-permute-start(bf16[88,2048]{1,0:T(8,128)(2,1)S(1)} %fusion.1.refs_0_), channel_id=1, source_target_pairs={{0,64},{16,208},{64,128},{80,16},{128,192},{144,80},{192,0},{208,1... | collective-permute-start | bytes 1081352 | tf_op jit(solution)/shard_map/ppermute | solution.py:294
  15.9 1.7 %copy-done = bf16[2048,640]{1,0:T(8,128)(2,1)S(1)} copy-done((bf16[2048,640]{1,0:T(8,128)(2,1)S(1)}, bf16[2048,640]{1,0:T(8,128)(2,1)}, u32[]{:S(2)}) %copy-start) | copy-done | bytes 2621464
  19.8 2.0 %front.5 = (f32[176,640]{1,0:T(8,128)S(1)}, s16[192,640]{1,0:T(8,128)(2,1)S(1)}, f32[176,640]{1,0:T(8,128)S(1)}, bf16[176,2048]{1,0:T(8,128)(2,1)S(1)}) custom-call(bf16[88,2048]{1,0:T(8,128)(2,1)S(1)} %fusion.1.refs_0_, bf16[88,2048]{1,0:T(8,128)(2,1)S(1)} %collective-permute-done.3.refs_1_, f32[1,2048]{1,0:T(1,128)S(1)} %bitcast.24, ...), custom_call_target="tpu_custom_call" | custom-call | flops 1384120320 | bytes 1441792 | tf_op jit(solution)/shard_map/front/pallas_call | solution.py:89
  22.3 2.0 %collective-permute-start.4 = (bf16[88,2048]{1,0:T(8,128)(2,1)S(1)}, bf16[88,2048]{1,0:T(8,128)(2,1)S(1)}, u32[]{:S(2)}, u32[]{:S(2)}) collective-permute-start(bf16[88,2048]{1,0:T(8,128)(2,1)S(1)} %collective-permute-done), channel_id=1, source_target_pairs={{0,1},{16,49},{1,32},{17,16},{32,33},{48,17},{33,0},{49,48},{2,3},... | collective-permute-start | bytes 1081352 | tf_op jit(solution)/shard_map/ppermute | solution.py:305
  24.7 3.1 %collective-permute-start.5 = (bf16[88,2048]{1,0:T(8,128)(2,1)S(1)}, bf16[88,2048]{1,0:T(8,128)(2,1)S(1)}, u32[]{:S(2)}, u32[]{:S(2)}) collective-permute-start(bf16[88,2048]{1,0:T(8,128)(2,1)S(1)} %collective-permute-done.1.refs_0_), channel_id=1, source_target_pairs={{0,64},{16,208},{64,128},{80,16},{128,192},{144,80},{192,0},{208,1... | collective-permute-start | bytes 1081352 | tf_op jit(solution)/shard_map/ppermute | solution.py:294
  28.1 2.0 %front.6 = (f32[176,640]{1,0:T(8,128)S(1)}, s16[192,640]{1,0:T(8,128)(2,1)S(1)}, f32[176,640]{1,0:T(8,128)S(1)}, bf16[176,2048]{1,0:T(8,128)(2,1)S(1)}) custom-call(bf16[88,2048]{1,0:T(8,128)(2,1)S(1)} %collective-permute-done.1.refs_0_, bf16[88,2048]{1,0:T(8,128)(2,1)S(1)} %collective-permute-done.2.refs_1_, f32[1,2048]{1,0:T(1,128)S(1)} %bitcast.25, ...), custom_call_target="tpu_custom_call" | custom-call | flops 1384120320 | bytes 1441792 | tf_op jit(solution)/shard_map/front/pallas_call | solution.py:89
  30.1 4.0 %collective-permute-done.8.code_ref = s16[192,640]{1,0:T(8,128)(2,1)S(1)} collective-permute-done((s16[192,640]{1,0:T(8,128)(2,1)S(1)}, s16[192,640]{1,0:T(8,128)(2,1)S(1)}, u32[]{:S(2)}, u32[]{:S(2)}) %collective-permute-start.8) | collective-permute-done | bytes 245792 | tf_op jit(solution)/shard_map/ppermute | solution.py:309
  34.1 2.1 %collective-permute-start.13 = (s16[192,640]{1,0:T(8,128)(2,1)S(1)}, s16[192,640]{1,0:T(8,128)(2,1)S(1)}, u32[]{:S(2)}, u32[]{:S(2)}) collective-permute-start(s16[192,640]{1,0:T(8,128)(2,1)S(1)} %get-tuple-element.108), channel_id=1, source_target_pairs={{0,1},{1,0},{2,3},{3,2},{4,5},{5,4},{6,7},{7,6},{8,9},{9,8},{10,11... | collective-permute-start | bytes 737288 | tf_op jit(solution)/shard_map/ppermute | solution.py:309
  37.1 2.7 %collective-permute-start.9 = (bf16[88,2048]{1,0:T(8,128)(2,1)S(1)}, bf16[88,2048]{1,0:T(8,128)(2,1)S(1)}, u32[]{:S(2)}, u32[]{:S(2)}) collective-permute-start(bf16[88,2048]{1,0:T(8,128)(2,1)S(1)} %collective-permute-done.4.refs_2_), channel_id=1, source_target_pairs={{0,64},{16,208},{64,128},{80,16},{128,192},{144,80},{192,0},{208,1... | collective-permute-start | bytes 1081352 | tf_op jit(solution)/shard_map/ppermute | solution.py:294
  40.1 3.7 %front.7 = (f32[352,640]{1,0:T(8,128)S(1)}, s16[368,640]{1,0:T(8,128)(2,1)S(1)}, f32[352,640]{1,0:T(8,128)S(1)}, bf16[352,2048]{1,0:T(8,128)(2,1)S(1)}) custom-call(bf16[88,2048]{1,0:T(8,128)(2,1)S(1)} %collective-permute-done.6.refs_0_, bf16[88,2048]{1,0:T(8,128)(2,1)S(1)} %collective-permute-done.7.refs_1_, ...), custom_call_target="tpu_custom_call" | custom-call | flops 2768240640 | bytes 2883584 | tf_op jit(solution)/shard_map/front/pallas_call | solution.py:89
  45.2 2.4 %collective-permute-done.9.refs_2_ = bf16[88,2048]{1,0:T(8,128)(2,1)S(1)} collective-permute-done((bf16[88,2048]{1,0:T(8,128)(2,1)S(1)}, bf16[88,2048]{1,0:T(8,128)(2,1)S(1)}, u32[]{:S(2)}, u32[]{:S(2)}) %collective-permute-start.9) | collective-permute-done | bytes 360480 | tf_op jit(solution)/shard_map/ppermute | solution.py:294
  49.1 2.7 %collective-permute-start.14 = (bf16[88,2048]{1,0:T(8,128)(2,1)S(1)}, bf16[88,2048]{1,0:T(8,128)(2,1)S(1)}, u32[]{:S(2)}, u32[]{:S(2)}) collective-permute-start(bf16[88,2048]{1,0:T(8,128)(2,1)S(1)} %collective-permute-done.9.refs_2_), channel_id=1, source_target_pairs={{0,64},{16,208},{64,128},{80,16},{128,192},{144,80},{192,0},{208,1... | collective-permute-start | bytes 1081352 | tf_op jit(solution)/shard_map/ppermute | solution.py:294
  52.9 3.7 %front.8 = (f32[352,640]{1,0:T(8,128)S(1)}, s16[368,640]{1,0:T(8,128)(2,1)S(1)}, f32[352,640]{1,0:T(8,128)S(1)}, bf16[352,2048]{1,0:T(8,128)(2,1)S(1)}) custom-call(bf16[88,2048]{1,0:T(8,128)(2,1)S(1)} %collective-permute-done.11.refs_0_, bf16[88,2048]{1,0:T(8,128)(2,1)S(1)} %collective-permute-done.12.refs_1_, ...), custom_call_target="tpu_custom_call" | custom-call | flops 2768240640 | bytes 2883584 | tf_op jit(solution)/shard_map/front/pallas_call | solution.py:89
  59.6 3.7 %front.9 = (f32[352,640]{1,0:T(8,128)S(1)}, s16[368,640]{1,0:T(8,128)(2,1)S(1)}, f32[352,640]{1,0:T(8,128)S(1)}, bf16[352,2048]{1,0:T(8,128)(2,1)S(1)}) custom-call(bf16[88,2048]{1,0:T(8,128)(2,1)S(1)} %collective-permute-done.15.refs_0_, bf16[88,2048]{1,0:T(8,128)(2,1)S(1)} %collective-permute-done.16.refs_1_, ...), custom_call_target="tpu_custom_call" | custom-call | flops 2768240640 | bytes 2883584 | tf_op jit(solution)/shard_map/front/pallas_call | solution.py:89
  64.8 5.9 %collective-permute-done.19.code_ref = s16[368,640]{1,0:T(8,128)(2,1)S(1)} collective-permute-done((s16[368,640]{1,0:T(8,128)(2,1)S(1)}, s16[368,640]{1,0:T(8,128)(2,1)S(1)}, u32[]{:S(2)}, u32[]{:S(2)}) %collective-permute-start.19) | collective-permute-done | bytes 471072 | tf_op jit(solution)/shard_map/ppermute | solution.py:309
  71.9 8.9 %collective-permute-done.20.code_ref = s16[368,640]{1,0:T(8,128)(2,1)S(1)} collective-permute-done((s16[368,640]{1,0:T(8,128)(2,1)S(1)}, s16[368,640]{1,0:T(8,128)(2,1)S(1)}, u32[]{:S(2)}, u32[]{:S(2)}) %collective-permute-start.20) | collective-permute-done | bytes 471072 | tf_op jit(solution)/shard_map/ppermute | solution.py:309
  82.1 16.2 %all_to_all.20.parts_ref = f32[8,4,1408]{2,1,0:T(4,128)S(1)} all-to-all(f32[8,4,1408]{2,1,0:T(4,128)S(1)} %copies.1), channel_id=1, replica_groups=mesh['x'=4,'yh'=2,'c'=2,'z'=8,'t'=2] {'z'}, dimensions={0} | all-to-all | bytes 360448 | tf_op jit(solution)/shard_map/all_to_all | solution.py:396
  99.1 2.8 %collective-permute-start.21 = (f32[4,1408]{1,0:T(4,128)S(1)}, f32[4,1408]{1,0:T(4,128)S(1)}, u32[]{:S(2)}, u32[]{:S(2)}) collective-permute-start(f32[4,1408]{1,0:T(4,128)S(1)} %first_merge.1.one_ref), channel_id=1, source_target_pairs={{0,16},{16,0},{1,17},{17,1},{2,18},{18,2},{3,19},{19,3},{4,20},{20... | collective-permute-start | bytes 67592 | tf_op jit(solution)/shard_map/ppermute | solution.py:309
  102.7 13.8 %all_to_all.21.parts_ref = f32[16,4,1408]{2,1,0:T(4,128)S(1)} all-to-all(f32[16,4,1408]{2,1,0:T(4,128)S(1)} %pair_merge.1), channel_id=1, replica_groups=mesh['x'=4,'yh'=2,'c'=2,'z'=8,'t'=2] {'x','yh','t'}, dimensions={0} | all-to-all | bytes 720896 | tf_op jit(solution)/shard_map/all_to_all | solution.py:406
  116.7 9.3 %product.1 = (f32[2048,640]{1,0:T(8,128)}, f32[1,2048]{1,0:T(1,128)S(1)}) custom-call(s32[16]{0:T(128)S(1)} %stack.67.place_ref.refs_0_, f32[16,128]{1,0:T(8,128)S(1)} %pad.4.ids_ref.refs_1_, f32[16,4,128]{2,1,0:T(4,128)S(1)} %last_merge.1.refs_2_, f32[176,640]{1,0:T(8,128)S(1)} %get-tuple-element.167.refs_3_, f32[176,640]{1,0:T(8,128)S(1)} %get-tuple-element.168.refs_4_, ...), custom_call_target="tpu_custom_call" | custom-call | flops 3690987520 | bytes 5242880 | tf_op jit(solution)/shard_map/product/pallas_call | solution.py:254
  126.0 12.7 %all_to_all.22 = f32[16,1,2048]{2,1,0:T(1,128)S(1)} all-to-all(f32[16,1,2048]{2,1,0:T(1,128)S(1)} %broadcast_in_dim.24), channel_id=1, replica_groups=mesh['x'=4,'yh'=2,'c'=2,'z'=8,'t'=2] {'x','yh','c'}, dimensions={0} | all-to-all | bytes 262144 | tf_op jit(solution)/shard_map/all_to_all | solution.py:286
  138.9 9.5 %all_to_all.23 = f32[8,1,2048]{2,1,0:T(1,128)S(1)} all-to-all(f32[8,1,2048]{2,1,0:T(1,128)S(1)} %broadcast_in_dim.25), channel_id=1, replica_groups=mesh['x'=4,'yh'=2,'c'=2,'z'=8,'t'=2] {'z'}, dimensions={0} | all-to-all | bytes 131072 | tf_op jit(solution)/shard_map/all_to_all | solution.py:286
  (60 shorter events, 22.4 us)
Async XLA Ops:
  7.3 12.5 %copy-start.2 = (f32[2048]{0:T(1024)S(1)}, f32[2048]{0:T(1024)}, u32[]{:S(2)}) copy-start(f32[2048]{0:T(1024)} %param.8) | copy-start | bytes 24580
  7.3 12.5 %copy-start.3 = (f32[2048]{0:T(1024)S(1)}, f32[2048]{0:T(1024)}, u32[]{:S(2)}) copy-start(f32[2048]{0:T(1024)} %param.7) | copy-start | bytes 24580
  8.4 11.4 %collective-permute-start.3 = (bf16[88,2048]{1,0:T(8,128)(2,1)S(1)}, bf16[88,2048]{1,0:T(8,128)(2,1)S(1)}, u32[]{:S(2)}, u32[]{:S(2)}) collective-permute-start(bf16[88,2048]{1,0:T(8,128)(2,1)S(1)} %fusion.1.refs_0_), channel_id=1, source_target_pairs={{0,16},{16,0},{1,17},{17,1},{2,18},{18,2},{3,19},{19,3},{4,20},{20... | collective-permute-start | bytes 1081352 | tf_op jit(solution)/shard_map/ppermute | solution.py:309
  12.2 10.0 %collective-permute-start.2 = (bf16[88,2048]{1,0:T(8,128)(2,1)S(1)}, bf16[88,2048]{1,0:T(8,128)(2,1)S(1)}, u32[]{:S(2)}, u32[]{:S(2)}) collective-permute-start(bf16[88,2048]{1,0:T(8,128)(2,1)S(1)} %fusion.1.refs_0_), channel_id=1, source_target_pairs={{0,192},{16,80},{64,0},{80,144},{128,64},{144,208},{192,128},{208,... | collective-permute-start | bytes 1081352 | tf_op jit(solution)/shard_map/ppermute | solution.py:294
  12.2 10.0 %collective-permute-start.1 = (bf16[88,2048]{1,0:T(8,128)(2,1)S(1)}, bf16[88,2048]{1,0:T(8,128)(2,1)S(1)}, u32[]{:S(2)}, u32[]{:S(2)}) collective-permute-start(bf16[88,2048]{1,0:T(8,128)(2,1)S(1)} %fusion.1.refs_0_), channel_id=1, source_target_pairs={{0,64},{16,208},{64,128},{80,16},{128,192},{144,80},{192,0},{208,1... | collective-permute-start | bytes 1081352 | tf_op jit(solution)/shard_map/ppermute | solution.py:294
  14.9 7.3 %collective-permute-start = (bf16[88,2048]{1,0:T(8,128)(2,1)S(1)}, bf16[88,2048]{1,0:T(8,128)(2,1)S(1)}, u32[]{:S(2)}, u32[]{:S(2)}) collective-permute-start(bf16[88,2048]{1,0:T(8,128)(2,1)S(1)} %fusion.1.refs_0_), channel_id=1, source_target_pairs={{0,1},{16,49},{1,32},{17,16},{32,33},{48,17},{33,0},{49,48},{2,3},... | collective-permute-start | bytes 1081352 | tf_op jit(solution)/shard_map/ppermute | solution.py:305
  22.3 13.9 %collective-permute-start.4 = (bf16[88,2048]{1,0:T(8,128)(2,1)S(1)}, bf16[88,2048]{1,0:T(8,128)(2,1)S(1)}, u32[]{:S(2)}, u32[]{:S(2)}) collective-permute-start(bf16[88,2048]{1,0:T(8,128)(2,1)S(1)} %collective-permute-done), channel_id=1, source_target_pairs={{0,1},{16,49},{1,32},{17,16},{32,33},{48,17},{33,0},{49,48},{2,3},... | collective-permute-start | bytes 1081352 | tf_op jit(solution)/shard_map/ppermute | solution.py:305
  24.2 11.9 %collective-permute-start.7 = (bf16[88,2048]{1,0:T(8,128)(2,1)S(1)}, bf16[88,2048]{1,0:T(8,128)(2,1)S(1)}, u32[]{:S(2)}, u32[]{:S(2)}) collective-permute-start(bf16[88,2048]{1,0:T(8,128)(2,1)S(1)} %collective-permute-done.2.refs_1_), channel_id=1, source_target_pairs={{0,16},{16,0},{1,17},{17,1},{2,18},{18,2},{3,19},{19,3},{4,20},{20... | collective-permute-start | bytes 1081352 | tf_op jit(solution)/shard_map/ppermute | solution.py:309
  24.3 11.9 %collective-permute-start.6 = (bf16[88,2048]{1,0:T(8,128)(2,1)S(1)}, bf16[88,2048]{1,0:T(8,128)(2,1)S(1)}, u32[]{:S(2)}, u32[]{:S(2)}) collective-permute-start(bf16[88,2048]{1,0:T(8,128)(2,1)S(1)} %collective-permute-done.1.refs_0_), channel_id=1, source_target_pairs={{0,16},{16,0},{1,17},{17,1},{2,18},{18,2},{3,19},{19,3},{4,20},{20... | collective-permute-start | bytes 1081352 | tf_op jit(solution)/shard_map/ppermute | solution.py:309
  24.7 11.4 %collective-permute-start.5 = (bf16[88,2048]{1,0:T(8,128)(2,1)S(1)}, bf16[88,2048]{1,0:T(8,128)(2,1)S(1)}, u32[]{:S(2)}, u32[]{:S(2)}) collective-permute-start(bf16[88,2048]{1,0:T(8,128)(2,1)S(1)} %collective-permute-done.1.refs_0_), channel_id=1, source_target_pairs={{0,64},{16,208},{64,128},{80,16},{128,192},{144,80},{192,0},{208,1... | collective-permute-start | bytes 1081352 | tf_op jit(solution)/shard_map/ppermute | solution.py:294
  27.8 6.3 %collective-permute-start.8 = (s16[192,640]{1,0:T(8,128)(2,1)S(1)}, s16[192,640]{1,0:T(8,128)(2,1)S(1)}, u32[]{:S(2)}, u32[]{:S(2)}) collective-permute-start(s16[192,640]{1,0:T(8,128)(2,1)S(1)} %get-tuple-element.101), channel_id=1, source_target_pairs={{0,1},{1,0},{2,3},{3,2},{4,5},{5,4},{6,7},{7,6},{8,9},{9,8},{10,11... | collective-permute-start | bytes 737288 | tf_op jit(solution)/shard_map/ppermute | solution.py:309
  34.1 9.8 %collective-permute-start.13 = (s16[192,640]{1,0:T(8,128)(2,1)S(1)}, s16[192,640]{1,0:T(8,128)(2,1)S(1)}, u32[]{:S(2)}, u32[]{:S(2)}) collective-permute-start(s16[192,640]{1,0:T(8,128)(2,1)S(1)} %get-tuple-element.108), channel_id=1, source_target_pairs={{0,1},{1,0},{2,3},{3,2},{4,5},{5,4},{6,7},{7,6},{8,9},{9,8},{10,11... | collective-permute-start | bytes 737288 | tf_op jit(solution)/shard_map/ppermute | solution.py:309
  36.2 8.9 %collective-permute-start.11 = (bf16[88,2048]{1,0:T(8,128)(2,1)S(1)}, bf16[88,2048]{1,0:T(8,128)(2,1)S(1)}, u32[]{:S(2)}, u32[]{:S(2)}) collective-permute-start(bf16[88,2048]{1,0:T(8,128)(2,1)S(1)} %collective-permute-done.4.refs_2_), channel_id=1, source_target_pairs={{0,16},{16,0},{1,17},{17,1},{2,18},{18,2},{3,19},{19,3},{4,20},{20... | collective-permute-start | bytes 1081352 | tf_op jit(solution)/shard_map/ppermute | solution.py:309
  37.1 8.1 %collective-permute-start.10 = (bf16[88,2048]{1,0:T(8,128)(2,1)S(1)}, bf16[88,2048]{1,0:T(8,128)(2,1)S(1)}, u32[]{:S(2)}, u32[]{:S(2)}) collective-permute-start(bf16[88,2048]{1,0:T(8,128)(2,1)S(1)} %collective-permute-done.4.refs_2_), channel_id=1, source_target_pairs={{0,192},{16,80},{64,0},{80,144},{128,64},{144,208},{192,128},{208,... | collective-permute-start | bytes 1081352 | tf_op jit(solution)/shard_map/ppermute | solution.py:294
  37.1 10.4 %collective-permute-start.9 = (bf16[88,2048]{1,0:T(8,128)(2,1)S(1)}, bf16[88,2048]{1,0:T(8,128)(2,1)S(1)}, u32[]{:S(2)}, u32[]{:S(2)}) collective-permute-start(bf16[88,2048]{1,0:T(8,128)(2,1)S(1)} %collective-permute-done.4.refs_2_), channel_id=1, source_target_pairs={{0,64},{16,208},{64,128},{80,16},{128,192},{144,80},{192,0},{208,1... | collective-permute-start | bytes 1081352 | tf_op jit(solution)/shard_map/ppermute | solution.py:294
  39.8 5.3 %collective-permute-start.12 = (bf16[88,2048]{1,0:T(8,128)(2,1)S(1)}, bf16[88,2048]{1,0:T(8,128)(2,1)S(1)}, u32[]{:S(2)}, u32[]{:S(2)}) collective-permute-start(bf16[88,2048]{1,0:T(8,128)(2,1)S(1)} %collective-permute-done.5.refs_3_), channel_id=1, source_target_pairs={{0,16},{16,0},{1,17},{17,1},{2,18},{18,2},{3,19},{19,3},{4,20},{20... | collective-permute-start | bytes 1081352 | tf_op jit(solution)/shard_map/ppermute | solution.py:309
  43.9 12.7 %collective-permute-start.17 = (s16[368,640]{1,0:T(8,128)(2,1)S(1)}, s16[368,640]{1,0:T(8,128)(2,1)S(1)}, u32[]{:S(2)}, u32[]{:S(2)}) collective-permute-start(s16[368,640]{1,0:T(8,128)(2,1)S(1)} %get-tuple-element.116), channel_id=1, source_target_pairs={{0,1},{1,0},{2,3},{3,2},{4,5},{5,4},{6,7},{7,6},{8,9},{9,8},{10,11... | collective-permute-start | bytes 1413128 | tf_op jit(solution)/shard_map/ppermute | solution.py:309
  47.5 9.1 %collective-permute-start.16 = (bf16[88,2048]{1,0:T(8,128)(2,1)S(1)}, bf16[88,2048]{1,0:T(8,128)(2,1)S(1)}, u32[]{:S(2)}, u32[]{:S(2)}) collective-permute-start(bf16[88,2048]{1,0:T(8,128)(2,1)S(1)} %collective-permute-done.10.refs_3_), channel_id=1, source_target_pairs={{0,16},{16,0},{1,17},{17,1},{2,18},{18,2},{3,19},{19,3},{4,20},{20... | collective-permute-start | bytes 1081352 | tf_op jit(solution)/shard_map/ppermute | solution.py:309
  49.1 7.5 %collective-permute-start.15 = (bf16[88,2048]{1,0:T(8,128)(2,1)S(1)}, bf16[88,2048]{1,0:T(8,128)(2,1)S(1)}, u32[]{:S(2)}, u32[]{:S(2)}) collective-permute-start(bf16[88,2048]{1,0:T(8,128)(2,1)S(1)} %collective-permute-done.9.refs_2_), channel_id=1, source_target_pairs={{0,16},{16,0},{1,17},{17,1},{2,18},{18,2},{3,19},{19,3},{4,20},{20... | collective-permute-start | bytes 1081352 | tf_op jit(solution)/shard_map/ppermute | solution.py:309
  49.1 7.5 %collective-permute-start.14 = (bf16[88,2048]{1,0:T(8,128)(2,1)S(1)}, bf16[88,2048]{1,0:T(8,128)(2,1)S(1)}, u32[]{:S(2)}, u32[]{:S(2)}) collective-permute-start(bf16[88,2048]{1,0:T(8,128)(2,1)S(1)} %collective-permute-done.9.refs_2_), channel_id=1, source_target_pairs={{0,64},{16,208},{64,128},{80,16},{128,192},{144,80},{192,0},{208,1... | collective-permute-start | bytes 1081352 | tf_op jit(solution)/shard_map/ppermute | solution.py:294
  56.7 2.9 %collective-permute-start.18 = (bf16[88,2048]{1,0:T(8,128)(2,1)S(1)}, bf16[88,2048]{1,0:T(8,128)(2,1)S(1)}, u32[]{:S(2)}, u32[]{:S(2)}) collective-permute-start(bf16[88,2048]{1,0:T(8,128)(2,1)S(1)} %collective-permute-done.14.refs_2_), channel_id=1, source_target_pairs={{0,16},{16,0},{1,17},{17,1},{2,18},{18,2},{3,19},{19,3},{4,20},{20... | collective-permute-start | bytes 1081352 | tf_op jit(solution)/shard_map/ppermute | solution.py:309
  58.3 12.4 %collective-permute-start.19 = (s16[368,640]{1,0:T(8,128)(2,1)S(1)}, s16[368,640]{1,0:T(8,128)(2,1)S(1)}, u32[]{:S(2)}, u32[]{:S(2)}) collective-permute-start(s16[368,640]{1,0:T(8,128)(2,1)S(1)} %get-tuple-element.131), channel_id=1, source_target_pairs={{0,1},{1,0},{2,3},{3,2},{4,5},{5,4},{6,7},{7,6},{8,9},{9,8},{10,11... | collective-permute-start | bytes 1413128 | tf_op jit(solution)/shard_map/ppermute | solution.py:309
  63.3 17.5 %collective-permute-start.20 = (s16[368,640]{1,0:T(8,128)(2,1)S(1)}, s16[368,640]{1,0:T(8,128)(2,1)S(1)}, u32[]{:S(2)}, u32[]{:S(2)}) collective-permute-start(s16[368,640]{1,0:T(8,128)(2,1)S(1)} %get-tuple-element.154), channel_id=1, source_target_pairs={{0,1},{1,0},{2,3},{3,2},{4,5},{5,4},{6,7},{7,6},{8,9},{9,8},{10,11... | collective-permute-start | bytes 1413128 | tf_op jit(solution)/shard_map/ppermute | solution.py:309
  99.1 3.6 %collective-permute-start.21 = (f32[4,1408]{1,0:T(4,128)S(1)}, f32[4,1408]{1,0:T(4,128)S(1)}, u32[]{:S(2)}, u32[]{:S(2)}) collective-permute-start(f32[4,1408]{1,0:T(4,128)S(1)} %first_merge.1.one_ref), channel_id=1, source_target_pairs={{0,16},{16,0},{1,17},{17,1},{2,18},{18,2},{3,19},{19,3},{4,20},{20... | collective-permute-start | bytes 67592 | tf_op jit(solution)/shard_map/ppermute | solution.py:309
  (2 other events, 3.5 us)

commit v6 on v5

--- a/solution.py
+++ b/solution.py
@@ -354,23 +354,23 @@
     one2, two2 = swap(one, "c"), swap(two, "c")
     made1 = chunk_front(one, two)
     code1 = swap(made1[1], "t")
-    across, far, one2, two2, made1, code0 = together(across, far, one2, two2, made1, code0)
+    across, far, one2, two2, made1 = together(across, far, one2, two2, made1)
 
     y_one, y_two = along_x(across, 1), along_x(across, -1)
+    made2 = chunk_front(one2, two2, across, far)
+    code2 = swap(made2[1], "t")
+    across, far, made2, code0, code1 = together(across, far, made2, code0, code1)
     across2, far2 = swap(across, "c"), swap(far, "c")
     expo0 = chunk_expo(0, made0, code0)
-    made2 = chunk_front(one2, two2, across, far)
-    code2 = swap(made2[1], "t")
-    y_one, y_two, across2, far2, made2, expo0, code1 = together(
-        y_one, y_two, across2, far2, made2, expo0, code1
-    )
+    y_one, y_two, across2, far2, expo0 = together(y_one, y_two, across2, far2, expo0)
 
     y_far = along_x(y_one, 1)
+    made3 = chunk_front(across2, far2, y_one, y_two)
+    code3 = swap(made3[1], "t")
+    y_one, y_two, made3 = together(y_one, y_two, made3)
     y_one2, y_two2 = swap(y_one, "c"), swap(y_two, "c")
     expo1 = chunk_expo(1, made1, code1)
-    made3 = chunk_front(across2, far2, y_one, y_two)
-    code3 = swap(made3[1], "t")
-    y_far, y_one2, y_two2, made3, expo1, code2 = together(y_far, y_one2, y_two2, made3, expo1, code2)
+    y_far, y_one2, y_two2, expo1, code2 = together(y_far, y_one2, y_two2, expo1, code2)
 
     y_far2 = swap(y_far, "c")
     expo2 = chunk_expo(2, made2, code2)

time: 149 us -> 147 us (0.987)
  waiting for transfers between devices: 22.6 us -> 18.8 us
    ppermute x14, waiting for transfers between devices: 19.7 us -> 17.5 us  [swap(): return lax.ppermute(x, (axis,), [(0, 1), (1, 0)])]
    ppermute x6, waiting for transfers between devices: 2.92 us -> 1.25 us  [along_x(): return lax.ppermute(x, ('x', 'c'), pairs)]
  transfers between devices with their start and end apart: 22 -> 22, of which waited for: 8 -> 8; matrix products, arithmetic and copies ran while one was open for 0% -> 0% of each run, Pallas kernels for 13% -> 14%
where the time goes in v6:
time: 147 us; the launch traced here: 146 us
  blocking collectives  57.6 us (39%)
  Pallas kernels  31.6 us (21%)
  starting transfers between devices  29.9 us (20%)
  waiting for transfers between devices  18.8 us (13%)
  local copies, waits for them, and re-layouts  3.77 us (3%)
  other arithmetic  3.75 us (3%)
    all_to_all x2, blocking collectives, everyone(): return lax.all_to_all(copies, axes, 0, 0, tiled=True)  22.2 us
    ppermute x14, waiting for transfers between devices, swap(): return lax.ppermute(x, (axis,), [(0, 1), (1, 0)])  17.5 us
    all_to_all x1, blocking collectives, local(): lax.all_to_all(own, 'z', 0, 0, tiled=True)  16 us
    pallas_call x5, Pallas kernels, front(): pl.pallas_call(functools.partial(front_kernel, pieces=len(pieces), rows=r...  15.2 us
    ppermute x14, starting transfers between devices, swap(): return lax.ppermute(x, (axis,), [(0, 1), (1, 0)])  15 us
    all_to_all x1, blocking collectives, local(): lax.all_to_all(on_chip, rest, 0, 0, tiled=True)  15 us
    ppermute x6, starting transfers between devices, along_x(): return lax.ppermute(x, ('x', 'c'), pairs)  11.8 us
    pallas_call x1, Pallas kernels, finish(): pl.pallas_call(functools.partial(product_kernel, chunks=chunks, size=size...  9.24 us
  transfers between devices with their start and end apart: 22, of which 8 were waited for; matrix products, arithmetic and copies ran while one was open for 0% of the time, Pallas kernels for 14%

profile of v6, /device:TPU:1, one launch (start us, length us, event | category | flops | bytes accessed | tf_op | source)
XLA Modules:
  0.0 146.3 jit_solution(4337773013175844283)
XLA Ops:
  2.8 4.4 %psum.7 = f32[88]{0:T(128)S(1)} all-reduce(f32[88]{0:T(128)S(1)} %fusion), channel_id=1, replica_groups=mesh['x'=4,'yh'=2,'c'=2,'z'=8,'t'=2] {'t'}, use_global_device_ids=true, to_apply=%region_1.2 | all-reduce | flops 88 | bytes 704 | tf_op jit(solution)/shard_map/psum | solution.py:335
  8.4 3.8 %collective-permute-start.3 = (bf16[88,2048]{1,0:T(8,128)(2,1)S(1)}, bf16[88,2048]{1,0:T(8,128)(2,1)S(1)}, u32[]{:S(2)}, u32[]{:S(2)}) collective-permute-start(bf16[88,2048]{1,0:T(8,128)(2,1)S(1)} %fusion.1.refs_0_), channel_id=1, source_target_pairs={{0,16},{16,0},{1,17},{17,1},{2,18},{18,2},{3,19},{19,3},{4,20},{20... | collective-permute-start | bytes 1081352 | tf_op jit(solution)/shard_map/ppermute | solution.py:309
  12.2 2.7 %collective-permute-start.1 = (bf16[88,2048]{1,0:T(8,128)(2,1)S(1)}, bf16[88,2048]{1,0:T(8,128)(2,1)S(1)}, u32[]{:S(2)}, u32[]{:S(2)}) collective-permute-start(bf16[88,2048]{1,0:T(8,128)(2,1)S(1)} %fusion.1.refs_0_), channel_id=1, source_target_pairs={{0,64},{16,208},{64,128},{80,16},{128,192},{144,80},{192,0},{208,1... | collective-permute-start | bytes 1081352 | tf_op jit(solution)/shard_map/ppermute | solution.py:294
  15.9 1.7 %copy-done = bf16[2048,640]{1,0:T(8,128)(2,1)S(1)} copy-done((bf16[2048,640]{1,0:T(8,128)(2,1)S(1)}, bf16[2048,640]{1,0:T(8,128)(2,1)}, u32[]{:S(2)}) %copy-start) | copy-done | bytes 2621464
  17.7 1.7 %copy-done.1 = bf16[2048,640]{1,0:T(8,128)(2,1)S(1)} copy-done((bf16[2048,640]{1,0:T(8,128)(2,1)S(1)}, bf16[2048,640]{1,0:T(8,128)(2,1)}, u32[]{:S(2)}) %copy-start.1) | copy-done | bytes 2621464
  19.8 2.0 %front.5 = (f32[176,640]{1,0:T(8,128)S(1)}, s16[192,640]{1,0:T(8,128)(2,1)S(1)}, f32[176,640]{1,0:T(8,128)S(1)}, bf16[176,2048]{1,0:T(8,128)(2,1)S(1)}) custom-call(bf16[88,2048]{1,0:T(8,128)(2,1)S(1)} %fusion.1.refs_0_, bf16[88,2048]{1,0:T(8,128)(2,1)S(1)} %collective-permute-done.3.refs_1_, f32[1,2048]{1,0:T(1,128)S(1)} %bitcast.24, ...), custom_call_target="tpu_custom_call" | custom-call | flops 1384120320 | bytes 1441792 | tf_op jit(solution)/shard_map/front/pallas_call | solution.py:89
  22.3 2.0 %collective-permute-start.4 = (bf16[88,2048]{1,0:T(8,128)(2,1)S(1)}, bf16[88,2048]{1,0:T(8,128)(2,1)S(1)}, u32[]{:S(2)}, u32[]{:S(2)}) collective-permute-start(bf16[88,2048]{1,0:T(8,128)(2,1)S(1)} %collective-permute-done), channel_id=1, source_target_pairs={{0,1},{16,49},{1,32},{17,16},{32,33},{48,17},{33,0},{49,48},{2,3},... | collective-permute-start | bytes 1081352 | tf_op jit(solution)/shard_map/ppermute | solution.py:305
  24.7 3.1 %collective-permute-start.5 = (bf16[88,2048]{1,0:T(8,128)(2,1)S(1)}, bf16[88,2048]{1,0:T(8,128)(2,1)S(1)}, u32[]{:S(2)}, u32[]{:S(2)}) collective-permute-start(bf16[88,2048]{1,0:T(8,128)(2,1)S(1)} %collective-permute-done.1.refs_0_), channel_id=1, source_target_pairs={{0,64},{16,208},{64,128},{80,16},{128,192},{144,80},{192,0},{208,1... | collective-permute-start | bytes 1081352 | tf_op jit(solution)/shard_map/ppermute | solution.py:294
  28.1 2.0 %front.6 = (f32[176,640]{1,0:T(8,128)S(1)}, s16[192,640]{1,0:T(8,128)(2,1)S(1)}, f32[176,640]{1,0:T(8,128)S(1)}, bf16[176,2048]{1,0:T(8,128)(2,1)S(1)}) custom-call(bf16[88,2048]{1,0:T(8,128)(2,1)S(1)} %collective-permute-done.1.refs_0_, bf16[88,2048]{1,0:T(8,128)(2,1)S(1)} %collective-permute-done.2.refs_1_, f32[1,2048]{1,0:T(1,128)S(1)} %bitcast.25, ...), custom_call_target="tpu_custom_call" | custom-call | flops 1384120320 | bytes 1441792 | tf_op jit(solution)/shard_map/front/pallas_call | solution.py:89
  32.2 3.1 %collective-permute-start.8 = (bf16[88,2048]{1,0:T(8,128)(2,1)S(1)}, bf16[88,2048]{1,0:T(8,128)(2,1)S(1)}, u32[]{:S(2)}, u32[]{:S(2)}) collective-permute-start(bf16[88,2048]{1,0:T(8,128)(2,1)S(1)} %collective-permute-done.4.refs_2_), channel_id=1, source_target_pairs={{0,64},{16,208},{64,128},{80,16},{128,192},{144,80},{192,0},{208,1... | collective-permute-start | bytes 1081352 | tf_op jit(solution)/shard_map/ppermute | solution.py:294
  35.3 3.7 %front.7 = (f32[352,640]{1,0:T(8,128)S(1)}, s16[368,640]{1,0:T(8,128)(2,1)S(1)}, f32[352,640]{1,0:T(8,128)S(1)}, bf16[352,2048]{1,0:T(8,128)(2,1)S(1)}) custom-call(bf16[88,2048]{1,0:T(8,128)(2,1)S(1)} %collective-permute-done.6.refs_0_, bf16[88,2048]{1,0:T(8,128)(2,1)S(1)} %collective-permute-done.7.refs_1_, ...), custom_call_target="tpu_custom_call" | custom-call | flops 2768240640 | bytes 2883584 | tf_op jit(solution)/shard_map/front/pallas_call | solution.py:89
  39.2 2.2 %collective-permute-start.12 = (bf16[88,2048]{1,0:T(8,128)(2,1)S(1)}, bf16[88,2048]{1,0:T(8,128)(2,1)S(1)}, u32[]{:S(2)}, u32[]{:S(2)}) collective-permute-start(bf16[88,2048]{1,0:T(8,128)(2,1)S(1)} %collective-permute-done.4.refs_2_), channel_id=1, source_target_pairs={{0,16},{16,0},{1,17},{17,1},{2,18},{18,2},{3,19},{19,3},{4,20},{20... | collective-permute-start | bytes 1081352 | tf_op jit(solution)/shard_map/ppermute | solution.py:309
  43.3 3.0 %collective-permute-start.14 = (bf16[88,2048]{1,0:T(8,128)(2,1)S(1)}, bf16[88,2048]{1,0:T(8,128)(2,1)S(1)}, u32[]{:S(2)}, u32[]{:S(2)}) collective-permute-start(bf16[88,2048]{1,0:T(8,128)(2,1)S(1)} %collective-permute-done.8.refs_2_), channel_id=1, source_target_pairs={{0,64},{16,208},{64,128},{80,16},{128,192},{144,80},{192,0},{208,1... | collective-permute-start | bytes 1081352 | tf_op jit(solution)/shard_map/ppermute | solution.py:294
  46.2 3.7 %front.8 = (f32[352,640]{1,0:T(8,128)S(1)}, s16[368,640]{1,0:T(8,128)(2,1)S(1)}, f32[352,640]{1,0:T(8,128)S(1)}, bf16[352,2048]{1,0:T(8,128)(2,1)S(1)}) custom-call(bf16[88,2048]{1,0:T(8,128)(2,1)S(1)} %collective-permute-done.12.refs_0_, bf16[88,2048]{1,0:T(8,128)(2,1)S(1)} %collective-permute-done.13.refs_1_, ...), custom_call_target="tpu_custom_call" | custom-call | flops 2768240640 | bytes 2883584 | tf_op jit(solution)/shard_map/front/pallas_call | solution.py:89
  51.6 1.9 %collective-permute-done.17.code_ref = s16[368,640]{1,0:T(8,128)(2,1)S(1)} collective-permute-done((s16[368,640]{1,0:T(8,128)(2,1)S(1)}, s16[368,640]{1,0:T(8,128)(2,1)S(1)}, u32[]{:S(2)}, u32[]{:S(2)}) %collective-permute-start.17) | collective-permute-done | bytes 471072 | tf_op jit(solution)/shard_map/ppermute | solution.py:309
  56.5 3.7 %front.9 = (f32[352,640]{1,0:T(8,128)S(1)}, s16[368,640]{1,0:T(8,128)(2,1)S(1)}, f32[352,640]{1,0:T(8,128)S(1)}, bf16[352,2048]{1,0:T(8,128)(2,1)S(1)}) custom-call(bf16[88,2048]{1,0:T(8,128)(2,1)S(1)} %collective-permute-done.15.refs_0_, bf16[88,2048]{1,0:T(8,128)(2,1)S(1)} %collective-permute-done.16.refs_1_, ...), custom_call_target="tpu_custom_call" | custom-call | flops 2768240640 | bytes 2883584 | tf_op jit(solution)/shard_map/front/pallas_call | solution.py:89
  61.5 5.5 %collective-permute-done.19.code_ref = s16[368,640]{1,0:T(8,128)(2,1)S(1)} collective-permute-done((s16[368,640]{1,0:T(8,128)(2,1)S(1)}, s16[368,640]{1,0:T(8,128)(2,1)S(1)}, u32[]{:S(2)}, u32[]{:S(2)}) %collective-permute-start.19) | collective-permute-done | bytes 471072 | tf_op jit(solution)/shard_map/ppermute | solution.py:309
  68.2 8.8 %collective-permute-done.20.code_ref = s16[368,640]{1,0:T(8,128)(2,1)S(1)} collective-permute-done((s16[368,640]{1,0:T(8,128)(2,1)S(1)}, s16[368,640]{1,0:T(8,128)(2,1)S(1)}, u32[]{:S(2)}, u32[]{:S(2)}) %collective-permute-start.20) | collective-permute-done | bytes 471072 | tf_op jit(solution)/shard_map/ppermute | solution.py:309
  78.4 16.0 %all_to_all.20.parts_ref = f32[8,4,1408]{2,1,0:T(4,128)S(1)} all-to-all(f32[8,4,1408]{2,1,0:T(4,128)S(1)} %copies.1), channel_id=1, replica_groups=mesh['x'=4,'yh'=2,'c'=2,'z'=8,'t'=2] {'z'}, dimensions={0} | all-to-all | bytes 360448 | tf_op jit(solution)/shard_map/all_to_all | solution.py:396
  95.2 2.8 %collective-permute-start.21 = (f32[4,1408]{1,0:T(4,128)S(1)}, f32[4,1408]{1,0:T(4,128)S(1)}, u32[]{:S(2)}, u32[]{:S(2)}) collective-permute-start(f32[4,1408]{1,0:T(4,128)S(1)} %first_merge.1.one_ref), channel_id=1, source_target_pairs={{0,16},{16,0},{1,17},{17,1},{2,18},{18,2},{3,19},{19,3},{4,20},{20... | collective-permute-start | bytes 67592 | tf_op jit(solution)/shard_map/ppermute | solution.py:309
  98.9 15.0 %all_to_all.21.parts_ref = f32[16,4,1408]{2,1,0:T(4,128)S(1)} all-to-all(f32[16,4,1408]{2,1,0:T(4,128)S(1)} %pair_merge.1), channel_id=1, replica_groups=mesh['x'=4,'yh'=2,'c'=2,'z'=8,'t'=2] {'x','yh','t'}, dimensions={0} | all-to-all | bytes 720896 | tf_op jit(solution)/shard_map/all_to_all | solution.py:406
  114.1 9.2 %product.1 = (f32[2048,640]{1,0:T(8,128)}, f32[1,2048]{1,0:T(1,128)S(1)}) custom-call(s32[16]{0:T(128)S(1)} %stack.67.place_ref.refs_0_, f32[16,128]{1,0:T(8,128)S(1)} %pad.4.ids_ref.refs_1_, f32[16,4,128]{2,1,0:T(4,128)S(1)} %last_merge.1.refs_2_, f32[176,640]{1,0:T(8,128)S(1)} %get-tuple-element.175.refs_3_, f32[176,640]{1,0:T(8,128)S(1)} %get-tuple-element.176.refs_4_, ...), custom_call_target="tpu_custom_call" | custom-call | flops 3690987520 | bytes 5242880 | tf_op jit(solution)/shard_map/product/pallas_call | solution.py:254
  123.4 12.7 %all_to_all.22 = f32[16,1,2048]{2,1,0:T(1,128)S(1)} all-to-all(f32[16,1,2048]{2,1,0:T(1,128)S(1)} %broadcast_in_dim.24), channel_id=1, replica_groups=mesh['x'=4,'yh'=2,'c'=2,'z'=8,'t'=2] {'x','yh','c'}, dimensions={0} | all-to-all | bytes 262144 | tf_op jit(solution)/shard_map/all_to_all | solution.py:286
  136.2 9.5 %all_to_all.23 = f32[8,1,2048]{2,1,0:T(1,128)S(1)} all-to-all(f32[8,1,2048]{2,1,0:T(1,128)S(1)} %broadcast_in_dim.25), channel_id=1, replica_groups=mesh['x'=4,'yh'=2,'c'=2,'z'=8,'t'=2] {'z'}, dimensions={0} | all-to-all | bytes 131072 | tf_op jit(solution)/shard_map/all_to_all | solution.py:286
  (60 shorter events, 20.9 us)
Async XLA Ops:
  7.3 12.5 %copy-start.2 = (f32[2048]{0:T(1024)S(1)}, f32[2048]{0:T(1024)}, u32[]{:S(2)}) copy-start(f32[2048]{0:T(1024)} %param.8) | copy-start | bytes 24580
  7.3 12.5 %copy-start.3 = (f32[2048]{0:T(1024)S(1)}, f32[2048]{0:T(1024)}, u32[]{:S(2)}) copy-start(f32[2048]{0:T(1024)} %param.7) | copy-start | bytes 24580
  8.4 11.4 %collective-permute-start.3 = (bf16[88,2048]{1,0:T(8,128)(2,1)S(1)}, bf16[88,2048]{1,0:T(8,128)(2,1)S(1)}, u32[]{:S(2)}, u32[]{:S(2)}) collective-permute-start(bf16[88,2048]{1,0:T(8,128)(2,1)S(1)} %fusion.1.refs_0_), channel_id=1, source_target_pairs={{0,16},{16,0},{1,17},{17,1},{2,18},{18,2},{3,19},{19,3},{4,20},{20... | collective-permute-start | bytes 1081352 | tf_op jit(solution)/shard_map/ppermute | solution.py:309
  12.2 10.0 %collective-permute-start.2 = (bf16[88,2048]{1,0:T(8,128)(2,1)S(1)}, bf16[88,2048]{1,0:T(8,128)(2,1)S(1)}, u32[]{:S(2)}, u32[]{:S(2)}) collective-permute-start(bf16[88,2048]{1,0:T(8,128)(2,1)S(1)} %fusion.1.refs_0_), channel_id=1, source_target_pairs={{0,192},{16,80},{64,0},{80,144},{128,64},{144,208},{192,128},{208,... | collective-permute-start | bytes 1081352 | tf_op jit(solution)/shard_map/ppermute | solution.py:294
  12.2 10.0 %collective-permute-start.1 = (bf16[88,2048]{1,0:T(8,128)(2,1)S(1)}, bf16[88,2048]{1,0:T(8,128)(2,1)S(1)}, u32[]{:S(2)}, u32[]{:S(2)}) collective-permute-start(bf16[88,2048]{1,0:T(8,128)(2,1)S(1)} %fusion.1.refs_0_), channel_id=1, source_target_pairs={{0,64},{16,208},{64,128},{80,16},{128,192},{144,80},{192,0},{208,1... | collective-permute-start | bytes 1081352 | tf_op jit(solution)/shard_map/ppermute | solution.py:294
  14.9 7.3 %collective-permute-start = (bf16[88,2048]{1,0:T(8,128)(2,1)S(1)}, bf16[88,2048]{1,0:T(8,128)(2,1)S(1)}, u32[]{:S(2)}, u32[]{:S(2)}) collective-permute-start(bf16[88,2048]{1,0:T(8,128)(2,1)S(1)} %fusion.1.refs_0_), channel_id=1, source_target_pairs={{0,1},{16,49},{1,32},{17,16},{32,33},{48,17},{33,0},{49,48},{2,3},... | collective-permute-start | bytes 1081352 | tf_op jit(solution)/shard_map/ppermute | solution.py:305
  22.3 7.9 %collective-permute-start.4 = (bf16[88,2048]{1,0:T(8,128)(2,1)S(1)}, bf16[88,2048]{1,0:T(8,128)(2,1)S(1)}, u32[]{:S(2)}, u32[]{:S(2)}) collective-permute-start(bf16[88,2048]{1,0:T(8,128)(2,1)S(1)} %collective-permute-done), channel_id=1, source_target_pairs={{0,1},{16,49},{1,32},{17,16},{32,33},{48,17},{33,0},{49,48},{2,3},... | collective-permute-start | bytes 1081352 | tf_op jit(solution)/shard_map/ppermute | solution.py:305
  24.2 7.2 %collective-permute-start.7 = (bf16[88,2048]{1,0:T(8,128)(2,1)S(1)}, bf16[88,2048]{1,0:T(8,128)(2,1)S(1)}, u32[]{:S(2)}, u32[]{:S(2)}) collective-permute-start(bf16[88,2048]{1,0:T(8,128)(2,1)S(1)} %collective-permute-done.2.refs_1_), channel_id=1, source_target_pairs={{0,16},{16,0},{1,17},{17,1},{2,18},{18,2},{3,19},{19,3},{4,20},{20... | collective-permute-start | bytes 1081352 | tf_op jit(solution)/shard_map/ppermute | solution.py:309
  24.3 7.1 %collective-permute-start.6 = (bf16[88,2048]{1,0:T(8,128)(2,1)S(1)}, bf16[88,2048]{1,0:T(8,128)(2,1)S(1)}, u32[]{:S(2)}, u32[]{:S(2)}) collective-permute-start(bf16[88,2048]{1,0:T(8,128)(2,1)S(1)} %collective-permute-done.1.refs_0_), channel_id=1, source_target_pairs={{0,16},{16,0},{1,17},{17,1},{2,18},{18,2},{3,19},{19,3},{4,20},{20... | collective-permute-start | bytes 1081352 | tf_op jit(solution)/shard_map/ppermute | solution.py:309
  24.7 7.4 %collective-permute-start.5 = (bf16[88,2048]{1,0:T(8,128)(2,1)S(1)}, bf16[88,2048]{1,0:T(8,128)(2,1)S(1)}, u32[]{:S(2)}, u32[]{:S(2)}) collective-permute-start(bf16[88,2048]{1,0:T(8,128)(2,1)S(1)} %collective-permute-done.1.refs_0_), channel_id=1, source_target_pairs={{0,64},{16,208},{64,128},{80,16},{128,192},{144,80},{192,0},{208,1... | collective-permute-start | bytes 1081352 | tf_op jit(solution)/shard_map/ppermute | solution.py:294
  27.8 11.2 %collective-permute-start.10 = (s16[192,640]{1,0:T(8,128)(2,1)S(1)}, s16[192,640]{1,0:T(8,128)(2,1)S(1)}, u32[]{:S(2)}, u32[]{:S(2)}) collective-permute-start(s16[192,640]{1,0:T(8,128)(2,1)S(1)} %get-tuple-element.105), channel_id=1, source_target_pairs={{0,1},{1,0},{2,3},{3,2},{4,5},{5,4},{6,7},{7,6},{8,9},{9,8},{10,11... | collective-permute-start | bytes 737288 | tf_op jit(solution)/shard_map/ppermute | solution.py:309
  30.1 9.1 %collective-permute-start.11 = (s16[192,640]{1,0:T(8,128)(2,1)S(1)}, s16[192,640]{1,0:T(8,128)(2,1)S(1)}, u32[]{:S(2)}, u32[]{:S(2)}) collective-permute-start(s16[192,640]{1,0:T(8,128)(2,1)S(1)} %get-tuple-element.112), channel_id=1, source_target_pairs={{0,1},{1,0},{2,3},{3,2},{4,5},{5,4},{6,7},{7,6},{8,9},{9,8},{10,11... | collective-permute-start | bytes 737288 | tf_op jit(solution)/shard_map/ppermute | solution.py:309
  32.2 10.8 %collective-permute-start.9 = (bf16[88,2048]{1,0:T(8,128)(2,1)S(1)}, bf16[88,2048]{1,0:T(8,128)(2,1)S(1)}, u32[]{:S(2)}, u32[]{:S(2)}) collective-permute-start(bf16[88,2048]{1,0:T(8,128)(2,1)S(1)} %collective-permute-done.4.refs_2_), channel_id=1, source_target_pairs={{0,192},{16,80},{64,0},{80,144},{128,64},{144,208},{192,128},{208,... | collective-permute-start | bytes 1081352 | tf_op jit(solution)/shard_map/ppermute | solution.py:294
  32.2 10.8 %collective-permute-start.8 = (bf16[88,2048]{1,0:T(8,128)(2,1)S(1)}, bf16[88,2048]{1,0:T(8,128)(2,1)S(1)}, u32[]{:S(2)}, u32[]{:S(2)}) collective-permute-start(bf16[88,2048]{1,0:T(8,128)(2,1)S(1)} %collective-permute-done.4.refs_2_), channel_id=1, source_target_pairs={{0,64},{16,208},{64,128},{80,16},{128,192},{144,80},{192,0},{208,1... | collective-permute-start | bytes 1081352 | tf_op jit(solution)/shard_map/ppermute | solution.py:294
  39.2 3.8 %collective-permute-start.12 = (bf16[88,2048]{1,0:T(8,128)(2,1)S(1)}, bf16[88,2048]{1,0:T(8,128)(2,1)S(1)}, u32[]{:S(2)}, u32[]{:S(2)}) collective-permute-start(bf16[88,2048]{1,0:T(8,128)(2,1)S(1)} %collective-permute-done.4.refs_2_), channel_id=1, source_target_pairs={{0,16},{16,0},{1,17},{17,1},{2,18},{18,2},{3,19},{19,3},{4,20},{20... | collective-permute-start | bytes 1081352 | tf_op jit(solution)/shard_map/ppermute | solution.py:309
  41.5 1.8 %collective-permute-start.13 = (bf16[88,2048]{1,0:T(8,128)(2,1)S(1)}, bf16[88,2048]{1,0:T(8,128)(2,1)S(1)}, u32[]{:S(2)}, u32[]{:S(2)}) collective-permute-start(bf16[88,2048]{1,0:T(8,128)(2,1)S(1)} %collective-permute-done.5.refs_3_), channel_id=1, source_target_pairs={{0,16},{16,0},{1,17},{17,1},{2,18},{18,2},{3,19},{19,3},{4,20},{20... | collective-permute-start | bytes 1081352 | tf_op jit(solution)/shard_map/ppermute | solution.py:309
  41.6 12.0 %collective-permute-start.17 = (s16[368,640]{1,0:T(8,128)(2,1)S(1)}, s16[368,640]{1,0:T(8,128)(2,1)S(1)}, u32[]{:S(2)}, u32[]{:S(2)}) collective-permute-start(s16[368,640]{1,0:T(8,128)(2,1)S(1)} %get-tuple-element.120), channel_id=1, source_target_pairs={{0,1},{1,0},{2,3},{3,2},{4,5},{5,4},{6,7},{7,6},{8,9},{9,8},{10,11... | collective-permute-start | bytes 1413128 | tf_op jit(solution)/shard_map/ppermute | solution.py:309
  43.3 10.2 %collective-permute-start.14 = (bf16[88,2048]{1,0:T(8,128)(2,1)S(1)}, bf16[88,2048]{1,0:T(8,128)(2,1)S(1)}, u32[]{:S(2)}, u32[]{:S(2)}) collective-permute-start(bf16[88,2048]{1,0:T(8,128)(2,1)S(1)} %collective-permute-done.8.refs_2_), channel_id=1, source_target_pairs={{0,64},{16,208},{64,128},{80,16},{128,192},{144,80},{192,0},{208,1... | collective-permute-start | bytes 1081352 | tf_op jit(solution)/shard_map/ppermute | solution.py:294
  50.0 3.5 %collective-permute-start.15 = (bf16[88,2048]{1,0:T(8,128)(2,1)S(1)}, bf16[88,2048]{1,0:T(8,128)(2,1)S(1)}, u32[]{:S(2)}, u32[]{:S(2)}) collective-permute-start(bf16[88,2048]{1,0:T(8,128)(2,1)S(1)} %collective-permute-done.8.refs_2_), channel_id=1, source_target_pairs={{0,16},{16,0},{1,17},{17,1},{2,18},{18,2},{3,19},{19,3},{4,20},{20... | collective-permute-start | bytes 1081352 | tf_op jit(solution)/shard_map/ppermute | solution.py:309
  50.1 3.4 %collective-permute-start.16 = (bf16[88,2048]{1,0:T(8,128)(2,1)S(1)}, bf16[88,2048]{1,0:T(8,128)(2,1)S(1)}, u32[]{:S(2)}, u32[]{:S(2)}) collective-permute-start(bf16[88,2048]{1,0:T(8,128)(2,1)S(1)} %collective-permute-done.9.refs_3_), channel_id=1, source_target_pairs={{0,16},{16,0},{1,17},{17,1},{2,18},{18,2},{3,19},{19,3},{4,20},{20... | collective-permute-start | bytes 1081352 | tf_op jit(solution)/shard_map/ppermute | solution.py:309
  53.5 3.0 %collective-permute-start.18 = (bf16[88,2048]{1,0:T(8,128)(2,1)S(1)}, bf16[88,2048]{1,0:T(8,128)(2,1)S(1)}, u32[]{:S(2)}, u32[]{:S(2)}) collective-permute-start(bf16[88,2048]{1,0:T(8,128)(2,1)S(1)} %collective-permute-done.14.refs_2_), channel_id=1, source_target_pairs={{0,16},{16,0},{1,17},{17,1},{2,18},{18,2},{3,19},{19,3},{4,20},{20... | collective-permute-start | bytes 1081352 | tf_op jit(solution)/shard_map/ppermute | solution.py:309
  54.9 12.1 %collective-permute-start.19 = (s16[368,640]{1,0:T(8,128)(2,1)S(1)}, s16[368,640]{1,0:T(8,128)(2,1)S(1)}, u32[]{:S(2)}, u32[]{:S(2)}) collective-permute-start(s16[368,640]{1,0:T(8,128)(2,1)S(1)} %get-tuple-element.137), channel_id=1, source_target_pairs={{0,1},{1,0},{2,3},{3,2},{4,5},{5,4},{6,7},{7,6},{8,9},{9,8},{10,11... | collective-permute-start | bytes 1413128 | tf_op jit(solution)/shard_map/ppermute | solution.py:309
  60.2 16.8 %collective-permute-start.20 = (s16[368,640]{1,0:T(8,128)(2,1)S(1)}, s16[368,640]{1,0:T(8,128)(2,1)S(1)}, u32[]{:S(2)}, u32[]{:S(2)}) collective-permute-start(s16[368,640]{1,0:T(8,128)(2,1)S(1)} %get-tuple-element.162), channel_id=1, source_target_pairs={{0,1},{1,0},{2,3},{3,2},{4,5},{5,4},{6,7},{7,6},{8,9},{9,8},{10,11... | collective-permute-start | bytes 1413128 | tf_op jit(solution)/shard_map/ppermute | solution.py:309
  95.2 3.7 %collective-permute-start.21 = (f32[4,1408]{1,0:T(4,128)S(1)}, f32[4,1408]{1,0:T(4,128)S(1)}, u32[]{:S(2)}, u32[]{:S(2)}) collective-permute-start(f32[4,1408]{1,0:T(4,128)S(1)} %first_merge.1.one_ref), channel_id=1, source_target_pairs={{0,16},{16,0},{1,17},{17,1},{2,18},{18,2},{3,19},{19,3},{4,20},{20... | collective-permute-start | bytes 67592 | tf_op jit(solution)/shard_map/ppermute | solution.py:309
  (2 other events, 3.5 us)

commit v7 on v6

--- a/solution.py
+++ b/solution.py
@@ -40,27 +40,31 @@
     return filled.T[:size]
 
 
-def load_kernel(*refs, count):
-    copies = [
-        pltpu.make_async_copy(refs[i], refs[count + i], refs[2 * count].at[i]) for i in range(count)
-    ]
+def load_kernel(place_ref, sampled_ref, *refs, count, size):
+    sources, ids_ref, targets, sems = refs[:count], refs[count], refs[count + 1 : 2 * count + 1], refs[-1]
+    copies = [pltpu.make_async_copy(f, t, sems.at[i]) for i, (f, t) in enumerate(zip(sources, targets))]
     for copy in copies:
         copy.start()
+    ids = sampled_ref[...].astype(F32) - place_ref[len(BLOCKS)].astype(F32)
+    ids_ref[...] = jnp.zeros_like(ids_ref)
+    for b in range(len(BLOCKS)):
+        ids_ref[b : b + 1, :size] = ids[:, b * size : (b + 1) * size]
     for copy in copies:
         copy.wait()
 
 
-def load(*arrays):
+def load(place, sampled, *arrays):
     count = len(arrays)
     return pl.pallas_call(
-        functools.partial(load_kernel, count=count),
-        in_specs=[pl.BlockSpec(memory_space=pl.ANY)] * count,
-        out_specs=[ON_CHIP] * count,
-        out_shape=[pltpu.VMEM(a.shape, a.dtype) for a in arrays],
+        functools.partial(load_kernel, count=count, size=sampled.shape[1] // len(BLOCKS)),
+        in_specs=[SCALARS, ON_CHIP] + [pl.BlockSpec(memory_space=pl.ANY)] * count,
+        out_specs=[ON_CHIP] * (count + 1),
+        out_shape=[pltpu.VMEM((len(BLOCKS), LANES), F32)]
+        + [pltpu.VMEM(a.shape, a.dtype) for a in arrays],
         scratch_shapes=[pltpu.SemaphoreType.DMA((count,))],
         compiler_params=pltpu.CompilerParams(vmem_limit_bytes=VMEM_BYTES),
         name="load",
-    )(*arrays)
+    )(place, sampled, *arrays)
 
 
 def front_kernel(*refs, pieces, rows):
@@ -247,7 +251,7 @@
     part_ref[...] = jnp.broadcast_to(part, (part.shape[0], LANES)).T[:1]
 
 
-def finish(place, ids, merged, e, stats, x, weight, gain, size, block=512):
+def finish(place, ids, merged, e, stats, x, weight, gain, size, block=1024):
     width, cols = weight.shape
     rows = sum(a.shape[0] for a in x)
     chunks = len(x)
@@ -323,19 +327,17 @@
         back = 1 - 2 * (c_at ^ g)
         x_of = x_at + (0, -back, back, 2)[way]
         place.append((((x_of + around) % around) * 2 + (y_at ^ h)) * 2 + (c_at ^ g))
-    place = jnp.stack(place).astype(jnp.int32)
     offset = (((x_at * 2 + y_at) * 2 + c_at) * lax.axis_size("z") + z_at) * vocab_dev
-    ids = jnp.pad(
-        (sampled - offset).astype(F32).reshape(len(BLOCKS), size), ((0, 0), (0, LANES - size))
-    )
+    place = jnp.stack(place + [offset]).astype(jnp.int32)
+    sampled = sampled[None]
     gain_row, dir_row = norm_gain[None], gain_dir[None]
 
-    place, ids, residual, gain_row, dir_row = together(place, ids, residual, gain_row, dir_row)
+    place, sampled, residual, gain_row, dir_row = together(place, sampled, residual, gain_row, dir_row)
     entries = residual.astype(F32)
     squares = lax.psum(jnp.sum(entries * entries, axis=1), "t")
     normed = (entries * lax.rsqrt(squares / (2 * width) + EPSILON)[:, None]).astype(BF16)
 
-    weight, slope = load(head_weight, head_dir)
+    ids, weight, slope = load(place, sampled, head_weight, head_dir)
 
     def chunk_front(*pieces):
         return front(pieces, gain_row, dir_row, weight, slope)

time: 147 us -> 146 us (level)
  transfers between devices with their start and end apart: 22 -> 22, of which waited for: 8 -> 7; matrix products, arithmetic and copies ran while one was open for 0% -> 0% of each run, Pallas kernels for 14% -> 14%
where the time goes in v7:
time: 146 us
  blocking collectives  57.6 us (39%)
  Pallas kernels  31.8 us (22%)
  starting transfers between devices  29.6 us (20%)
  waiting for transfers between devices  18.4 us (13%)
  local copies, waits for them, and re-layouts  4.38 us (3%)
  other arithmetic  3.05 us (2%)
    all_to_all x2, blocking collectives, everyone(): return lax.all_to_all(copies, axes, 0, 0, tiled=True)  22.2 us
    ppermute x14, waiting for transfers between devices, swap(): return lax.ppermute(x, (axis,), [(0, 1), (1, 0)])  17.5 us
    all_to_all x1, blocking collectives, local(): lax.all_to_all(own, 'z', 0, 0, tiled=True)  16 us
    pallas_call x5, Pallas kernels, front(): pl.pallas_call(functools.partial(front_kernel, pieces=len(pieces), rows=r...  15.1 us
    ppermute x14, starting transfers between devices, swap(): return lax.ppermute(x, (axis,), [(0, 1), (1, 0)])  15.1 us
    all_to_all x1, blocking collectives, local(): lax.all_to_all(on_chip, rest, 0, 0, tiled=True)  15 us
    ppermute x6, starting transfers between devices, along_x(): return lax.ppermute(x, ('x', 'c'), pairs)  11.8 us
    pallas_call x1, Pallas kernels, finish(): pl.pallas_call(functools.partial(product_kernel, chunks=chunks, size=size...  8.87 us
  transfers between devices with their start and end apart: 22, of which 7 were waited for; matrix products, arithmetic and copies ran while one was open for 0% of the time, Pallas kernels for 14%

profile of v7, /device:TPU:1, one launch (start us, length us, event | category | flops | bytes accessed | tf_op | source)
XLA Modules:
  0.0 145.9 jit_solution(7743819156891597134)
XLA Ops:
  2.7 4.4 %psum.7 = f32[88]{0:T(128)S(1)} all-reduce(f32[88]{0:T(128)S(1)} %fusion), channel_id=1, replica_groups=mesh['x'=4,'yh'=2,'c'=2,'z'=8,'t'=2] {'t'}, use_global_device_ids=true, to_apply=%region_1.2 | all-reduce | flops 88 | bytes 704 | tf_op jit(solution)/shard_map/psum | solution.py:337
  8.3 3.8 %collective-permute-start.3 = (bf16[88,2048]{1,0:T(8,128)(2,1)S(1)}, bf16[88,2048]{1,0:T(8,128)(2,1)S(1)}, u32[]{:S(2)}, u32[]{:S(2)}) collective-permute-start(bf16[88,2048]{1,0:T(8,128)(2,1)S(1)} %fusion.1.refs_0_), channel_id=1, source_target_pairs={{0,16},{16,0},{1,17},{17,1},{2,18},{18,2},{3,19},{19,3},{4,20},{20... | collective-permute-start | bytes 1081352 | tf_op jit(solution)/shard_map/ppermute | solution.py:313
  12.1 2.7 %collective-permute-start.1 = (bf16[88,2048]{1,0:T(8,128)(2,1)S(1)}, bf16[88,2048]{1,0:T(8,128)(2,1)S(1)}, u32[]{:S(2)}, u32[]{:S(2)}) collective-permute-start(bf16[88,2048]{1,0:T(8,128)(2,1)S(1)} %fusion.1.refs_0_), channel_id=1, source_target_pairs={{0,64},{16,208},{64,128},{80,16},{128,192},{144,80},{192,0},{208,1... | collective-permute-start | bytes 1081352 | tf_op jit(solution)/shard_map/ppermute | solution.py:298
  15.8 1.7 %copy-done = bf16[2048,640]{1,0:T(8,128)(2,1)S(1)} copy-done((bf16[2048,640]{1,0:T(8,128)(2,1)S(1)}, bf16[2048,640]{1,0:T(8,128)(2,1)}, u32[]{:S(2)}) %copy-start) | copy-done | bytes 2621464
  17.6 1.7 %copy-done.1 = bf16[2048,640]{1,0:T(8,128)(2,1)S(1)} copy-done((bf16[2048,640]{1,0:T(8,128)(2,1)S(1)}, bf16[2048,640]{1,0:T(8,128)(2,1)}, u32[]{:S(2)}) %copy-start.1) | copy-done | bytes 2621464
  20.3 2.0 %front.5 = (f32[176,640]{1,0:T(8,128)S(1)}, s16[192,640]{1,0:T(8,128)(2,1)S(1)}, f32[176,640]{1,0:T(8,128)S(1)}, bf16[176,2048]{1,0:T(8,128)(2,1)S(1)}) custom-call(bf16[88,2048]{1,0:T(8,128)(2,1)S(1)} %fusion.1.refs_0_, bf16[88,2048]{1,0:T(8,128)(2,1)S(1)} %collective-permute-done.3.refs_1_, f32[1,2048]{1,0:T(1,128)S(1)} %bitcast.25, ...), custom_call_target="tpu_custom_call" | custom-call | flops 1384120320 | bytes 1441792 | tf_op jit(solution)/shard_map/front/pallas_call | solution.py:93
  22.4 1.8 %collective-permute-start.4 = (bf16[88,2048]{1,0:T(8,128)(2,1)S(1)}, bf16[88,2048]{1,0:T(8,128)(2,1)S(1)}, u32[]{:S(2)}, u32[]{:S(2)}) collective-permute-start(bf16[88,2048]{1,0:T(8,128)(2,1)S(1)} %collective-permute-done), channel_id=1, source_target_pairs={{0,1},{16,49},{1,32},{17,16},{32,33},{48,17},{33,0},{49,48},{2,3},... | collective-permute-start | bytes 1081352 | tf_op jit(solution)/shard_map/ppermute | solution.py:309
  24.6 3.1 %collective-permute-start.5 = (bf16[88,2048]{1,0:T(8,128)(2,1)S(1)}, bf16[88,2048]{1,0:T(8,128)(2,1)S(1)}, u32[]{:S(2)}, u32[]{:S(2)}) collective-permute-start(bf16[88,2048]{1,0:T(8,128)(2,1)S(1)} %collective-permute-done.1.refs_0_), channel_id=1, source_target_pairs={{0,64},{16,208},{64,128},{80,16},{128,192},{144,80},{192,0},{208,1... | collective-permute-start | bytes 1081352 | tf_op jit(solution)/shard_map/ppermute | solution.py:298
  28.0 2.0 %front.6 = (f32[176,640]{1,0:T(8,128)S(1)}, s16[192,640]{1,0:T(8,128)(2,1)S(1)}, f32[176,640]{1,0:T(8,128)S(1)}, bf16[176,2048]{1,0:T(8,128)(2,1)S(1)}) custom-call(bf16[88,2048]{1,0:T(8,128)(2,1)S(1)} %collective-permute-done.1.refs_0_, bf16[88,2048]{1,0:T(8,128)(2,1)S(1)} %collective-permute-done.2.refs_1_, f32[1,2048]{1,0:T(1,128)S(1)} %bitcast.26, ...), custom_call_target="tpu_custom_call" | custom-call | flops 1384120320 | bytes 1441792 | tf_op jit(solution)/shard_map/front/pallas_call | solution.py:93
  32.1 3.1 %collective-permute-start.8 = (bf16[88,2048]{1,0:T(8,128)(2,1)S(1)}, bf16[88,2048]{1,0:T(8,128)(2,1)S(1)}, u32[]{:S(2)}, u32[]{:S(2)}) collective-permute-start(bf16[88,2048]{1,0:T(8,128)(2,1)S(1)} %collective-permute-done.4.refs_2_), channel_id=1, source_target_pairs={{0,64},{16,208},{64,128},{80,16},{128,192},{144,80},{192,0},{208,1... | collective-permute-start | bytes 1081352 | tf_op jit(solution)/shard_map/ppermute | solution.py:298
  35.2 3.7 %front.7 = (f32[352,640]{1,0:T(8,128)S(1)}, s16[368,640]{1,0:T(8,128)(2,1)S(1)}, f32[352,640]{1,0:T(8,128)S(1)}, bf16[352,2048]{1,0:T(8,128)(2,1)S(1)}) custom-call(bf16[88,2048]{1,0:T(8,128)(2,1)S(1)} %collective-permute-done.6.refs_0_, bf16[88,2048]{1,0:T(8,128)(2,1)S(1)} %collective-permute-done.7.refs_1_, ...), custom_call_target="tpu_custom_call" | custom-call | flops 2768240640 | bytes 2883584 | tf_op jit(solution)/shard_map/front/pallas_call | solution.py:93
  39.1 2.2 %collective-permute-start.12 = (bf16[88,2048]{1,0:T(8,128)(2,1)S(1)}, bf16[88,2048]{1,0:T(8,128)(2,1)S(1)}, u32[]{:S(2)}, u32[]{:S(2)}) collective-permute-start(bf16[88,2048]{1,0:T(8,128)(2,1)S(1)} %collective-permute-done.4.refs_2_), channel_id=1, source_target_pairs={{0,16},{16,0},{1,17},{17,1},{2,18},{18,2},{3,19},{19,3},{4,20},{20... | collective-permute-start | bytes 1081352 | tf_op jit(solution)/shard_map/ppermute | solution.py:313
  43.2 3.0 %collective-permute-start.14 = (bf16[88,2048]{1,0:T(8,128)(2,1)S(1)}, bf16[88,2048]{1,0:T(8,128)(2,1)S(1)}, u32[]{:S(2)}, u32[]{:S(2)}) collective-permute-start(bf16[88,2048]{1,0:T(8,128)(2,1)S(1)} %collective-permute-done.8.refs_2_), channel_id=1, source_target_pairs={{0,64},{16,208},{64,128},{80,16},{128,192},{144,80},{192,0},{208,1... | collective-permute-start | bytes 1081352 | tf_op jit(solution)/shard_map/ppermute | solution.py:298
  46.1 3.7 %front.8 = (f32[352,640]{1,0:T(8,128)S(1)}, s16[368,640]{1,0:T(8,128)(2,1)S(1)}, f32[352,640]{1,0:T(8,128)S(1)}, bf16[352,2048]{1,0:T(8,128)(2,1)S(1)}) custom-call(bf16[88,2048]{1,0:T(8,128)(2,1)S(1)} %collective-permute-done.12.refs_0_, bf16[88,2048]{1,0:T(8,128)(2,1)S(1)} %collective-permute-done.13.refs_1_, ...), custom_call_target="tpu_custom_call" | custom-call | flops 2768240640 | bytes 2883584 | tf_op jit(solution)/shard_map/front/pallas_call | solution.py:93
  51.5 1.9 %collective-permute-done.17.code_ref = s16[368,640]{1,0:T(8,128)(2,1)S(1)} collective-permute-done((s16[368,640]{1,0:T(8,128)(2,1)S(1)}, s16[368,640]{1,0:T(8,128)(2,1)S(1)}, u32[]{:S(2)}, u32[]{:S(2)}) %collective-permute-start.17) | collective-permute-done | bytes 471072 | tf_op jit(solution)/shard_map/ppermute | solution.py:313
  56.4 3.7 %front.9 = (f32[352,640]{1,0:T(8,128)S(1)}, s16[368,640]{1,0:T(8,128)(2,1)S(1)}, f32[352,640]{1,0:T(8,128)S(1)}, bf16[352,2048]{1,0:T(8,128)(2,1)S(1)}) custom-call(bf16[88,2048]{1,0:T(8,128)(2,1)S(1)} %collective-permute-done.15.refs_0_, bf16[88,2048]{1,0:T(8,128)(2,1)S(1)} %collective-permute-done.16.refs_1_, ...), custom_call_target="tpu_custom_call" | custom-call | flops 2768240640 | bytes 2883584 | tf_op jit(solution)/shard_map/front/pallas_call | solution.py:93
  61.3 5.5 %collective-permute-done.19.code_ref = s16[368,640]{1,0:T(8,128)(2,1)S(1)} collective-permute-done((s16[368,640]{1,0:T(8,128)(2,1)S(1)}, s16[368,640]{1,0:T(8,128)(2,1)S(1)}, u32[]{:S(2)}, u32[]{:S(2)}) %collective-permute-start.19) | collective-permute-done | bytes 471072 | tf_op jit(solution)/shard_map/ppermute | solution.py:313
  68.1 8.8 %collective-permute-done.20.code_ref = s16[368,640]{1,0:T(8,128)(2,1)S(1)} collective-permute-done((s16[368,640]{1,0:T(8,128)(2,1)S(1)}, s16[368,640]{1,0:T(8,128)(2,1)S(1)}, u32[]{:S(2)}, u32[]{:S(2)}) %collective-permute-start.20) | collective-permute-done | bytes 471072 | tf_op jit(solution)/shard_map/ppermute | solution.py:313
  78.3 16.0 %all_to_all.20.parts_ref = f32[8,4,1408]{2,1,0:T(4,128)S(1)} all-to-all(f32[8,4,1408]{2,1,0:T(4,128)S(1)} %copies.1), channel_id=1, replica_groups=mesh['x'=4,'yh'=2,'c'=2,'z'=8,'t'=2] {'z'}, dimensions={0} | all-to-all | bytes 360448 | tf_op jit(solution)/shard_map/all_to_all | solution.py:398
  95.0 2.8 %collective-permute-start.21 = (f32[4,1408]{1,0:T(4,128)S(1)}, f32[4,1408]{1,0:T(4,128)S(1)}, u32[]{:S(2)}, u32[]{:S(2)}) collective-permute-start(f32[4,1408]{1,0:T(4,128)S(1)} %first_merge.1.one_ref), channel_id=1, source_target_pairs={{0,16},{16,0},{1,17},{17,1},{2,18},{18,2},{3,19},{19,3},{4,20},{20... | collective-permute-start | bytes 67592 | tf_op jit(solution)/shard_map/ppermute | solution.py:313
  98.8 15.0 %all_to_all.21.parts_ref = f32[16,4,1408]{2,1,0:T(4,128)S(1)} all-to-all(f32[16,4,1408]{2,1,0:T(4,128)S(1)} %pair_merge.1), channel_id=1, replica_groups=mesh['x'=4,'yh'=2,'c'=2,'z'=8,'t'=2] {'x','yh','t'}, dimensions={0} | all-to-all | bytes 720896 | tf_op jit(solution)/shard_map/all_to_all | solution.py:408
  113.9 8.9 %product.1 = (f32[2048,640]{1,0:T(8,128)}, f32[1,2048]{1,0:T(1,128)S(1)}) custom-call(s32[17]{0:T(128)S(1)} %stack.71.place_ref.refs_0_, f32[16,128]{1,0:T(8,128)S(1)} %get-tuple-element.100.ids_ref.refs_1_, f32[16,4,128]{2,1,0:T(4,128)S(1)} %last_merge.1.refs_2_, f32[176,640]{1,0:T(8,128)S(1)} %get-tuple-element.177.refs_3_, ...), custom_call_target="tpu_custom_call" | custom-call | flops 3690987520 | bytes 5242880 | tf_op jit(solution)/shard_map/product/pallas_call | solution.py:258
  122.9 12.7 %all_to_all.22 = f32[16,1,2048]{2,1,0:T(1,128)S(1)} all-to-all(f32[16,1,2048]{2,1,0:T(1,128)S(1)} %broadcast_in_dim.28), channel_id=1, replica_groups=mesh['x'=4,'yh'=2,'c'=2,'z'=8,'t'=2] {'x','yh','c'}, dimensions={0} | all-to-all | bytes 262144 | tf_op jit(solution)/shard_map/all_to_all | solution.py:290
  135.7 9.5 %all_to_all.23 = f32[8,1,2048]{2,1,0:T(1,128)S(1)} all-to-all(f32[8,1,2048]{2,1,0:T(1,128)S(1)} %broadcast_in_dim.29), channel_id=1, replica_groups=mesh['x'=4,'yh'=2,'c'=2,'z'=8,'t'=2] {'z'}, dimensions={0} | all-to-all | bytes 131072 | tf_op jit(solution)/shard_map/all_to_all | solution.py:290
  (58 shorter events, 21.1 us)
Async XLA Ops:
  7.2 13.2 %copy-start.2 = (f32[2048]{0:T(1024)S(1)}, f32[2048]{0:T(1024)}, u32[]{:S(2)}) copy-start(f32[2048]{0:T(1024)} %param.8) | copy-start | bytes 24580
  7.2 13.2 %copy-start.3 = (f32[2048]{0:T(1024)S(1)}, f32[2048]{0:T(1024)}, u32[]{:S(2)}) copy-start(f32[2048]{0:T(1024)} %param.7) | copy-start | bytes 24580
  8.3 12.0 %collective-permute-start.3 = (bf16[88,2048]{1,0:T(8,128)(2,1)S(1)}, bf16[88,2048]{1,0:T(8,128)(2,1)S(1)}, u32[]{:S(2)}, u32[]{:S(2)}) collective-permute-start(bf16[88,2048]{1,0:T(8,128)(2,1)S(1)} %fusion.1.refs_0_), channel_id=1, source_target_pairs={{0,16},{16,0},{1,17},{17,1},{2,18},{18,2},{3,19},{19,3},{4,20},{20... | collective-permute-start | bytes 1081352 | tf_op jit(solution)/shard_map/ppermute | solution.py:313
  12.1 10.2 %collective-permute-start.2 = (bf16[88,2048]{1,0:T(8,128)(2,1)S(1)}, bf16[88,2048]{1,0:T(8,128)(2,1)S(1)}, u32[]{:S(2)}, u32[]{:S(2)}) collective-permute-start(bf16[88,2048]{1,0:T(8,128)(2,1)S(1)} %fusion.1.refs_0_), channel_id=1, source_target_pairs={{0,192},{16,80},{64,0},{80,144},{128,64},{144,208},{192,128},{208,... | collective-permute-start | bytes 1081352 | tf_op jit(solution)/shard_map/ppermute | solution.py:298
  12.1 10.2 %collective-permute-start.1 = (bf16[88,2048]{1,0:T(8,128)(2,1)S(1)}, bf16[88,2048]{1,0:T(8,128)(2,1)S(1)}, u32[]{:S(2)}, u32[]{:S(2)}) collective-permute-start(bf16[88,2048]{1,0:T(8,128)(2,1)S(1)} %fusion.1.refs_0_), channel_id=1, source_target_pairs={{0,64},{16,208},{64,128},{80,16},{128,192},{144,80},{192,0},{208,1... | collective-permute-start | bytes 1081352 | tf_op jit(solution)/shard_map/ppermute | solution.py:298
  14.8 7.6 %collective-permute-start = (bf16[88,2048]{1,0:T(8,128)(2,1)S(1)}, bf16[88,2048]{1,0:T(8,128)(2,1)S(1)}, u32[]{:S(2)}, u32[]{:S(2)}) collective-permute-start(bf16[88,2048]{1,0:T(8,128)(2,1)S(1)} %fusion.1.refs_0_), channel_id=1, source_target_pairs={{0,1},{16,49},{1,32},{17,16},{32,33},{48,17},{33,0},{49,48},{2,3},... | collective-permute-start | bytes 1081352 | tf_op jit(solution)/shard_map/ppermute | solution.py:309
  22.4 7.6 %collective-permute-start.4 = (bf16[88,2048]{1,0:T(8,128)(2,1)S(1)}, bf16[88,2048]{1,0:T(8,128)(2,1)S(1)}, u32[]{:S(2)}, u32[]{:S(2)}) collective-permute-start(bf16[88,2048]{1,0:T(8,128)(2,1)S(1)} %collective-permute-done), channel_id=1, source_target_pairs={{0,1},{16,49},{1,32},{17,16},{32,33},{48,17},{33,0},{49,48},{2,3},... | collective-permute-start | bytes 1081352 | tf_op jit(solution)/shard_map/ppermute | solution.py:309
  24.1 7.1 %collective-permute-start.7 = (bf16[88,2048]{1,0:T(8,128)(2,1)S(1)}, bf16[88,2048]{1,0:T(8,128)(2,1)S(1)}, u32[]{:S(2)}, u32[]{:S(2)}) collective-permute-start(bf16[88,2048]{1,0:T(8,128)(2,1)S(1)} %collective-permute-done.2.refs_1_), channel_id=1, source_target_pairs={{0,16},{16,0},{1,17},{17,1},{2,18},{18,2},{3,19},{19,3},{4,20},{20... | collective-permute-start | bytes 1081352 | tf_op jit(solution)/shard_map/ppermute | solution.py:313
  24.2 7.1 %collective-permute-start.6 = (bf16[88,2048]{1,0:T(8,128)(2,1)S(1)}, bf16[88,2048]{1,0:T(8,128)(2,1)S(1)}, u32[]{:S(2)}, u32[]{:S(2)}) collective-permute-start(bf16[88,2048]{1,0:T(8,128)(2,1)S(1)} %collective-permute-done.1.refs_0_), channel_id=1, source_target_pairs={{0,16},{16,0},{1,17},{17,1},{2,18},{18,2},{3,19},{19,3},{4,20},{20... | collective-permute-start | bytes 1081352 | tf_op jit(solution)/shard_map/ppermute | solution.py:313
  24.6 7.4 %collective-permute-start.5 = (bf16[88,2048]{1,0:T(8,128)(2,1)S(1)}, bf16[88,2048]{1,0:T(8,128)(2,1)S(1)}, u32[]{:S(2)}, u32[]{:S(2)}) collective-permute-start(bf16[88,2048]{1,0:T(8,128)(2,1)S(1)} %collective-permute-done.1.refs_0_), channel_id=1, source_target_pairs={{0,64},{16,208},{64,128},{80,16},{128,192},{144,80},{192,0},{208,1... | collective-permute-start | bytes 1081352 | tf_op jit(solution)/shard_map/ppermute | solution.py:298
  27.7 11.2 %collective-permute-start.10 = (s16[192,640]{1,0:T(8,128)(2,1)S(1)}, s16[192,640]{1,0:T(8,128)(2,1)S(1)}, u32[]{:S(2)}, u32[]{:S(2)}) collective-permute-start(s16[192,640]{1,0:T(8,128)(2,1)S(1)} %get-tuple-element.107), channel_id=1, source_target_pairs={{0,1},{1,0},{2,3},{3,2},{4,5},{5,4},{6,7},{7,6},{8,9},{9,8},{10,11... | collective-permute-start | bytes 737288 | tf_op jit(solution)/shard_map/ppermute | solution.py:313
  30.0 9.1 %collective-permute-start.11 = (s16[192,640]{1,0:T(8,128)(2,1)S(1)}, s16[192,640]{1,0:T(8,128)(2,1)S(1)}, u32[]{:S(2)}, u32[]{:S(2)}) collective-permute-start(s16[192,640]{1,0:T(8,128)(2,1)S(1)} %get-tuple-element.114), channel_id=1, source_target_pairs={{0,1},{1,0},{2,3},{3,2},{4,5},{5,4},{6,7},{7,6},{8,9},{9,8},{10,11... | collective-permute-start | bytes 737288 | tf_op jit(solution)/shard_map/ppermute | solution.py:313
  32.1 10.8 %collective-permute-start.9 = (bf16[88,2048]{1,0:T(8,128)(2,1)S(1)}, bf16[88,2048]{1,0:T(8,128)(2,1)S(1)}, u32[]{:S(2)}, u32[]{:S(2)}) collective-permute-start(bf16[88,2048]{1,0:T(8,128)(2,1)S(1)} %collective-permute-done.4.refs_2_), channel_id=1, source_target_pairs={{0,192},{16,80},{64,0},{80,144},{128,64},{144,208},{192,128},{208,... | collective-permute-start | bytes 1081352 | tf_op jit(solution)/shard_map/ppermute | solution.py:298
  32.1 10.8 %collective-permute-start.8 = (bf16[88,2048]{1,0:T(8,128)(2,1)S(1)}, bf16[88,2048]{1,0:T(8,128)(2,1)S(1)}, u32[]{:S(2)}, u32[]{:S(2)}) collective-permute-start(bf16[88,2048]{1,0:T(8,128)(2,1)S(1)} %collective-permute-done.4.refs_2_), channel_id=1, source_target_pairs={{0,64},{16,208},{64,128},{80,16},{128,192},{144,80},{192,0},{208,1... | collective-permute-start | bytes 1081352 | tf_op jit(solution)/shard_map/ppermute | solution.py:298
  39.1 3.8 %collective-permute-start.12 = (bf16[88,2048]{1,0:T(8,128)(2,1)S(1)}, bf16[88,2048]{1,0:T(8,128)(2,1)S(1)}, u32[]{:S(2)}, u32[]{:S(2)}) collective-permute-start(bf16[88,2048]{1,0:T(8,128)(2,1)S(1)} %collective-permute-done.4.refs_2_), channel_id=1, source_target_pairs={{0,16},{16,0},{1,17},{17,1},{2,18},{18,2},{3,19},{19,3},{4,20},{20... | collective-permute-start | bytes 1081352 | tf_op jit(solution)/shard_map/ppermute | solution.py:313
  41.3 1.8 %collective-permute-start.13 = (bf16[88,2048]{1,0:T(8,128)(2,1)S(1)}, bf16[88,2048]{1,0:T(8,128)(2,1)S(1)}, u32[]{:S(2)}, u32[]{:S(2)}) collective-permute-start(bf16[88,2048]{1,0:T(8,128)(2,1)S(1)} %collective-permute-done.5.refs_3_), channel_id=1, source_target_pairs={{0,16},{16,0},{1,17},{17,1},{2,18},{18,2},{3,19},{19,3},{4,20},{20... | collective-permute-start | bytes 1081352 | tf_op jit(solution)/shard_map/ppermute | solution.py:313
  41.4 12.0 %collective-permute-start.17 = (s16[368,640]{1,0:T(8,128)(2,1)S(1)}, s16[368,640]{1,0:T(8,128)(2,1)S(1)}, u32[]{:S(2)}, u32[]{:S(2)}) collective-permute-start(s16[368,640]{1,0:T(8,128)(2,1)S(1)} %get-tuple-element.122), channel_id=1, source_target_pairs={{0,1},{1,0},{2,3},{3,2},{4,5},{5,4},{6,7},{7,6},{8,9},{9,8},{10,11... | collective-permute-start | bytes 1413128 | tf_op jit(solution)/shard_map/ppermute | solution.py:313
  43.2 10.2 %collective-permute-start.14 = (bf16[88,2048]{1,0:T(8,128)(2,1)S(1)}, bf16[88,2048]{1,0:T(8,128)(2,1)S(1)}, u32[]{:S(2)}, u32[]{:S(2)}) collective-permute-start(bf16[88,2048]{1,0:T(8,128)(2,1)S(1)} %collective-permute-done.8.refs_2_), channel_id=1, source_target_pairs={{0,64},{16,208},{64,128},{80,16},{128,192},{144,80},{192,0},{208,1... | collective-permute-start | bytes 1081352 | tf_op jit(solution)/shard_map/ppermute | solution.py:298
  49.8 3.6 %collective-permute-start.15 = (bf16[88,2048]{1,0:T(8,128)(2,1)S(1)}, bf16[88,2048]{1,0:T(8,128)(2,1)S(1)}, u32[]{:S(2)}, u32[]{:S(2)}) collective-permute-start(bf16[88,2048]{1,0:T(8,128)(2,1)S(1)} %collective-permute-done.8.refs_2_), channel_id=1, source_target_pairs={{0,16},{16,0},{1,17},{17,1},{2,18},{18,2},{3,19},{19,3},{4,20},{20... | collective-permute-start | bytes 1081352 | tf_op jit(solution)/shard_map/ppermute | solution.py:313
  50.0 3.4 %collective-permute-start.16 = (bf16[88,2048]{1,0:T(8,128)(2,1)S(1)}, bf16[88,2048]{1,0:T(8,128)(2,1)S(1)}, u32[]{:S(2)}, u32[]{:S(2)}) collective-permute-start(bf16[88,2048]{1,0:T(8,128)(2,1)S(1)} %collective-permute-done.9.refs_3_), channel_id=1, source_target_pairs={{0,16},{16,0},{1,17},{17,1},{2,18},{18,2},{3,19},{19,3},{4,20},{20... | collective-permute-start | bytes 1081352 | tf_op jit(solution)/shard_map/ppermute | solution.py:313
  53.4 3.0 %collective-permute-start.18 = (bf16[88,2048]{1,0:T(8,128)(2,1)S(1)}, bf16[88,2048]{1,0:T(8,128)(2,1)S(1)}, u32[]{:S(2)}, u32[]{:S(2)}) collective-permute-start(bf16[88,2048]{1,0:T(8,128)(2,1)S(1)} %collective-permute-done.14.refs_2_), channel_id=1, source_target_pairs={{0,16},{16,0},{1,17},{17,1},{2,18},{18,2},{3,19},{19,3},{4,20},{20... | collective-permute-start | bytes 1081352 | tf_op jit(solution)/shard_map/ppermute | solution.py:313
  54.8 12.1 %collective-permute-start.19 = (s16[368,640]{1,0:T(8,128)(2,1)S(1)}, s16[368,640]{1,0:T(8,128)(2,1)S(1)}, u32[]{:S(2)}, u32[]{:S(2)}) collective-permute-start(s16[368,640]{1,0:T(8,128)(2,1)S(1)} %get-tuple-element.139), channel_id=1, source_target_pairs={{0,1},{1,0},{2,3},{3,2},{4,5},{5,4},{6,7},{7,6},{8,9},{9,8},{10,11... | collective-permute-start | bytes 1413128 | tf_op jit(solution)/shard_map/ppermute | solution.py:313
  60.1 16.8 %collective-permute-start.20 = (s16[368,640]{1,0:T(8,128)(2,1)S(1)}, s16[368,640]{1,0:T(8,128)(2,1)S(1)}, u32[]{:S(2)}, u32[]{:S(2)}) collective-permute-start(s16[368,640]{1,0:T(8,128)(2,1)S(1)} %get-tuple-element.164), channel_id=1, source_target_pairs={{0,1},{1,0},{2,3},{3,2},{4,5},{5,4},{6,7},{7,6},{8,9},{9,8},{10,11... | collective-permute-start | bytes 1413128 | tf_op jit(solution)/shard_map/ppermute | solution.py:313
  95.0 3.7 %collective-permute-start.21 = (f32[4,1408]{1,0:T(4,128)S(1)}, f32[4,1408]{1,0:T(4,128)S(1)}, u32[]{:S(2)}, u32[]{:S(2)}) collective-permute-start(f32[4,1408]{1,0:T(4,128)S(1)} %first_merge.1.one_ref), channel_id=1, source_target_pairs={{0,16},{16,0},{1,17},{17,1},{2,18},{18,2},{3,19},{19,3},{4,20},{20... | collective-permute-start | bytes 67592 | tf_op jit(solution)/shard_map/ppermute | solution.py:313
  (2 other events, 3.5 us)

commit v8 on v6

--- a/solution.py
+++ b/solution.py
@@ -371,13 +371,11 @@
     y_one2, y_two2 = swap(y_one, "c"), swap(y_two, "c")
     expo1 = chunk_expo(1, made1, code1)
     y_far, y_one2, y_two2, expo1, code2 = together(y_far, y_one2, y_two2, expo1, code2)
-
-    y_far2 = swap(y_far, "c")
+    made4 = chunk_front(y_one2, y_two2, y_far, swap(y_far, "c"))
+
+    code4 = swap(made4[1], "t")
     expo2 = chunk_expo(2, made2, code2)
-    y_far2, expo2 = together(y_far2, expo2)
-    made4 = chunk_front(y_one2, y_two2, y_far, y_far2)
-    code4 = swap(made4[1], "t")
-    made4, code3 = together(made4, code3)
+    made4, expo2, code3 = together(made4, expo2, code3)
     expo3 = chunk_expo(3, made3, code3)
     expo3, code4 = together(expo3, code4)
     expo4 = chunk_expo(4, made4, code4)

time: 147 us -> 147 us (level)
  transfers between devices with their start and end apart: 22 -> 22, of which waited for: 8 -> 9; matrix products, arithmetic and copies ran while one was open for 0% -> 0% of each run, Pallas kernels for 14% -> 14%
where the time goes in v8:
time: 147 us; the launch traced here: 146 us
  blocking collectives  57.6 us (39%)
  Pallas kernels  31.6 us (21%)
  starting transfers between devices  29.1 us (20%)
  waiting for transfers between devices  19.5 us (13%)
  local copies, waits for them, and re-layouts  3.77 us (3%)
  other arithmetic  3.75 us (3%)
    all_to_all x2, blocking collectives, everyone(): return lax.all_to_all(copies, axes, 0, 0, tiled=True)  22.2 us
    ppermute x14, waiting for transfers between devices, swap(): return lax.ppermute(x, (axis,), [(0, 1), (1, 0)])  18.3 us
    all_to_all x1, blocking collectives, local(): lax.all_to_all(own, 'z', 0, 0, tiled=True)  16 us
    pallas_call x5, Pallas kernels, front(): pl.pallas_call(functools.partial(front_kernel, pieces=len(pieces), rows=r...  15.2 us
    all_to_all x1, blocking collectives, local(): lax.all_to_all(on_chip, rest, 0, 0, tiled=True)  15 us
    ppermute x14, starting transfers between devices, swap(): return lax.ppermute(x, (axis,), [(0, 1), (1, 0)])  14.3 us
    ppermute x6, starting transfers between devices, along_x(): return lax.ppermute(x, ('x', 'c'), pairs)  11.8 us
    pallas_call x1, Pallas kernels, finish(): pl.pallas_call(functools.partial(product_kernel, chunks=chunks, size=size...  9.2 us
  transfers between devices with their start and end apart: 22, of which 9 were waited for; matrix products, arithmetic and copies ran while one was open for 0% of the time, Pallas kernels for 14%

profile of v8, /device:TPU:1, one launch (start us, length us, event | category | flops | bytes accessed | tf_op | source)
XLA Modules:
  0.0 146.3 jit_solution(7480397103912221530)
XLA Ops:
  2.8 4.4 %psum.7 = f32[88]{0:T(128)S(1)} all-reduce(f32[88]{0:T(128)S(1)} %fusion), channel_id=1, replica_groups=mesh['x'=4,'yh'=2,'c'=2,'z'=8,'t'=2] {'t'}, use_global_device_ids=true, to_apply=%region_1.2 | all-reduce | flops 88 | bytes 704 | tf_op jit(solution)/shard_map/psum | solution.py:335
  8.4 3.8 %collective-permute-start.3 = (bf16[88,2048]{1,0:T(8,128)(2,1)S(1)}, bf16[88,2048]{1,0:T(8,128)(2,1)S(1)}, u32[]{:S(2)}, u32[]{:S(2)}) collective-permute-start(bf16[88,2048]{1,0:T(8,128)(2,1)S(1)} %fusion.1.refs_0_), channel_id=1, source_target_pairs={{0,16},{16,0},{1,17},{17,1},{2,18},{18,2},{3,19},{19,3},{4,20},{20... | collective-permute-start | bytes 1081352 | tf_op jit(solution)/shard_map/ppermute | solution.py:309
  12.2 2.7 %collective-permute-start.1 = (bf16[88,2048]{1,0:T(8,128)(2,1)S(1)}, bf16[88,2048]{1,0:T(8,128)(2,1)S(1)}, u32[]{:S(2)}, u32[]{:S(2)}) collective-permute-start(bf16[88,2048]{1,0:T(8,128)(2,1)S(1)} %fusion.1.refs_0_), channel_id=1, source_target_pairs={{0,64},{16,208},{64,128},{80,16},{128,192},{144,80},{192,0},{208,1... | collective-permute-start | bytes 1081352 | tf_op jit(solution)/shard_map/ppermute | solution.py:294
  15.9 1.7 %copy-done = bf16[2048,640]{1,0:T(8,128)(2,1)S(1)} copy-done((bf16[2048,640]{1,0:T(8,128)(2,1)S(1)}, bf16[2048,640]{1,0:T(8,128)(2,1)}, u32[]{:S(2)}) %copy-start) | copy-done | bytes 2621464
  17.7 1.7 %copy-done.1 = bf16[2048,640]{1,0:T(8,128)(2,1)S(1)} copy-done((bf16[2048,640]{1,0:T(8,128)(2,1)S(1)}, bf16[2048,640]{1,0:T(8,128)(2,1)}, u32[]{:S(2)}) %copy-start.1) | copy-done | bytes 2621464
  19.8 2.0 %front.5 = (f32[176,640]{1,0:T(8,128)S(1)}, s16[192,640]{1,0:T(8,128)(2,1)S(1)}, f32[176,640]{1,0:T(8,128)S(1)}, bf16[176,2048]{1,0:T(8,128)(2,1)S(1)}) custom-call(bf16[88,2048]{1,0:T(8,128)(2,1)S(1)} %fusion.1.refs_0_, bf16[88,2048]{1,0:T(8,128)(2,1)S(1)} %collective-permute-done.3.refs_1_, f32[1,2048]{1,0:T(1,128)S(1)} %bitcast.24, ...), custom_call_target="tpu_custom_call" | custom-call | flops 1384120320 | bytes 1441792 | tf_op jit(solution)/shard_map/front/pallas_call | solution.py:89
  22.3 2.0 %collective-permute-start.4 = (bf16[88,2048]{1,0:T(8,128)(2,1)S(1)}, bf16[88,2048]{1,0:T(8,128)(2,1)S(1)}, u32[]{:S(2)}, u32[]{:S(2)}) collective-permute-start(bf16[88,2048]{1,0:T(8,128)(2,1)S(1)} %collective-permute-done), channel_id=1, source_target_pairs={{0,1},{16,49},{1,32},{17,16},{32,33},{48,17},{33,0},{49,48},{2,3},... | collective-permute-start | bytes 1081352 | tf_op jit(solution)/shard_map/ppermute | solution.py:305
  24.7 3.1 %collective-permute-start.5 = (bf16[88,2048]{1,0:T(8,128)(2,1)S(1)}, bf16[88,2048]{1,0:T(8,128)(2,1)S(1)}, u32[]{:S(2)}, u32[]{:S(2)}) collective-permute-start(bf16[88,2048]{1,0:T(8,128)(2,1)S(1)} %collective-permute-done.1.refs_0_), channel_id=1, source_target_pairs={{0,64},{16,208},{64,128},{80,16},{128,192},{144,80},{192,0},{208,1... | collective-permute-start | bytes 1081352 | tf_op jit(solution)/shard_map/ppermute | solution.py:294
  28.1 2.0 %front.6 = (f32[176,640]{1,0:T(8,128)S(1)}, s16[192,640]{1,0:T(8,128)(2,1)S(1)}, f32[176,640]{1,0:T(8,128)S(1)}, bf16[176,2048]{1,0:T(8,128)(2,1)S(1)}) custom-call(bf16[88,2048]{1,0:T(8,128)(2,1)S(1)} %collective-permute-done.1.refs_0_, bf16[88,2048]{1,0:T(8,128)(2,1)S(1)} %collective-permute-done.2.refs_1_, f32[1,2048]{1,0:T(1,128)S(1)} %bitcast.25, ...), custom_call_target="tpu_custom_call" | custom-call | flops 1384120320 | bytes 1441792 | tf_op jit(solution)/shard_map/front/pallas_call | solution.py:89
  32.2 3.1 %collective-permute-start.8 = (bf16[88,2048]{1,0:T(8,128)(2,1)S(1)}, bf16[88,2048]{1,0:T(8,128)(2,1)S(1)}, u32[]{:S(2)}, u32[]{:S(2)}) collective-permute-start(bf16[88,2048]{1,0:T(8,128)(2,1)S(1)} %collective-permute-done.4.refs_2_), channel_id=1, source_target_pairs={{0,64},{16,208},{64,128},{80,16},{128,192},{144,80},{192,0},{208,1... | collective-permute-start | bytes 1081352 | tf_op jit(solution)/shard_map/ppermute | solution.py:294
  35.3 3.7 %front.7 = (f32[352,640]{1,0:T(8,128)S(1)}, s16[368,640]{1,0:T(8,128)(2,1)S(1)}, f32[352,640]{1,0:T(8,128)S(1)}, bf16[352,2048]{1,0:T(8,128)(2,1)S(1)}) custom-call(bf16[88,2048]{1,0:T(8,128)(2,1)S(1)} %collective-permute-done.6.refs_0_, bf16[88,2048]{1,0:T(8,128)(2,1)S(1)} %collective-permute-done.7.refs_1_, ...), custom_call_target="tpu_custom_call" | custom-call | flops 2768240640 | bytes 2883584 | tf_op jit(solution)/shard_map/front/pallas_call | solution.py:89
  39.2 2.2 %collective-permute-start.12 = (bf16[88,2048]{1,0:T(8,128)(2,1)S(1)}, bf16[88,2048]{1,0:T(8,128)(2,1)S(1)}, u32[]{:S(2)}, u32[]{:S(2)}) collective-permute-start(bf16[88,2048]{1,0:T(8,128)(2,1)S(1)} %collective-permute-done.4.refs_2_), channel_id=1, source_target_pairs={{0,16},{16,0},{1,17},{17,1},{2,18},{18,2},{3,19},{19,3},{4,20},{20... | collective-permute-start | bytes 1081352 | tf_op jit(solution)/shard_map/ppermute | solution.py:309
  43.3 3.0 %collective-permute-start.14 = (bf16[88,2048]{1,0:T(8,128)(2,1)S(1)}, bf16[88,2048]{1,0:T(8,128)(2,1)S(1)}, u32[]{:S(2)}, u32[]{:S(2)}) collective-permute-start(bf16[88,2048]{1,0:T(8,128)(2,1)S(1)} %collective-permute-done.8.refs_2_), channel_id=1, source_target_pairs={{0,64},{16,208},{64,128},{80,16},{128,192},{144,80},{192,0},{208,1... | collective-permute-start | bytes 1081352 | tf_op jit(solution)/shard_map/ppermute | solution.py:294
  46.2 3.7 %front.8 = (f32[352,640]{1,0:T(8,128)S(1)}, s16[368,640]{1,0:T(8,128)(2,1)S(1)}, f32[352,640]{1,0:T(8,128)S(1)}, bf16[352,2048]{1,0:T(8,128)(2,1)S(1)}) custom-call(bf16[88,2048]{1,0:T(8,128)(2,1)S(1)} %collective-permute-done.12.refs_0_, bf16[88,2048]{1,0:T(8,128)(2,1)S(1)} %collective-permute-done.13.refs_1_, ...), custom_call_target="tpu_custom_call" | custom-call | flops 2768240640 | bytes 2883584 | tf_op jit(solution)/shard_map/front/pallas_call | solution.py:89
  51.6 1.9 %collective-permute-done.17.code_ref = s16[368,640]{1,0:T(8,128)(2,1)S(1)} collective-permute-done((s16[368,640]{1,0:T(8,128)(2,1)S(1)}, s16[368,640]{1,0:T(8,128)(2,1)S(1)}, u32[]{:S(2)}, u32[]{:S(2)}) %collective-permute-start.17) | collective-permute-done | bytes 471072 | tf_op jit(solution)/shard_map/ppermute | solution.py:309
  56.2 3.7 %front.9 = (f32[352,640]{1,0:T(8,128)S(1)}, s16[368,640]{1,0:T(8,128)(2,1)S(1)}, f32[352,640]{1,0:T(8,128)S(1)}, bf16[352,2048]{1,0:T(8,128)(2,1)S(1)}) custom-call(bf16[88,2048]{1,0:T(8,128)(2,1)S(1)} %collective-permute-done.15.refs_0_, bf16[88,2048]{1,0:T(8,128)(2,1)S(1)} %collective-permute-done.16.refs_1_, ...), custom_call_target="tpu_custom_call" | custom-call | flops 2768240640 | bytes 2883584 | tf_op jit(solution)/shard_map/front/pallas_call | solution.py:89
  61.6 5.3 %collective-permute-done.19.code_ref = s16[368,640]{1,0:T(8,128)(2,1)S(1)} collective-permute-done((s16[368,640]{1,0:T(8,128)(2,1)S(1)}, s16[368,640]{1,0:T(8,128)(2,1)S(1)}, u32[]{:S(2)}, u32[]{:S(2)}) %collective-permute-start.19) | collective-permute-done | bytes 471072 | tf_op jit(solution)/shard_map/ppermute | solution.py:309
  68.2 8.8 %collective-permute-done.20.code_ref = s16[368,640]{1,0:T(8,128)(2,1)S(1)} collective-permute-done((s16[368,640]{1,0:T(8,128)(2,1)S(1)}, s16[368,640]{1,0:T(8,128)(2,1)S(1)}, u32[]{:S(2)}, u32[]{:S(2)}) %collective-permute-start.20) | collective-permute-done | bytes 471072 | tf_op jit(solution)/shard_map/ppermute | solution.py:309
  78.4 16.0 %all_to_all.20.parts_ref = f32[8,4,1408]{2,1,0:T(4,128)S(1)} all-to-all(f32[8,4,1408]{2,1,0:T(4,128)S(1)} %copies.1), channel_id=1, replica_groups=mesh['x'=4,'yh'=2,'c'=2,'z'=8,'t'=2] {'z'}, dimensions={0} | all-to-all | bytes 360448 | tf_op jit(solution)/shard_map/all_to_all | solution.py:394
  95.2 2.8 %collective-permute-start.21 = (f32[4,1408]{1,0:T(4,128)S(1)}, f32[4,1408]{1,0:T(4,128)S(1)}, u32[]{:S(2)}, u32[]{:S(2)}) collective-permute-start(f32[4,1408]{1,0:T(4,128)S(1)} %first_merge.1.one_ref), channel_id=1, source_target_pairs={{0,16},{16,0},{1,17},{17,1},{2,18},{18,2},{3,19},{19,3},{4,20},{20... | collective-permute-start | bytes 67592 | tf_op jit(solution)/shard_map/ppermute | solution.py:309
  98.9 15.0 %all_to_all.21.parts_ref = f32[16,4,1408]{2,1,0:T(4,128)S(1)} all-to-all(f32[16,4,1408]{2,1,0:T(4,128)S(1)} %pair_merge.1), channel_id=1, replica_groups=mesh['x'=4,'yh'=2,'c'=2,'z'=8,'t'=2] {'x','yh','t'}, dimensions={0} | all-to-all | bytes 720896 | tf_op jit(solution)/shard_map/all_to_all | solution.py:404
  114.1 9.2 %product.1 = (f32[2048,640]{1,0:T(8,128)}, f32[1,2048]{1,0:T(1,128)S(1)}) custom-call(s32[16]{0:T(128)S(1)} %stack.67.place_ref.refs_0_, f32[16,128]{1,0:T(8,128)S(1)} %pad.4.ids_ref.refs_1_, f32[16,4,128]{2,1,0:T(4,128)S(1)} %last_merge.1.refs_2_, f32[176,640]{1,0:T(8,128)S(1)} %get-tuple-element.173.refs_3_, f32[176,640]{1,0:T(8,128)S(1)} %get-tuple-element.174.refs_4_, ...), custom_call_target="tpu_custom_call" | custom-call | flops 3690987520 | bytes 5242880 | tf_op jit(solution)/shard_map/product/pallas_call | solution.py:254
  123.3 12.7 %all_to_all.22 = f32[16,1,2048]{2,1,0:T(1,128)S(1)} all-to-all(f32[16,1,2048]{2,1,0:T(1,128)S(1)} %broadcast_in_dim.24), channel_id=1, replica_groups=mesh['x'=4,'yh'=2,'c'=2,'z'=8,'t'=2] {'x','yh','c'}, dimensions={0} | all-to-all | bytes 262144 | tf_op jit(solution)/shard_map/all_to_all | solution.py:286
  136.1 9.5 %all_to_all.23 = f32[8,1,2048]{2,1,0:T(1,128)S(1)} all-to-all(f32[8,1,2048]{2,1,0:T(1,128)S(1)} %broadcast_in_dim.25), channel_id=1, replica_groups=mesh['x'=4,'yh'=2,'c'=2,'z'=8,'t'=2] {'z'}, dimensions={0} | all-to-all | bytes 131072 | tf_op jit(solution)/shard_map/all_to_all | solution.py:286
  (60 shorter events, 21.1 us)
Async XLA Ops:
  7.3 12.5 %copy-start.2 = (f32[2048]{0:T(1024)S(1)}, f32[2048]{0:T(1024)}, u32[]{:S(2)}) copy-start(f32[2048]{0:T(1024)} %param.8) | copy-start | bytes 24580
  7.3 12.5 %copy-start.3 = (f32[2048]{0:T(1024)S(1)}, f32[2048]{0:T(1024)}, u32[]{:S(2)}) copy-start(f32[2048]{0:T(1024)} %param.7) | copy-start | bytes 24580
  8.4 11.4 %collective-permute-start.3 = (bf16[88,2048]{1,0:T(8,128)(2,1)S(1)}, bf16[88,2048]{1,0:T(8,128)(2,1)S(1)}, u32[]{:S(2)}, u32[]{:S(2)}) collective-permute-start(bf16[88,2048]{1,0:T(8,128)(2,1)S(1)} %fusion.1.refs_0_), channel_id=1, source_target_pairs={{0,16},{16,0},{1,17},{17,1},{2,18},{18,2},{3,19},{19,3},{4,20},{20... | collective-permute-start | bytes 1081352 | tf_op jit(solution)/shard_map/ppermute | solution.py:309
  12.2 10.0 %collective-permute-start.2 = (bf16[88,2048]{1,0:T(8,128)(2,1)S(1)}, bf16[88,2048]{1,0:T(8,128)(2,1)S(1)}, u32[]{:S(2)}, u32[]{:S(2)}) collective-permute-start(bf16[88,2048]{1,0:T(8,128)(2,1)S(1)} %fusion.1.refs_0_), channel_id=1, source_target_pairs={{0,192},{16,80},{64,0},{80,144},{128,64},{144,208},{192,128},{208,... | collective-permute-start | bytes 1081352 | tf_op jit(solution)/shard_map/ppermute | solution.py:294
  12.2 10.0 %collective-permute-start.1 = (bf16[88,2048]{1,0:T(8,128)(2,1)S(1)}, bf16[88,2048]{1,0:T(8,128)(2,1)S(1)}, u32[]{:S(2)}, u32[]{:S(2)}) collective-permute-start(bf16[88,2048]{1,0:T(8,128)(2,1)S(1)} %fusion.1.refs_0_), channel_id=1, source_target_pairs={{0,64},{16,208},{64,128},{80,16},{128,192},{144,80},{192,0},{208,1... | collective-permute-start | bytes 1081352 | tf_op jit(solution)/shard_map/ppermute | solution.py:294
  14.9 7.3 %collective-permute-start = (bf16[88,2048]{1,0:T(8,128)(2,1)S(1)}, bf16[88,2048]{1,0:T(8,128)(2,1)S(1)}, u32[]{:S(2)}, u32[]{:S(2)}) collective-permute-start(bf16[88,2048]{1,0:T(8,128)(2,1)S(1)} %fusion.1.refs_0_), channel_id=1, source_target_pairs={{0,1},{16,49},{1,32},{17,16},{32,33},{48,17},{33,0},{49,48},{2,3},... | collective-permute-start | bytes 1081352 | tf_op jit(solution)/shard_map/ppermute | solution.py:305
  22.3 7.9 %collective-permute-start.4 = (bf16[88,2048]{1,0:T(8,128)(2,1)S(1)}, bf16[88,2048]{1,0:T(8,128)(2,1)S(1)}, u32[]{:S(2)}, u32[]{:S(2)}) collective-permute-start(bf16[88,2048]{1,0:T(8,128)(2,1)S(1)} %collective-permute-done), channel_id=1, source_target_pairs={{0,1},{16,49},{1,32},{17,16},{32,33},{48,17},{33,0},{49,48},{2,3},... | collective-permute-start | bytes 1081352 | tf_op jit(solution)/shard_map/ppermute | solution.py:305
  24.2 7.2 %collective-permute-start.7 = (bf16[88,2048]{1,0:T(8,128)(2,1)S(1)}, bf16[88,2048]{1,0:T(8,128)(2,1)S(1)}, u32[]{:S(2)}, u32[]{:S(2)}) collective-permute-start(bf16[88,2048]{1,0:T(8,128)(2,1)S(1)} %collective-permute-done.2.refs_1_), channel_id=1, source_target_pairs={{0,16},{16,0},{1,17},{17,1},{2,18},{18,2},{3,19},{19,3},{4,20},{20... | collective-permute-start | bytes 1081352 | tf_op jit(solution)/shard_map/ppermute | solution.py:309
  24.3 7.1 %collective-permute-start.6 = (bf16[88,2048]{1,0:T(8,128)(2,1)S(1)}, bf16[88,2048]{1,0:T(8,128)(2,1)S(1)}, u32[]{:S(2)}, u32[]{:S(2)}) collective-permute-start(bf16[88,2048]{1,0:T(8,128)(2,1)S(1)} %collective-permute-done.1.refs_0_), channel_id=1, source_target_pairs={{0,16},{16,0},{1,17},{17,1},{2,18},{18,2},{3,19},{19,3},{4,20},{20... | collective-permute-start | bytes 1081352 | tf_op jit(solution)/shard_map/ppermute | solution.py:309
  24.7 7.4 %collective-permute-start.5 = (bf16[88,2048]{1,0:T(8,128)(2,1)S(1)}, bf16[88,2048]{1,0:T(8,128)(2,1)S(1)}, u32[]{:S(2)}, u32[]{:S(2)}) collective-permute-start(bf16[88,2048]{1,0:T(8,128)(2,1)S(1)} %collective-permute-done.1.refs_0_), channel_id=1, source_target_pairs={{0,64},{16,208},{64,128},{80,16},{128,192},{144,80},{192,0},{208,1... | collective-permute-start | bytes 1081352 | tf_op jit(solution)/shard_map/ppermute | solution.py:294
  27.8 11.2 %collective-permute-start.10 = (s16[192,640]{1,0:T(8,128)(2,1)S(1)}, s16[192,640]{1,0:T(8,128)(2,1)S(1)}, u32[]{:S(2)}, u32[]{:S(2)}) collective-permute-start(s16[192,640]{1,0:T(8,128)(2,1)S(1)} %get-tuple-element.104), channel_id=1, source_target_pairs={{0,1},{1,0},{2,3},{3,2},{4,5},{5,4},{6,7},{7,6},{8,9},{9,8},{10,11... | collective-permute-start | bytes 737288 | tf_op jit(solution)/shard_map/ppermute | solution.py:309
  30.1 9.1 %collective-permute-start.11 = (s16[192,640]{1,0:T(8,128)(2,1)S(1)}, s16[192,640]{1,0:T(8,128)(2,1)S(1)}, u32[]{:S(2)}, u32[]{:S(2)}) collective-permute-start(s16[192,640]{1,0:T(8,128)(2,1)S(1)} %get-tuple-element.111), channel_id=1, source_target_pairs={{0,1},{1,0},{2,3},{3,2},{4,5},{5,4},{6,7},{7,6},{8,9},{9,8},{10,11... | collective-permute-start | bytes 737288 | tf_op jit(solution)/shard_map/ppermute | solution.py:309
  32.2 10.8 %collective-permute-start.9 = (bf16[88,2048]{1,0:T(8,128)(2,1)S(1)}, bf16[88,2048]{1,0:T(8,128)(2,1)S(1)}, u32[]{:S(2)}, u32[]{:S(2)}) collective-permute-start(bf16[88,2048]{1,0:T(8,128)(2,1)S(1)} %collective-permute-done.4.refs_2_), channel_id=1, source_target_pairs={{0,192},{16,80},{64,0},{80,144},{128,64},{144,208},{192,128},{208,... | collective-permute-start | bytes 1081352 | tf_op jit(solution)/shard_map/ppermute | solution.py:294
  32.2 10.8 %collective-permute-start.8 = (bf16[88,2048]{1,0:T(8,128)(2,1)S(1)}, bf16[88,2048]{1,0:T(8,128)(2,1)S(1)}, u32[]{:S(2)}, u32[]{:S(2)}) collective-permute-start(bf16[88,2048]{1,0:T(8,128)(2,1)S(1)} %collective-permute-done.4.refs_2_), channel_id=1, source_target_pairs={{0,64},{16,208},{64,128},{80,16},{128,192},{144,80},{192,0},{208,1... | collective-permute-start | bytes 1081352 | tf_op jit(solution)/shard_map/ppermute | solution.py:294
  39.2 3.8 %collective-permute-start.12 = (bf16[88,2048]{1,0:T(8,128)(2,1)S(1)}, bf16[88,2048]{1,0:T(8,128)(2,1)S(1)}, u32[]{:S(2)}, u32[]{:S(2)}) collective-permute-start(bf16[88,2048]{1,0:T(8,128)(2,1)S(1)} %collective-permute-done.4.refs_2_), channel_id=1, source_target_pairs={{0,16},{16,0},{1,17},{17,1},{2,18},{18,2},{3,19},{19,3},{4,20},{20... | collective-permute-start | bytes 1081352 | tf_op jit(solution)/shard_map/ppermute | solution.py:309
  41.5 1.8 %collective-permute-start.13 = (bf16[88,2048]{1,0:T(8,128)(2,1)S(1)}, bf16[88,2048]{1,0:T(8,128)(2,1)S(1)}, u32[]{:S(2)}, u32[]{:S(2)}) collective-permute-start(bf16[88,2048]{1,0:T(8,128)(2,1)S(1)} %collective-permute-done.5.refs_3_), channel_id=1, source_target_pairs={{0,16},{16,0},{1,17},{17,1},{2,18},{18,2},{3,19},{19,3},{4,20},{20... | collective-permute-start | bytes 1081352 | tf_op jit(solution)/shard_map/ppermute | solution.py:309
  41.6 12.0 %collective-permute-start.17 = (s16[368,640]{1,0:T(8,128)(2,1)S(1)}, s16[368,640]{1,0:T(8,128)(2,1)S(1)}, u32[]{:S(2)}, u32[]{:S(2)}) collective-permute-start(s16[368,640]{1,0:T(8,128)(2,1)S(1)} %get-tuple-element.119), channel_id=1, source_target_pairs={{0,1},{1,0},{2,3},{3,2},{4,5},{5,4},{6,7},{7,6},{8,9},{9,8},{10,11... | collective-permute-start | bytes 1413128 | tf_op jit(solution)/shard_map/ppermute | solution.py:309
  43.3 10.2 %collective-permute-start.14 = (bf16[88,2048]{1,0:T(8,128)(2,1)S(1)}, bf16[88,2048]{1,0:T(8,128)(2,1)S(1)}, u32[]{:S(2)}, u32[]{:S(2)}) collective-permute-start(bf16[88,2048]{1,0:T(8,128)(2,1)S(1)} %collective-permute-done.8.refs_2_), channel_id=1, source_target_pairs={{0,64},{16,208},{64,128},{80,16},{128,192},{144,80},{192,0},{208,1... | collective-permute-start | bytes 1081352 | tf_op jit(solution)/shard_map/ppermute | solution.py:294
  50.0 3.6 %collective-permute-start.15 = (bf16[88,2048]{1,0:T(8,128)(2,1)S(1)}, bf16[88,2048]{1,0:T(8,128)(2,1)S(1)}, u32[]{:S(2)}, u32[]{:S(2)}) collective-permute-start(bf16[88,2048]{1,0:T(8,128)(2,1)S(1)} %collective-permute-done.8.refs_2_), channel_id=1, source_target_pairs={{0,16},{16,0},{1,17},{17,1},{2,18},{18,2},{3,19},{19,3},{4,20},{20... | collective-permute-start | bytes 1081352 | tf_op jit(solution)/shard_map/ppermute | solution.py:309
  50.1 3.4 %collective-permute-start.16 = (bf16[88,2048]{1,0:T(8,128)(2,1)S(1)}, bf16[88,2048]{1,0:T(8,128)(2,1)S(1)}, u32[]{:S(2)}, u32[]{:S(2)}) collective-permute-start(bf16[88,2048]{1,0:T(8,128)(2,1)S(1)} %collective-permute-done.9.refs_3_), channel_id=1, source_target_pairs={{0,16},{16,0},{1,17},{17,1},{2,18},{18,2},{3,19},{19,3},{4,20},{20... | collective-permute-start | bytes 1081352 | tf_op jit(solution)/shard_map/ppermute | solution.py:309
  53.5 2.7 %collective-permute-start.18 = (bf16[88,2048]{1,0:T(8,128)(2,1)S(1)}, bf16[88,2048]{1,0:T(8,128)(2,1)S(1)}, u32[]{:S(2)}, u32[]{:S(2)}) collective-permute-start(bf16[88,2048]{1,0:T(8,128)(2,1)S(1)} %collective-permute-done.14.refs_2_), channel_id=1, source_target_pairs={{0,16},{16,0},{1,17},{17,1},{2,18},{18,2},{3,19},{19,3},{4,20},{20... | collective-permute-start | bytes 1081352 | tf_op jit(solution)/shard_map/ppermute | solution.py:309
  54.9 12.1 %collective-permute-start.19 = (s16[368,640]{1,0:T(8,128)(2,1)S(1)}, s16[368,640]{1,0:T(8,128)(2,1)S(1)}, u32[]{:S(2)}, u32[]{:S(2)}) collective-permute-start(s16[368,640]{1,0:T(8,128)(2,1)S(1)} %get-tuple-element.136), channel_id=1, source_target_pairs={{0,1},{1,0},{2,3},{3,2},{4,5},{5,4},{6,7},{7,6},{8,9},{9,8},{10,11... | collective-permute-start | bytes 1413128 | tf_op jit(solution)/shard_map/ppermute | solution.py:309
  60.0 17.1 %collective-permute-start.20 = (s16[368,640]{1,0:T(8,128)(2,1)S(1)}, s16[368,640]{1,0:T(8,128)(2,1)S(1)}, u32[]{:S(2)}, u32[]{:S(2)}) collective-permute-start(s16[368,640]{1,0:T(8,128)(2,1)S(1)} %get-tuple-element.152), channel_id=1, source_target_pairs={{0,1},{1,0},{2,3},{3,2},{4,5},{5,4},{6,7},{7,6},{8,9},{9,8},{10,11... | collective-permute-start | bytes 1413128 | tf_op jit(solution)/shard_map/ppermute | solution.py:309
  95.2 3.7 %collective-permute-start.21 = (f32[4,1408]{1,0:T(4,128)S(1)}, f32[4,1408]{1,0:T(4,128)S(1)}, u32[]{:S(2)}, u32[]{:S(2)}) collective-permute-start(f32[4,1408]{1,0:T(4,128)S(1)} %first_merge.1.one_ref), channel_id=1, source_target_pairs={{0,16},{16,0},{1,17},{17,1},{2,18},{18,2},{3,19},{19,3},{4,20},{20... | collective-permute-start | bytes 67592 | tf_op jit(solution)/shard_map/ppermute | solution.py:309
  (2 other events, 3.5 us)
